TPU v7x, 128 devices: a whole 4x4x4 slice. The times are simulated.
128 devices in a mesh: row: 8 (over x, y_lo), col: 16 (over y_hi, z, core).
Axes of the slice: x: 4, y: 4 (y_hi: 2, y_lo: 2; y = y_hi * 2 + y_lo), z: 4, core: 2. Of those that a mesh axis runs over, the one named last changes fastest.
Arguments:
- a_blocks: bfloat16 [8, 160, 8, 128, 128], P('row', 'col'), may hold values from -6 to 6
- a_cols: int32 [8, 160, 8], P('row', 'col'), may hold values from 0 to 19, as said below
- a_count: int32 [8, 160], P('row', 'col'), may hold values from 4 to 8
- b_blocks: bfloat16 [16, 160, 8, 128, 128], P('col', 'row'), may hold values from -0.25 to 0.25
- b_cols: int32 [16, 160, 8], P('col', 'row'), may hold values from 0 to 19, as said below
- b_count: int32 [16, 160], P('col', 'row'), may hold values from 4 to 8
- c_cols: int32 [8, 160, 12], P('row', 'col'), may hold values from 0 to 19, as said below
- c_owner: int32 [8, 1920, 1], P('row', 'col'), may hold values from 0 to 127; in each aligned block of 120 rows (0 to 119, 120 to 239, ..., all dimensions but the last counted through in order) at most 2 rows name the same one
Outputs:
- owned: bfloat16 [128, 128, 2, 128, 128], P(('row', 'col'))
Inputs may be any that keep to these rules, and one draw needn't show every extreme that they name: `a_cols`: within each block row the 8 entries are distinct. `b_cols`: within each block row the 8 entries are distinct. `c_cols`: within each block row the 12 entries are distinct. `c_owner`: among the 120 entries of one device no owner appears more than 2 times, and some owner appears exactly 2 times.
All inputs are finite; a program needn't handle non-finite values.
Results may differ from a plain program's by a relative error of at most 0.001.
Values may be sent and summed in bfloat16 or wider, within the bound.
No kernel may reach another device: no remote copies, remote signals or barrier semaphores. Data moves between devices by JAX's collectives and lax.ppermute only.
A program may use at most 128 MiB of HBM per device.

v0:
```python
import jax
import jax.numpy as jnp
from jax import lax
from jax.sharding import PartitionSpec as P


def from_behind(value, axis, steps):
    count = lax.axis_size(axis)
    pairs = [(source, (source + steps) % count) for source in range(count)]
    return lax.ppermute(value, axis, pairs)


def choose_index(first_columns, first_counts, second_columns, second_counts, filter_columns):
    slots_first = first_columns.shape[1]
    slots_second = second_columns.shape[1]
    panel_rows = second_columns.shape[0]
    lookup = (
        first_columns[:, :, None] == jnp.arange(panel_rows, dtype=jnp.int32)[None, None, :]
    ).astype(jnp.int32)
    stored = jnp.sum(
        lookup[:, :, :, None] * second_columns[None, None, :, :], axis=2, dtype=jnp.int32
    )
    stored_counts = jnp.sum(lookup * second_counts[None, None, :], axis=2, dtype=jnp.int32)
    live_first = jnp.arange(slots_first, dtype=jnp.int32)[None, :] < first_counts[:, None]
    live_second = (
        jnp.arange(slots_second, dtype=jnp.int32)[None, None, :] < stored_counts[:, :, None]
    )
    matches = (
        (stored[:, :, :, None] == filter_columns[:, None, None, :])
        & live_second[:, :, :, None]
        & live_first[:, :, None, None]
    )
    flat_index = (
        first_columns[:, :, None] * slots_second
        + jnp.arange(slots_second, dtype=jnp.int32)[None, None, :]
    )
    picked = jnp.sum(jnp.where(matches, flat_index[:, :, :, None], 0), axis=2, dtype=jnp.int32)
    return jnp.where(jnp.any(matches, axis=2), picked, panel_rows * slots_second)


def stop_product(
    first_blocks,
    first_columns,
    first_counts,
    second_blocks,
    second_columns,
    second_counts,
    filter_columns,
):
    index = choose_index(first_columns, first_counts, second_columns, second_counts, filter_columns)
    side = second_blocks.shape[2]
    flat_blocks = jnp.concatenate(
        [second_blocks.reshape(-1, side, side), jnp.zeros((1, side, side), second_blocks.dtype)],
        axis=0,
    )
    chosen = flat_blocks[index]
    return jnp.einsum("iapq,iafqr->ifpr", first_blocks, chosen, preferred_element_type=jnp.float32)


def slot_sources(owners, devices, per_owner):
    length = owners.shape[0]
    positions = jnp.arange(length, dtype=jnp.int32)
    earlier = (owners[:, None] == owners[None, :]) & (positions[None, :] < positions[:, None])
    ranks = jnp.sum(earlier, axis=1, dtype=jnp.int32)
    slots = owners * per_owner + ranks
    return jnp.full((devices * per_owner,), length, jnp.int32).at[slots].set(positions)


def on_device(a_blocks, a_cols, a_count, b_blocks, b_cols, b_count, c_cols, c_owner):
    first_blocks = a_blocks[0]
    first_columns = a_cols[0]
    first_counts = a_count[0]
    second_blocks = b_blocks[0]
    second_columns = b_cols[0]
    second_counts = b_count[0]
    filter_columns = c_cols[0]
    total = stop_product(
        first_blocks,
        first_columns,
        first_counts,
        second_blocks,
        second_columns,
        second_counts,
        filter_columns,
    )
    first_blocks, first_columns, first_counts = from_behind(
        (first_blocks, first_columns, first_counts), "row", -1
    )
    second_blocks, second_columns, second_counts = from_behind(
        (second_blocks, second_columns, second_counts), "col", -1
    )
    total = total + stop_product(
        first_blocks,
        first_columns,
        first_counts,
        second_blocks,
        second_columns,
        second_counts,
        filter_columns,
    )
    grid_rows = lax.axis_size("row")
    grid_cols = lax.axis_size("col")
    devices = grid_rows * grid_cols
    row_total = total.shape[0]
    kept_total = total.shape[1]
    side = total.shape[2]
    per_owner = max(2, 3 * row_total * kept_total // (2 * devices))
    product = total.astype(jnp.bfloat16).reshape(row_total * kept_total, side, side)
    sources = slot_sources(c_owner[0, :, 0], devices, per_owner)
    padded = jnp.concatenate([product, jnp.zeros((1, side, side), jnp.bfloat16)], axis=0)
    outgoing = padded[sources]
    arrived = lax.all_to_all(
        outgoing.reshape(devices, per_owner, side, side),
        ("row", "col"),
        split_axis=0,
        concat_axis=0,
        tiled=True,
    )
    return arrived.reshape(1, devices, per_owner, side, side)


def solution(mesh):
    return jax.shard_map(
        on_device,
        mesh=mesh,
        in_specs=(
            P("row", "col", None, None, None),
            P("row", "col", None),
            P("row", "col"),
            P("col", "row", None, None, None),
            P("col", "row", None),
            P("col", "row"),
            P("row", "col", None),
            P("row", "col", None),
        ),
        out_specs=P(("row", "col"), None, None, None, None),
        check_vma=False,
    )
```

profile of v0, /device:TPU:1, one launch (start us, length us, event | category | flops | bytes accessed | tf_op | source)
XLA Modules:
  0.0 318.0 jit_solution(7039198054754580908)
XLA Ops:
  0.0 4.3 %collective-permute-start.1 = (s32[10,8]{0,1:T(8,128)}, s32[10,8]{0,1:T(8,128)S(1)}, u32[]{:S(2)}, u32[]{:S(2)}) collective-permute-start(s32[10,8]{0,1:T(8,128)} %bitcast.78), channel_id=1, source_target_pairs={{0,112},{16,0},{32,16},{48,32},{64,48},{80,64},{96,80},{112,96},{1... | collective-permute-start | bytes 968 | tf_op jit(solution)/shard_map/ppermute | solution.py:10
  4.3 1.0 collective-permute-start.2
  5.3 5.5 %collective-permute-start.3 = (s32[20]{0:T(128)}, s32[20]{0:T(128)S(1)}, u32[]{:S(2)}, u32[]{:S(2)}) collective-permute-start(s32[20]{0:T(128)} %bitcast.84), channel_id=1, source_target_pairs={{0,15},{1,0},{2,1},{3,2},{4,3},{5,4},{6,5},{7,6},{8,7},{9,8},{10,9... | collective-permute-start | bytes 248 | tf_op jit(solution)/shard_map/ppermute | solution.py:10
  10.8 1.1 collective-permute-start
  11.9 0.8 copy.25
  12.8 1.0 select_reduce_fusion.3
  15.2 2.1 multiply_reduce_fusion.1
  18.2 0.9 convert_reduce_fusion
  19.8 0.9 scatter_custom_fusion
  20.8 7.0 %concatenate.9 = bf16[161,128,128]{2,1,0:T(8,128)(2,1)} pad(bf16[160,128,128]{2,1,0:T(8,128)(2,1)} %bitcast.74, bf16[]{:T(256)} %constant.10.clone.1), padding=0_1x0_0x0_0 | pad | bytes 10518530 | tf_op jit(solution)/shard_map/concatenate | solution.py:52
  27.8 1.9 collective-permute-start.5
  30.5 1.4 multiply_reduce_fusion
  31.9 0.9 fusion.5
  32.8 1.1 select_reduce_fusion
  34.2 22.7 %gather_fusion = bf16[960,128,128]{2,1,0:T(8,128)(2,1)} fusion(bf16[161,128,128]{2,1,0:T(8,128)(2,1)} %concatenate.9, s32[1024]{0:T(1024)S(1)} %pad_clamp_fusion.2), kind=kCustom, calls=%fused_computation | custom fusion | bytes 62918400 | tf_op jit(solution)/shard_map/gather | solution.py:56
  56.8 17.5 %fusion.2 = f32[10,12,128,128,1]{3,2,1,4,0:T(8,128)} fusion(bf16[10,8,12,128,128]{4,3,2,1,0:T(8,128)(2,1)} %bitcast.68, bf16[1,10,8,128,128]{4,3,2,1,0:T(8,128)(2,1)S(1)} %copy-done), kind=kOutput, calls=%fused_computation.7 | convolution fusion | flops 4026531840 | bytes 41943040 | tf_op jit(solution)/shard_map/iapq,iafqr->ifpr/dot_general | solution.py:57
  74.3 7.0 %concatenate.10 = bf16[161,128,128]{2,1,0:T(8,128)(2,1)} pad(bf16[160,128,128]{2,1,0:T(8,128)(2,1)} %bitcast.13, bf16[]{:T(256)} %constant.10.clone.1), padding=0_1x0_0x0_0 | pad | bytes 10518530 | tf_op jit(solution)/shard_map/concatenate | solution.py:52
  81.3 23.0 %gather_fusion.1 = bf16[960,128,128]{2,1,0:T(8,128)(2,1)} fusion(bf16[161,128,128]{2,1,0:T(8,128)(2,1)} %concatenate.10, s32[1024]{0:T(1024)S(1)} %pad_clamp_fusion.1), kind=kCustom, calls=%fused_computation.1 | custom fusion | bytes 62918400 | tf_op jit(solution)/shard_map/gather | solution.py:56
  104.2 18.6 %fusion = bf16[10,12,128,128]{3,2,1,0:T(8,128)(2,1)} fusion(f32[10,12,128,128,1]{3,2,1,4,0:T(8,128)} %fusion.2, bf16[10,8,12,128,128]{4,3,2,1,0:T(8,128)(2,1)} %bitcast.69, bf16[10,8,128,128]{3,2,1,0:T(8,128)(2,1)} %collective-permute-done.5), kind=kOutput, calls=%fused_computation.5 | convolution fusion | flops 4030464000 | bytes 45875200 | tf_op jit(solution)/shard_map/iapq,iafqr->ifpr/dot_general | solution.py:57
  122.8 4.5 %concatenate.11 = bf16[121,128,128]{1,2,0:T(8,128)(2,1)} pad(bf16[120,128,128]{1,2,0:T(8,128)(2,1)} %bitcast.72, bf16[]{:T(256)} %constant.10.clone.1), padding=0_1x0_0x0_0 | pad | bytes 7897090 | tf_op jit(solution)/shard_map/concatenate | solution.py:110
  127.4 10.7 %gather_fusion.2 = bf16[256,128,128]{1,2,0:T(8,128)(2,1)} fusion(bf16[121,128,128]{1,2,0:T(8,128)(2,1)} %concatenate.11, s32[1024]{0:T(1024)S(1)} %pad_clamp_fusion), kind=kCustom, calls=%fused_computation.2 | custom fusion | bytes 16778240 | tf_op jit(solution)/shard_map/gather | solution.py:111
  138.1 11.9 %copy.31 = bf16[256,128,128]{2,1,0:T(8,128)(2,1)} copy(bf16[256,128,128]{1,2,0:T(8,128)(2,1)} %gather_fusion.2) | data formatting | bytes 16777216 | tf_op jit(solution)/shard_map/gather | solution.py:111
  150.0 157.5 %all_to_all.5 = bf16[128,2,128,128]{3,2,1,0:T(8,128)(2,1)} all-to-all(bf16[128,2,128,128]{3,2,1,0:T(8,128)(2,1)} %bitcast.70), channel_id=1, replica_groups=mesh['row'=8,'col'=16] {'row','col'}, dimensions={0} | all-to-all | bytes 16777216 | tf_op jit(solution)/shard_map/all_to_all | solution.py:112
  307.5 10.5 %copy.44 = bf16[1,128,2,128,128]{4,3,2,1,0:T(8,128)(2,1)} copy(bf16[1,128,2,128,128]{4,3,2,1,0:T(8,128)(2,1)} %bitcast.71) | data formatting | bytes 16777216
  (33 shorter events, 4.2 us)
Async XLA Ops:
  0.0 27.8 %copy-start = (bf16[1,10,8,128,128]{4,3,2,1,0:T(8,128)(2,1)S(1)}, bf16[1,10,8,128,128]{4,3,2,1,0:T(8,128)(2,1)}, u32[]{:S(2)}) copy-start(bf16[1,10,8,128,128]{4,3,2,1,0:T(8,128)(2,1)} %param.8) | copy-start | bytes 7864324
  0.0 29.7 %collective-permute-start.1 = (s32[10,8]{0,1:T(8,128)}, s32[10,8]{0,1:T(8,128)S(1)}, u32[]{:S(2)}, u32[]{:S(2)}) collective-permute-start(s32[10,8]{0,1:T(8,128)} %bitcast.78), channel_id=1, source_target_pairs={{0,112},{16,0},{32,16},{48,32},{64,48},{80,64},{96,80},{112,96},{1... | collective-permute-start | bytes 968 | tf_op jit(solution)/shard_map/ppermute | solution.py:10
  4.3 26.1 %collective-permute-start.2 = (s32[20,8]{0,1:T(8,128)}, s32[20,8]{0,1:T(8,128)S(1)}, u32[]{:S(2)}, u32[]{:S(2)}) collective-permute-start(s32[20,8]{0,1:T(8,128)} %bitcast.80), channel_id=1, source_target_pairs={{0,15},{1,0},{2,1},{3,2},{4,3},{5,4},{6,5},{7,6},{8,7},{9,8},{10,9... | collective-permute-start | bytes 1928 | tf_op jit(solution)/shard_map/ppermute | solution.py:10
  5.3 24.6 %collective-permute-start.3 = (s32[20]{0:T(128)}, s32[20]{0:T(128)S(1)}, u32[]{:S(2)}, u32[]{:S(2)}) collective-permute-start(s32[20]{0:T(128)} %bitcast.84), channel_id=1, source_target_pairs={{0,15},{1,0},{2,1},{3,2},{4,3},{5,4},{6,5},{7,6},{8,7},{9,8},{10,9... | collective-permute-start | bytes 248 | tf_op jit(solution)/shard_map/ppermute | solution.py:10
  10.8 16.9 %collective-permute-start.4 = (s32[10]{0:T(128)}, s32[10]{0:T(128)S(1)}, u32[]{:S(2)}, u32[]{:S(2)}) collective-permute-start(s32[10]{0:T(128)} %bitcast.82), channel_id=1, source_target_pairs={{0,112},{16,0},{32,16},{48,32},{64,48},{80,64},{96,80},{112,96},{1... | collective-permute-start | bytes 128 | tf_op jit(solution)/shard_map/ppermute | solution.py:10
  10.8 63.5 %collective-permute-start = (bf16[20,8,128,128]{3,2,1,0:T(8,128)(2,1)}, bf16[20,8,128,128]{3,2,1,0:T(8,128)(2,1)}, u32[]{:S(2)}, u32[]{:S(2)}) collective-permute-start(bf16[20,8,128,128]{3,2,1,0:T(8,128)(2,1)} %bitcast.73), channel_id=1, source_target_pairs={{0,15},{1,0},{2,1},{3,2},{4,3},{5,4},{6,5},{7,6},{8,7},{9,8},{10,9... | collective-permute-start | bytes 15728648 | tf_op jit(solution)/shard_map/ppermute | solution.py:10
  27.8 76.5 %collective-permute-start.5 = (bf16[10,8,128,128]{3,2,1,0:T(8,128)(2,1)S(1)}, bf16[10,8,128,128]{3,2,1,0:T(8,128)(2,1)}, u32[]{:S(2)}, u32[]{:S(2)}) collective-permute-start(bf16[10,8,128,128]{3,2,1,0:T(8,128)(2,1)S(1)} %bitcast.75), channel_id=1, source_target_pairs={{0,112},{16,0},{32,16},{48,32},{64,48},{80,64},{96,80},{112,96},{1... | collective-permute-start | bytes 7864328 | tf_op jit(solution)/shard_map/ppermute | solution.py:10
where the time goes:
time: 319 us; the launch traced here: 318 us
  blocking collectives  157 us (49%)
  local copies, waits for them, and re-layouts  100 us (31%)
  matrix products  36.1 us (11%)
  starting transfers between devices  13.8 us (4%)
  other arithmetic  10.4 us (3%)
    all_to_all x1, blocking collectives, on_device(): lax.all_to_all(outgoing.reshape(devices, per_owner, side, side), ('row',...  157 us
    gather x2, local copies, waits for them, and re-layouts, stop_product(): chosen = flat_blocks[index]  45.6 us
    dot_general x2, matrix products, stop_product(): jnp.einsum('iapq,iafqr->ifpr', first_blocks, chosen, preferred_element_ty...  36.1 us
    gather x2, local copies, waits for them, and re-layouts, on_device(): outgoing = padded[sources]  22.7 us
    concatenate x2, local copies, waits for them, and re-layouts, stop_product(): jnp.concatenate([second_blocks.reshape(-1, side, side), jnp.zeros((1, sid...  13.9 us
    ppermute x6, starting transfers between devices, from_behind(): return lax.ppermute(value, axis, pairs)  13.8 us
    unnamed x4, local copies, waits for them, and re-layouts  11.2 us
  transfers between devices with their start and end apart: 6, of which 0 were waited for; matrix products, arithmetic and copies ran while one was open for 28% of the time, Pallas kernels for 0%

commit v1 on v0

v1 whole, which is shorter than its diff:
```python
import functools

import jax
import jax.numpy as jnp
from jax import lax
from jax.experimental import pallas as pl
from jax.experimental.pallas import tpu as pltpu
from jax.sharding import PartitionSpec as P

VMEM_LIMIT = 40 * 1024 * 1024
TABLE_ROWS = 20


def move(value, chosen):
    rows, cols = lax.axis_size("row"), lax.axis_size("col")
    pairs = []
    for r in range(rows):
        for c in range(cols):
            to = chosen(r, c)
            if to is not None:
                pairs.append((r * cols + c, (to[0] % rows) * cols + to[1] % cols))
    return lax.ppermute(value, ("row", "col"), pairs)


def flat_meta(columns, counts):
    return jnp.concatenate([columns.reshape(-1), counts])


def fill_table(table, meta, slots, width):
    panel_rows = meta.shape[0] // (slots + 1)
    blank = panel_rows * slots

    def clear(n, carry):
        table[n] = blank
        return carry

    lax.fori_loop(0, table.shape[0], clear, 0, unroll=width)
    for k in range(panel_rows):
        count = meta[blank + k]
        for b in range(slots):
            block = k * slots + b
            table[k * width + meta[block]] = jnp.where(b < count, block, blank)


def load_second(second, held, sem):
    total = second.shape[0]
    copy = pltpu.make_async_copy(second, held.at[pl.ds(0, total)], sem)
    copy.start()
    held[total] = jnp.zeros(held.shape[1:], held.dtype)
    return copy


def row_starts(meta, i, slots, width):
    row_total = meta.shape[0] // (slots + 1)
    count = meta[row_total * slots + i]
    return [
        jnp.where(a < count, meta[i * slots + a] * width, TABLE_ROWS * width) for a in range(slots)
    ]


def pair_product(starts, table, columns, first, held):
    slots = first.shape[1]
    row = jnp.concatenate([first[0, a] for a in range(slots)], axis=1)
    picked = [
        jnp.concatenate([held[table[start + column]] for start in starts], axis=0)
        for column in columns
    ]
    return jnp.dot(row, jnp.concatenate(picked, axis=1), preferred_element_type=jnp.float32)


def first_stop_kernel(
    first_meta, second_meta, kept_columns, first, second,
    total, blank, table, held, zeros, held_sem, blank_sem,
):
    i = pl.program_id(0)
    kept, side = total.shape[1], total.shape[2]
    slots = first.shape[1]
    width = table.shape[0] // (TABLE_ROWS + 1)
    part = zeros.shape[0]

    @pl.when(i == 0)
    def _():
        copy = load_second(second, held, held_sem)
        zeros[...] = jnp.zeros(zeros.shape, zeros.dtype)
        for j in range(blank.shape[0] // part):
            pltpu.make_async_copy(zeros, blank.at[pl.ds(j * part, part)], blank_sem).start()
        fill_table(table, second_meta, slots, width)
        copy.wait()

    starts = row_starts(first_meta, i, slots, width)
    for f in range(0, kept, 2):
        columns = [kept_columns[i * kept + f + g] for g in range(2)]
        both = pair_product(starts, table, columns, first, held)
        total[0, f] = both[:, :side]
        total[0, f + 1] = both[:, side:]

    @pl.when(i == pl.num_programs(0) - 1)
    def _():
        pltpu.make_async_copy(blank, blank, blank_sem).wait()


def last_stop_kernel(
    first_meta, second_meta, kept_columns, owner, place,
    early, late, before, second, part_a, part_b, part_c, blank,
    out, table, used, held, rows, product, held_sem, row_sem, out_sem,
):
    del blank
    i = pl.program_id(0)
    kept, side = before.shape[1], before.shape[2]
    width = table.shape[0] // (TABLE_ROWS + 1)
    per_owner = out.shape[0] // used.shape[0]
    row_total, slots = rows.shape[0], rows.shape[1]
    total = held.shape[0] - 1

    @pl.when(i == 0)
    def _():
        whole = held.at[pl.ds(0, total)]

        @pl.when(place[0] == 0)
        def _():
            pltpu.make_async_copy(second, whole, held_sem).start()

        @pl.when(place[0] != 0)
        def _():
            at = 0
            for part in (part_a, part_b, part_c):
                span = pl.ds(at, part.shape[0])
                pltpu.make_async_copy(part, held.at[span], held_sem).start()
                at += part.shape[0]

        @pl.when(place[1] == 0)
        def _():
            for j in range(row_total):
                pltpu.make_async_copy(early.at[j], rows.at[j], row_sem.at[j]).start()

        @pl.when(place[1] != 0)
        def _():
            for j in range(row_total):
                pltpu.make_async_copy(late.at[j], rows.at[j], row_sem.at[j]).start()

        held[total] = jnp.zeros(held.shape[1:], held.dtype)

        def clear(n, carry):
            used[n] = 0
            return carry

        lax.fori_loop(0, used.shape[0], clear, 0, unroll=16)
        fill_table(table, second_meta, slots, width)
        pltpu.make_async_copy(whole, whole, held_sem).wait()

    pltpu.make_async_copy(rows.at[i], rows.at[i], row_sem.at[i]).wait()
    first = rows.at[pl.ds(i, 1)]
    starts = row_starts(first_meta, i, slots, width)
    for f in range(0, kept, 2):
        columns = [kept_columns[i * kept + f + g] for g in range(2)]
        both = pair_product(starts, table, columns, first, held)
        for g in range(2):
            l = i * kept + f + g
            value = both[:, g * side:(g + 1) * side] + before[0, f + g]
            product[l] = value.astype(product.dtype)
            rank = used[owner[l]]
            used[owner[l]] = rank + 1
            slot = owner[l] * per_owner + rank
            pltpu.make_async_copy(product.at[l], out.at[slot], out_sem).start()

    @pl.when(i == pl.num_programs(0) - 1)
    def _():
        pltpu.make_async_copy(product, out.at[pl.ds(0, product.shape[0])], out_sem).wait()


def first_stop(first_meta, second_meta, kept_columns, first, second, outgoing):
    rows, slots, side, _ = first.shape
    kept = kept_columns.shape[0] // rows
    second_total = second.shape[0]
    part = 16
    return pl.pallas_call(
        first_stop_kernel,
        grid_spec=pltpu.PrefetchScalarGridSpec(
            num_scalar_prefetch=3,
            grid=(rows,),
            in_specs=[
                pl.BlockSpec((1, slots, side, side), lambda i, *_: (i, 0, 0, 0)),
                pl.BlockSpec(memory_space=pl.ANY),
            ],
            out_specs=[
                pl.BlockSpec((1, kept, side, side), lambda i, *_: (i, 0, 0, 0)),
                pl.BlockSpec(memory_space=pl.ANY),
            ],
            scratch_shapes=[
                pltpu.SMEM(((TABLE_ROWS + 1) * TABLE_ROWS,), jnp.int32),
                pltpu.VMEM((second_total + 1, side, side), second.dtype),
                pltpu.VMEM((part, side, side), second.dtype),
                pltpu.SemaphoreType.DMA,
                pltpu.SemaphoreType.DMA,
            ],
        ),
        out_shape=[
            jax.ShapeDtypeStruct((rows, kept, side, side), jnp.float32),
            jax.ShapeDtypeStruct((outgoing, side, side), second.dtype),
        ],
        compiler_params=pltpu.CompilerParams(vmem_limit_bytes=62 * 1024 * 1024),
        cost_estimate=pl.CostEstimate(
            flops=4 * rows * slots * kept * side**3,
            bytes_accessed=2 * (rows * (slots * 2 + kept * 4) + 2 * second_total) * side**2,
            transcendentals=0,
        ),
    )(first_meta, second_meta, kept_columns, first, second)


def last_stop(
    first_meta, second_meta, kept_columns, owner, place,
    early, late, before, second, part_a, part_b, part_c, blank, owners,
):
    rows, slots, side, _ = early.shape
    kept = before.shape[1]
    second_total = second.shape[0]
    return pl.pallas_call(
        last_stop_kernel,
        grid_spec=pltpu.PrefetchScalarGridSpec(
            num_scalar_prefetch=5,
            grid=(rows,),
            in_specs=[
                pl.BlockSpec(memory_space=pl.ANY),
                pl.BlockSpec(memory_space=pl.ANY),
                pl.BlockSpec((1, kept, side, side), lambda i, *_: (i, 0, 0, 0)),
                pl.BlockSpec(memory_space=pl.ANY),
                pl.BlockSpec(memory_space=pl.ANY),
                pl.BlockSpec(memory_space=pl.ANY),
                pl.BlockSpec(memory_space=pl.ANY),
                pl.BlockSpec(memory_space=pl.ANY),
            ],
            out_specs=pl.BlockSpec(memory_space=pl.ANY),
            scratch_shapes=[
                pltpu.SMEM(((TABLE_ROWS + 1) * TABLE_ROWS,), jnp.int32),
                pltpu.SMEM((owners,), jnp.int32),
                pltpu.VMEM((second_total + 1, side, side), second.dtype),
                pltpu.VMEM(early.shape, early.dtype),
                pltpu.VMEM((rows * kept, side, side), second.dtype),
                pltpu.SemaphoreType.DMA,
                pltpu.SemaphoreType.DMA((rows,)),
                pltpu.SemaphoreType.DMA,
            ],
        ),
        out_shape=jax.ShapeDtypeStruct(blank.shape, blank.dtype),
        input_output_aliases={12: 0},
        compiler_params=pltpu.CompilerParams(vmem_limit_bytes=VMEM_LIMIT),
        cost_estimate=pl.CostEstimate(flops=1024, bytes_accessed=1024, transcendentals=0),
    )(
        first_meta, second_meta, kept_columns, owner, place,
        early, late, before, second, part_a, part_b, part_c, blank,
    )


def cut_kernel(place, source, *rest):
    targets, sem = rest[:-1], rest[-1]

    @pl.when(place[0] != 0)
    def _():
        copies, at = [], 0
        for n, target in enumerate(targets):
            piece = source.at[pl.ds(at, target.shape[0])]
            copies.append(pltpu.make_async_copy(piece, target, sem.at[n]))
            at += target.shape[0]
        for copy in copies:
            copy.start()
        for copy in copies:
            copy.wait()


def cut(place, value, sizes):
    return pl.pallas_call(
        cut_kernel,
        in_specs=[pl.BlockSpec(memory_space=pltpu.SMEM), pl.BlockSpec(memory_space=pl.ANY)],
        out_specs=[pl.BlockSpec(memory_space=pl.ANY)] * len(sizes),
        out_shape=[jax.ShapeDtypeStruct((size,) + value.shape[1:], value.dtype) for size in sizes],
        scratch_shapes=[pltpu.SemaphoreType.DMA((len(sizes),))],
        compiler_params=pltpu.CompilerParams(vmem_limit_bytes=VMEM_LIMIT),
        cost_estimate=pl.CostEstimate(flops=1024, bytes_accessed=1024, transcendentals=0),
    )(place, value)


def copy_kernel(parts, source, target, sem):
    size = source.shape[0] // parts
    for j in range(parts):
        piece = pl.ds(j * size, size)
        pltpu.make_async_copy(source.at[piece], target.at[piece], sem).start()
    pltpu.make_async_copy(source, target, sem).wait()


def hand_over(value):
    return pl.pallas_call(
        functools.partial(copy_kernel, 16),
        in_specs=[pl.BlockSpec(memory_space=pl.ANY)],
        out_specs=pl.BlockSpec(memory_space=pl.ANY),
        out_shape=jax.ShapeDtypeStruct(value.shape, value.dtype),
        scratch_shapes=[pltpu.SemaphoreType.DMA],
        compiler_params=pltpu.CompilerParams(vmem_limit_bytes=VMEM_LIMIT),
    )(value)


def on_device(a_blocks, a_cols, a_count, b_blocks, b_cols, b_count, c_cols, c_owner):
    devices = lax.axis_size("row") * lax.axis_size("col")
    span = lax.axis_size("col") // 2
    rows, kept = c_cols.shape[1], c_cols.shape[2]
    side = a_blocks.shape[3]
    per_owner = max(2, 3 * rows * kept // (2 * devices))
    first = a_blocks[0]
    second = b_blocks[0].reshape(-1, side, side)
    total = second.shape[0]
    large = total * 9 // 20
    spot = lax.axis_index("col") % span
    crossing = (spot == 0).astype(jnp.int32)[None]

    def near(r, c):
        return r ^ 1, c

    def far(r, c):
        return r ^ 1, c + span

    def to_last(r, c):
        return r, c + span - 1

    def at(place, step):
        return lambda r, c: step(r, c) if c % span == place else None

    part_a, part_b, part_c = cut(crossing, second, (large, large, total - 2 * large))
    part_a = move(part_a, at(0, near))
    part_b = move(part_b, at(0, to_last))
    part_c = move(part_c, at(0, lambda r, c: (r, c - 1)))
    early = move(first, lambda r, c: (r - 1, c) if c % span > 1 else None)
    second_next = move(second, lambda r, c: (r, c - 1) if c % span else None)

    own_first_meta = flat_meta(a_cols[0], a_count[0])
    own_second_meta = flat_meta(b_cols[0], b_count[0])
    kept_columns = c_cols[0].reshape(-1)
    owner = c_owner[0, :, 0]
    before, blank = first_stop(
        own_first_meta, own_second_meta, kept_columns, first, second, devices * per_owner
    )

    part_a, part_b, part_c, first, before, blank = lax.optimization_barrier(
        (part_a, part_b, part_c, first, before, blank)
    )
    late = move(first, lambda r, c: (r - 1, c) if c % span < 2 else None)
    part_a = move(part_a, at(0, far))
    part_b = move(part_b, at(span - 1, far))

    part_a, part_b, early, second_next, first_meta, second_meta = lax.optimization_barrier(
        (part_a, part_b, early, second_next, own_first_meta, own_second_meta)
    )
    part_a = move(part_a, at(0, to_last))
    part_b = move(part_b, at(span - 1, near))
    first_meta = move(first_meta, lambda r, c: (r - 1, c))
    second_meta = move(second_meta, lambda r, c: (r, c - 1))

    place = jnp.stack([spot == span - 1, spot < 2]).astype(jnp.int32)
    outgoing = last_stop(
        first_meta, second_meta, kept_columns, owner, place,
        early, late, before, second_next, part_a, part_b, part_c, blank, devices,
    )
    arrived = lax.all_to_all(
        outgoing.reshape(devices, per_owner, side, side),
        ("row", "col"),
        split_axis=0,
        concat_axis=0,
        tiled=True,
    )
    return hand_over(arrived).reshape(1, devices, per_owner, side, side)


def solution(mesh):
    return jax.shard_map(
        on_device,
        mesh=mesh,
        in_specs=(
            P("row", "col", None, None, None),
            P("row", "col", None),
            P("row", "col"),
            P("col", "row", None, None, None),
            P("col", "row", None),
            P("col", "row"),
            P("row", "col", None),
            P("row", "col", None),
        ),
        out_specs=P(("row", "col"), None, None, None, None),
        check_vma=False,
    )
```

time: 319 us -> 262 us (0.82)
  local copies, waits for them, and re-layouts: 100 us -> 3.51 us
  starting transfers between devices: 13.8 us -> 72.6 us
  matrix products: 36.1 us -> 0 us
  Pallas kernels: 0 us -> 33.9 us
  blocking collectives: 157 us -> 128 us
  waiting for transfers between devices: 0.02 us -> 21.6 us
  other arithmetic: 10.4 us -> 1.32 us
    gather x4 -> x0, local copies, waits for them, and re-layouts: 68.3 us -> none  [the longest x2 45.6 us: stop_product(): chosen = flat_blocks[index]]
    ppermute x6 -> x12, starting transfers between devices: 13.8 us -> 72.6 us  [move(): return lax.ppermute(value, ('row', 'col'), pairs)]
    dot_general x2 -> x0, matrix products: 36.1 us -> none  [stop_product(): jnp.einsum('iapq,iafqr->ifpr', first_blocks, chosen, preferred_element_ty...]
    pallas_call x0 -> x4, Pallas kernels: none -> 33.9 us  [the longest x1 16.9 us: first_stop(): pl.pallas_call(first_stop_kernel, grid_spec=pltpu.PrefetchScalarGridSpec(...]
    all_to_all x1, blocking collectives: 157 us -> 128 us  [on_device(): lax.all_to_all(outgoing.reshape(devices, per_owner, side, side), ('row',...]
    ppermute x6 -> x12, waiting for transfers between devices: 0.02 us -> 21.6 us  [move(): return lax.ppermute(value, ('row', 'col'), pairs)]
    concatenate x3 -> x0, local copies, waits for them, and re-layouts: 18.5 us -> none  [the longest x2 13.9 us: stop_product(): jnp.concatenate([second_blocks.reshape(-1, side, side), jnp.zeros((1, sid...]
    unnamed x4 -> x22, local copies, waits for them, and re-layouts: 11.2 us -> 2.68 us
  transfers between devices with their start and end apart: 6 -> 12, of which waited for: 0 -> 2; matrix products, arithmetic and copies ran while one was open for 28% -> 1% of each run, Pallas kernels for 0% -> 6%
where the time goes in v1:
time: 262 us; the launch traced here: 261 us
  blocking collectives  128 us (49%)
  starting transfers between devices  72.6 us (28%)
  Pallas kernels  33.9 us (13%)
  waiting for transfers between devices  21.6 us (8%)
  local copies, waits for them, and re-layouts  3.51 us (1%)
    all_to_all x1, blocking collectives, on_device(): lax.all_to_all(outgoing.reshape(devices, per_owner, side, side), ('row',...  128 us
    ppermute x12, starting transfers between devices, move(): return lax.ppermute(value, ('row', 'col'), pairs)  72.6 us
    ppermute x12, waiting for transfers between devices, move(): return lax.ppermute(value, ('row', 'col'), pairs)  21.6 us
    pallas_call x1, Pallas kernels, first_stop(): pl.pallas_call(first_stop_kernel, grid_spec=pltpu.PrefetchScalarGridSpec(...  16.9 us
    pallas_call x1, Pallas kernels, last_stop(): pl.pallas_call(last_stop_kernel, grid_spec=pltpu.PrefetchScalarGridSpec(n...  13.7 us
  transfers between devices with their start and end apart: 12, of which 2 were waited for; matrix products, arithmetic and copies ran while one was open for 1% of the time, Pallas kernels for 6%

profile of v1, /device:TPU:1, one launch (start us, length us, event | category | flops | bytes accessed | tf_op | source)
XLA Modules:
  0.0 260.8 jit_solution(15359834217208529499)
XLA Ops:
  0.0 3.3 %collective-permute-start.6 = (bf16[160,128,128]{2,1,0:T(8,128)(2,1)}, bf16[160,128,128]{2,1,0:T(8,128)(2,1)}, u32[]{:S(2)}, u32[]{:S(2)}) collective-permute-start(bf16[160,128,128]{2,1,0:T(8,128)(2,1)} %bitcast.10), channel_id=1, source_target_pairs={{1,0},{2,1},{3,2},{4,3},{5,4},{6,5},{7,6},{9,8},{10,9},{11,10},{12... | collective-permute-start | bytes 15728648 | tf_op jit(solution)/shard_map/ppermute | solution.py:22
  3.4 2.5 copy-done
  5.9 2.2 collective-permute-start
  8.1 2.0 collective-permute-start.1
  10.1 2.1 collective-permute-start.5
  12.3 0.7 collective-permute-start.2
  13.2 0.7 reshape_squeeze.15.kept_columns
  13.8 0.1 copy.12
  13.9 0.1 reshape_squeeze.14
  14.0 0.6 pad_add_fusion.1.first_meta
  14.6 0.6 pad_add_fusion.second_meta
  15.3 16.9 %shard_map.83 = (f32[10,12,128,128]{3,2,1,0:T(8,128)}, bf16[256,128,128]{2,1,0:T(8,128)(2,1)}) custom-call(s32[90]{0:T(128)} %pad_add_fusion.1.first_meta, s32[180]{0:T(256)} %pad_add_fusion.second_meta, s32[120]{0:T(128)} %reshape_squeeze.15.kept_columns, bf16[10,8,128,128]{3,2,1,0:T(8,128)(2,1)} %bitcast.2.first, bf16[160,128,128]{2,1,0:T(8,128)(2,1)} %bitcast.11), custom_call_target="tpu_custom_call" | custom-call | flops 8053063680 | bytes 31457280 | tf_op jit(solution)/shard_map/pallas_call | solution.py:176
  32.2 2.1 collective-permute-start.3
  34.3 2.1 collective-permute-start.4
  36.4 5.5 %collective-permute-start.9 = (bf16[10,8,128,128]{3,2,1,0:T(8,128)(2,1)}, bf16[10,8,128,128]{3,2,1,0:T(8,128)(2,1)S(1)}, u32[]{:S(2)}, u32[]{:S(2)}) collective-permute-start(bf16[10,8,128,128]{3,2,1,0:T(8,128)(2,1)} %bitcast.2.first), channel_id=1, source_target_pairs={{0,112},{1,113},{8,120},{9,121},{16,0},{17,1},{24,8},{25,9},{32,16... | collective-permute-start | bytes 7864328 | tf_op jit(solution)/shard_map/ppermute | solution.py:22
  41.9 20.8 %collective-permute-done.6.second = bf16[160,128,128]{2,1,0:T(8,128)(2,1)} collective-permute-done((bf16[160,128,128]{2,1,0:T(8,128)(2,1)}, bf16[160,128,128]{2,1,0:T(8,128)(2,1)}, u32[]{:S(2)}, u32[]{:S(2)}) %collective-permute-start.6) | collective-permute-done | bytes 5242912 | tf_op jit(solution)/shard_map/ppermute | solution.py:22
  62.7 2.1 collective-permute-start.10
  64.7 2.0 collective-permute-start.11
  66.8 3.5 %collective-permute-start.7 = (s32[90]{0:T(128)S(1)}, s32[90]{0:T(128)S(1)}, u32[]{:S(2)}, u32[]{:S(2)}) collective-permute-start(s32[90]{0:T(128)S(1)} %copy-done.9), channel_id=1, source_target_pairs={{0,112},{1,113},{2,114},{3,115},{4,116},{5,117},{6,118},{7,119},{8... | collective-permute-start | bytes 1088 | tf_op jit(solution)/shard_map/ppermute | solution.py:22
  70.3 45.0 %collective-permute-start.8 = (s32[180]{0:T(256)S(1)}, s32[180]{0:T(256)S(1)}, u32[]{:S(2)}, u32[]{:S(2)}) collective-permute-start(s32[180]{0:T(256)S(1)} %copy-done.6), channel_id=1, source_target_pairs={{0,15},{1,0},{2,1},{3,2},{4,3},{5,4},{6,5},{7,6},{8,7},{9,8},{10,9... | collective-permute-start | bytes 2168 | tf_op jit(solution)/shard_map/ppermute | solution.py:22
  115.4 0.7 collective-permute-done.8.second_meta
  116.1 13.7 %shard_map.84 = bf16[256,128,128]{2,1,0:T(8,128)(2,1)} custom-call(s32[90]{0:T(128)S(1)} %collective-permute-done.7.first_meta, s32[180]{0:T(256)S(1)} %collective-permute-done.8.second_meta, s32[120]{0:T(128)S(1)} %copy-done.1, s32[120]{0:T(128)S(1)} %bitcast.13, s32[2]{0:T(128)S(1)} %add_convert_fusion.place, ...), custom_call_target="tpu_custom_call", output_to_operand_aliasing={{}: (12, {})} | custom-call | flops 1024 | bytes 1024 | tf_op jit(solution)/shard_map/pallas_call | solution.py:217
  129.8 127.7 %all_to_all.5.source = bf16[128,2,128,128]{3,2,1,0:T(8,128)(2,1)S(1)} all-to-all(bf16[128,2,128,128]{3,2,1,0:T(8,128)(2,1)} %bitcast.14), channel_id=1, replica_groups=mesh['row'=8,'col'=16] {'row','col'}, dimensions={0} | all-to-all | bytes 16777216 | tf_op jit(solution)/shard_map/all_to_all | solution.py:361
  257.6 3.3 %shard_map.85 = bf16[128,2,128,128]{3,2,1,0:T(8,128)(2,1)} custom-call(bf16[128,2,128,128]{3,2,1,0:T(8,128)(2,1)S(1)} %all_to_all.5.source), custom_call_target="tpu_custom_call" | custom-call | tf_op jit(solution)/shard_map/pallas_call | solution.py:291
  (34 shorter events, 0.4 us)
Async XLA Ops:
  0.0 62.7 %collective-permute-start.6 = (bf16[160,128,128]{2,1,0:T(8,128)(2,1)}, bf16[160,128,128]{2,1,0:T(8,128)(2,1)}, u32[]{:S(2)}, u32[]{:S(2)}) collective-permute-start(bf16[160,128,128]{2,1,0:T(8,128)(2,1)} %bitcast.10), channel_id=1, source_target_pairs={{1,0},{2,1},{3,2},{4,3},{5,4},{6,5},{7,6},{9,8},{10,9},{11,10},{12... | collective-permute-start | bytes 15728648 | tf_op jit(solution)/shard_map/ppermute | solution.py:22
  3.3 2.5 copy-start
  5.8 7.1 %copy-start.4 = (s32[1,10,8]{1,2,0:T(8,128)S(1)}, s32[1,10,8]{1,2,0:T(8,128)}, u32[]{:S(2)}) copy-start(s32[1,10,8]{1,2,0:T(8,128)} %param.9) | copy-start | bytes 964
  5.8 7.3 %copy-start.3 = (s32[1,10,12]{2,0,1:T(1,128)S(1)}, s32[1,10,12]{2,0,1:T(1,128)}, u32[]{:S(2)}) copy-start(s32[1,10,12]{2,0,1:T(1,128)} %param.14) | copy-start | bytes 1444
  5.8 8.0 %copy-start.5 = (s32[1,20,8]{1,2,0:T(8,128)S(1)}, s32[1,20,8]{1,2,0:T(8,128)}, u32[]{:S(2)}) copy-start(s32[1,20,8]{1,2,0:T(8,128)} %param.12) | copy-start | bytes 1924
  5.8 8.2 %copy-start.8 = (s32[1,10]{1,0:T(1,128)S(1)}, s32[1,10]{1,0:T(1,128)}, u32[]{:S(2)}) copy-start(s32[1,10]{1,0:T(1,128)} %param.10) | copy-start | bytes 124
  5.8 8.7 %copy-start.7 = (s32[1,20]{1,0:T(1,128)S(1)}, s32[1,20]{1,0:T(1,128)}, u32[]{:S(2)}) copy-start(s32[1,20]{1,0:T(1,128)} %param.13) | copy-start | bytes 244
  5.9 26.3 %collective-permute-start = (bf16[72,128,128]{2,1,0:T(8,128)(2,1)}, bf16[72,128,128]{2,1,0:T(8,128)(2,1)}, u32[]{:S(2)}, u32[]{:S(2)}) collective-permute-start(bf16[72,128,128]{2,1,0:T(8,128)(2,1)} %get-tuple-element.22), channel_id=1, source_target_pairs={{0,16},{8,24},{16,0},{24,8},{32,48},{40,56},{48,32},{56,40},{64,80... | collective-permute-start | bytes 7077896 | tf_op jit(solution)/shard_map/ppermute | solution.py:22
  8.1 24.1 %collective-permute-start.1 = (bf16[72,128,128]{2,1,0:T(8,128)(2,1)}, bf16[72,128,128]{2,1,0:T(8,128)(2,1)}, u32[]{:S(2)}, u32[]{:S(2)}) collective-permute-start(bf16[72,128,128]{2,1,0:T(8,128)(2,1)} %get-tuple-element.23), channel_id=1, source_target_pairs={{0,7},{8,15},{16,23},{24,31},{32,39},{40,47},{48,55},{56,63},{64,7... | collective-permute-start | bytes 7077896 | tf_op jit(solution)/shard_map/ppermute | solution.py:22
  10.1 31.7 %collective-permute-start.5 = (bf16[10,8,128,128]{3,2,1,0:T(8,128)(2,1)}, bf16[10,8,128,128]{3,2,1,0:T(8,128)(2,1)}, u32[]{:S(2)}, u32[]{:S(2)}) collective-permute-start(bf16[10,8,128,128]{3,2,1,0:T(8,128)(2,1)} %bitcast.2.first), channel_id=1, source_target_pairs={{2,114},{3,115},{4,116},{5,117},{6,118},{7,119},{10,122},{11,123},... | collective-permute-start | bytes 7864328 | tf_op jit(solution)/shard_map/ppermute | solution.py:22
  12.3 19.9 %collective-permute-start.2 = (bf16[16,128,128]{2,1,0:T(8,128)(2,1)S(1)}, bf16[16,128,128]{2,1,0:T(8,128)(2,1)S(1)}, u32[]{:S(2)}, u32[]{:S(2)}) collective-permute-start(bf16[16,128,128]{2,1,0:T(8,128)(2,1)S(1)} %get-tuple-element.24), channel_id=1, source_target_pairs={{0,15},{8,7},{16,31},{24,23},{32,47},{40,39},{48,63},{56,55},{64,7... | collective-permute-start | bytes 1572872 | tf_op jit(solution)/shard_map/ppermute | solution.py:22
  15.2 51.5 %copy-start.9 = (s32[90]{0:T(128)S(1)}, s32[90]{0:T(128)}, u32[]{:S(2)}) copy-start(s32[90]{0:T(128)} %pad_add_fusion.1.first_meta) | copy-start | bytes 1084
  15.2 55.0 %copy-start.6 = (s32[180]{0:T(256)S(1)}, s32[180]{0:T(256)}, u32[]{:S(2)}) copy-start(s32[180]{0:T(256)} %pad_add_fusion.second_meta) | copy-start | bytes 2164
  15.2 100.9 %copy-start.1 = (s32[120]{0:T(128)S(1)}, s32[120]{0:T(128)}, u32[]{:S(2)}) copy-start(s32[120]{0:T(128)} %reshape_squeeze.15.kept_columns) | copy-start | bytes 1444
  15.2 100.9 %copy-start.2 = (s32[1,120,1]{1,2,0:T(1,128)S(1)}, s32[1,120,1]{1,2,0:T(1,128)}, u32[]{:S(2)}) copy-start(s32[1,120,1]{1,2,0:T(1,128)} %param.15) | copy-start | bytes 1444
  32.2 9.7 %collective-permute-start.3 = (bf16[72,128,128]{2,1,0:T(8,128)(2,1)}, bf16[72,128,128]{2,1,0:T(8,128)(2,1)}, u32[]{:S(2)}, u32[]{:S(2)}) collective-permute-start(bf16[72,128,128]{2,1,0:T(8,128)(2,1)} %collective-permute-done), channel_id=1, source_target_pairs={{0,24},{8,16},{16,8},{24,0},{32,56},{40,48},{48,40},{56,32},{64,88... | collective-permute-start | bytes 7077896 | tf_op jit(solution)/shard_map/ppermute | solution.py:22
  34.3 7.6 %collective-permute-start.4 = (bf16[72,128,128]{2,1,0:T(8,128)(2,1)}, bf16[72,128,128]{2,1,0:T(8,128)(2,1)}, u32[]{:S(2)}, u32[]{:S(2)}) collective-permute-start(bf16[72,128,128]{2,1,0:T(8,128)(2,1)} %collective-permute-done.1), channel_id=1, source_target_pairs={{7,31},{15,23},{23,15},{31,7},{39,63},{47,55},{55,47},{63,39},{71,... | collective-permute-start | bytes 7077896 | tf_op jit(solution)/shard_map/ppermute | solution.py:22
  36.4 79.0 %collective-permute-start.9 = (bf16[10,8,128,128]{3,2,1,0:T(8,128)(2,1)}, bf16[10,8,128,128]{3,2,1,0:T(8,128)(2,1)S(1)}, u32[]{:S(2)}, u32[]{:S(2)}) collective-permute-start(bf16[10,8,128,128]{3,2,1,0:T(8,128)(2,1)} %bitcast.2.first), channel_id=1, source_target_pairs={{0,112},{1,113},{8,120},{9,121},{16,0},{17,1},{24,8},{25,9},{32,16... | collective-permute-start | bytes 7864328 | tf_op jit(solution)/shard_map/ppermute | solution.py:22
  62.7 53.5 %collective-permute-start.10 = (bf16[72,128,128]{2,1,0:T(8,128)(2,1)}, bf16[72,128,128]{2,1,0:T(8,128)(2,1)}, u32[]{:S(2)}, u32[]{:S(2)}) collective-permute-start(bf16[72,128,128]{2,1,0:T(8,128)(2,1)} %collective-permute-done.3), channel_id=1, source_target_pairs={{0,7},{8,15},{16,23},{24,31},{32,39},{40,47},{48,55},{56,63},{64,7... | collective-permute-start | bytes 7077896 | tf_op jit(solution)/shard_map/ppermute | solution.py:22
  64.7 51.4 %collective-permute-start.11 = (bf16[72,128,128]{2,1,0:T(8,128)(2,1)}, bf16[72,128,128]{2,1,0:T(8,128)(2,1)}, u32[]{:S(2)}, u32[]{:S(2)}) collective-permute-start(bf16[72,128,128]{2,1,0:T(8,128)(2,1)} %collective-permute-done.4), channel_id=1, source_target_pairs={{7,23},{15,31},{23,7},{31,15},{39,55},{47,63},{55,39},{63,47},{71,... | collective-permute-start | bytes 7077896 | tf_op jit(solution)/shard_map/ppermute | solution.py:22
  66.8 48.6 %collective-permute-start.7 = (s32[90]{0:T(128)S(1)}, s32[90]{0:T(128)S(1)}, u32[]{:S(2)}, u32[]{:S(2)}) collective-permute-start(s32[90]{0:T(128)S(1)} %copy-done.9), channel_id=1, source_target_pairs={{0,112},{1,113},{2,114},{3,115},{4,116},{5,117},{6,118},{7,119},{8... | collective-permute-start | bytes 1088 | tf_op jit(solution)/shard_map/ppermute | solution.py:22
  70.3 45.9 %collective-permute-start.8 = (s32[180]{0:T(256)S(1)}, s32[180]{0:T(256)S(1)}, u32[]{:S(2)}, u32[]{:S(2)}) collective-permute-start(s32[180]{0:T(256)S(1)} %copy-done.6), channel_id=1, source_target_pairs={{0,15},{1,0},{2,1},{3,2},{4,3},{5,4},{6,5},{7,6},{8,7},{9,8},{10,9... | collective-permute-start | bytes 2168 | tf_op jit(solution)/shard_map/ppermute | solution.py:22

commit v2 on v1

--- a/solution.py
+++ b/solution.py
@@ -8,6 +8,7 @@
 from jax.sharding import PartitionSpec as P
 
 VMEM_LIMIT = 40 * 1024 * 1024
+LARGE_VMEM_LIMIT = 62 * 1024 * 1024
 TABLE_ROWS = 20
 
 
@@ -198,7 +199,7 @@
             jax.ShapeDtypeStruct((rows, kept, side, side), jnp.float32),
             jax.ShapeDtypeStruct((outgoing, side, side), second.dtype),
         ],
-        compiler_params=pltpu.CompilerParams(vmem_limit_bytes=62 * 1024 * 1024),
+        compiler_params=pltpu.CompilerParams(vmem_limit_bytes=LARGE_VMEM_LIMIT),
         cost_estimate=pl.CostEstimate(
             flops=4 * rows * slots * kept * side**3,
             bytes_accessed=2 * (rows * (slots * 2 + kept * 4) + 2 * second_total) * side**2,
@@ -252,19 +253,24 @@
 
 
 def cut_kernel(place, source, *rest):
-    targets, sem = rest[:-1], rest[-1]
+    held, in_sem, out_sem = rest[-3:]
+    targets = rest[:-3]
 
     @pl.when(place[0] != 0)
     def _():
-        copies, at = [], 0
+        loads, stores, at = [], [], 0
         for n, target in enumerate(targets):
-            piece = source.at[pl.ds(at, target.shape[0])]
-            copies.append(pltpu.make_async_copy(piece, target, sem.at[n]))
+            piece = pl.ds(at, target.shape[0])
+            loads.append(pltpu.make_async_copy(source.at[piece], held.at[piece], in_sem.at[n]))
+            stores.append(pltpu.make_async_copy(held.at[piece], target, out_sem.at[n]))
             at += target.shape[0]
-        for copy in copies:
-            copy.start()
-        for copy in copies:
-            copy.wait()
+        for load in loads:
+            load.start()
+        for load, store in zip(loads, stores):
+            load.wait()
+            store.start()
+        for store in stores:
+            store.wait()
 
 
 def cut(place, value, sizes):
@@ -273,8 +279,12 @@
         in_specs=[pl.BlockSpec(memory_space=pltpu.SMEM), pl.BlockSpec(memory_space=pl.ANY)],
         out_specs=[pl.BlockSpec(memory_space=pl.ANY)] * len(sizes),
         out_shape=[jax.ShapeDtypeStruct((size,) + value.shape[1:], value.dtype) for size in sizes],
-        scratch_shapes=[pltpu.SemaphoreType.DMA((len(sizes),))],
-        compiler_params=pltpu.CompilerParams(vmem_limit_bytes=VMEM_LIMIT),
+        scratch_shapes=[
+            pltpu.VMEM(value.shape, value.dtype),
+            pltpu.SemaphoreType.DMA((len(sizes),)),
+            pltpu.SemaphoreType.DMA((len(sizes),)),
+        ],
+        compiler_params=pltpu.CompilerParams(vmem_limit_bytes=LARGE_VMEM_LIMIT),
         cost_estimate=pl.CostEstimate(flops=1024, bytes_accessed=1024, transcendentals=0),
     )(place, value)
 
@@ -307,7 +317,7 @@
     first = a_blocks[0]
     second = b_blocks[0].reshape(-1, side, side)
     total = second.shape[0]
-    large = total * 9 // 20
+    large = total * 17 // 40
     spot = lax.axis_index("col") % span
     crossing = (spot == 0).astype(jnp.int32)[None]
 
@@ -319,6 +329,8 @@
 
     def to_last(r, c):
         return r, c + span - 1
+
+    middle = span - 3
 
     def at(place, step):
         return lambda r, c: step(r, c) if c % span == place else None
@@ -326,7 +338,7 @@
     part_a, part_b, part_c = cut(crossing, second, (large, large, total - 2 * large))
     part_a = move(part_a, at(0, near))
     part_b = move(part_b, at(0, to_last))
-    part_c = move(part_c, at(0, lambda r, c: (r, c - 1)))
+    part_c = move(part_c, at(0, lambda r, c: far(r, c + middle)))
     early = move(first, lambda r, c: (r - 1, c) if c % span > 1 else None)
     second_next = move(second, lambda r, c: (r, c - 1) if c % span else None)
 
@@ -345,12 +357,16 @@
     part_a = move(part_a, at(0, far))
     part_b = move(part_b, at(span - 1, far))
 
-    part_a, part_b, early, second_next, first_meta, second_meta = lax.optimization_barrier(
-        (part_a, part_b, early, second_next, own_first_meta, own_second_meta)
+    part_a, part_b, part_c, early, second_next, first_meta = lax.optimization_barrier(
+        (part_a, part_b, part_c, early, second_next, own_first_meta)
     )
     part_a = move(part_a, at(0, to_last))
     part_b = move(part_b, at(span - 1, near))
+    part_c = move(part_c, at(middle, near))
     first_meta = move(first_meta, lambda r, c: (r - 1, c))
+
+    part_c, second_meta = lax.optimization_barrier((part_c, own_second_meta))
+    part_c = move(part_c, at(middle, lambda r, c: (r, c + 2)))
     second_meta = move(second_meta, lambda r, c: (r, c - 1))
 
     place = jnp.stack([spot == span - 1, spot < 2]).astype(jnp.int32)

time: 262 us -> 228 us (0.87)
  starting transfers between devices: 72.6 us -> 41.6 us
  blocking collectives: 128 us -> 113 us
  waiting for transfers between devices: 21.6 us -> 36.2 us
    ppermute x12 -> x14, starting transfers between devices: 72.6 us -> 41.6 us  [move(): return lax.ppermute(value, ('row', 'col'), pairs)]
    all_to_all x1, blocking collectives: 128 us -> 113 us  [on_device(): lax.all_to_all(outgoing.reshape(devices, per_owner, side, side), ('row',...]
    ppermute x12 -> x14, waiting for transfers between devices: 21.6 us -> 36.2 us  [move(): return lax.ppermute(value, ('row', 'col'), pairs)]
  transfers between devices with their start and end apart: 12 -> 14, of which waited for: 2 -> 3; matrix products, arithmetic and copies ran while one was open for 1% -> 1% of each run, Pallas kernels for 6% -> 7%
where the time goes in v2:
time: 228 us; the launch traced here: 227 us
  blocking collectives  113 us (50%)
  starting transfers between devices  41.6 us (18%)
  waiting for transfers between devices  36.2 us (16%)
  Pallas kernels  33.9 us (15%)
    all_to_all x1, blocking collectives, on_device(): lax.all_to_all(outgoing.reshape(devices, per_owner, side, side), ('row',...  113 us
    ppermute x14, starting transfers between devices, move(): return lax.ppermute(value, ('row', 'col'), pairs)  41.6 us
    ppermute x14, waiting for transfers between devices, move(): return lax.ppermute(value, ('row', 'col'), pairs)  36.2 us
    pallas_call x1, Pallas kernels, first_stop(): pl.pallas_call(first_stop_kernel, grid_spec=pltpu.PrefetchScalarGridSpec(...  16.9 us
    pallas_call x1, Pallas kernels, last_stop(): pl.pallas_call(last_stop_kernel, grid_spec=pltpu.PrefetchScalarGridSpec(n...  13.7 us
  transfers between devices with their start and end apart: 14, of which 3 were waited for; matrix products, arithmetic and copies ran while one was open for 1% of the time, Pallas kernels for 7%

profile of v2, /device:TPU:1, one launch (start us, length us, event | category | flops | bytes accessed | tf_op | source)
XLA Modules:
  0.0 226.8 jit_solution(13469987899450129498)
XLA Ops:
  0.0 3.3 %collective-permute-start.6 = (bf16[160,128,128]{2,1,0:T(8,128)(2,1)}, bf16[160,128,128]{2,1,0:T(8,128)(2,1)}, u32[]{:S(2)}, u32[]{:S(2)}) collective-permute-start(bf16[160,128,128]{2,1,0:T(8,128)(2,1)} %bitcast.12), channel_id=1, source_target_pairs={{1,0},{2,1},{3,2},{4,3},{5,4},{6,5},{7,6},{9,8},{10,9},{11,10},{12... | collective-permute-start | bytes 15728648 | tf_op jit(solution)/shard_map/ppermute | solution.py:23
  3.5 2.0 collective-permute-start
  5.5 2.0 collective-permute-start.1
  7.5 2.1 collective-permute-start.5
  9.6 0.7 collective-permute-start.2
  10.7 0.6 pad_add_fusion.second_meta
  11.3 0.7 pad_add_fusion.1.first_meta
  12.0 0.6 reshape_squeeze.15.kept_columns
  12.6 16.9 %shard_map.83 = (f32[10,12,128,128]{3,2,1,0:T(8,128)}, bf16[256,128,128]{2,1,0:T(8,128)(2,1)}) custom-call(s32[90]{0:T(128)} %pad_add_fusion.1.first_meta, s32[180]{0:T(256)} %pad_add_fusion.second_meta, s32[120]{0:T(128)} %reshape_squeeze.15.kept_columns, bf16[10,8,128,128]{3,2,1,0:T(8,128)(2,1)} %bitcast.17, bf16[160,128,128]{2,1,0:T(8,128)(2,1)} %bitcast.14), custom_call_target="tpu_custom_call" | custom-call | flops 8053063680 | bytes 31457280 | tf_op jit(solution)/shard_map/pallas_call | solution.py:177
  29.5 2.1 collective-permute-start.3
  31.6 2.0 collective-permute-start.4
  33.6 5.5 %collective-permute-start.10 = (bf16[10,8,128,128]{3,2,1,0:T(8,128)(2,1)}, bf16[10,8,128,128]{3,2,1,0:T(8,128)(2,1)S(1)}, u32[]{:S(2)}, u32[]{:S(2)}) collective-permute-start(bf16[10,8,128,128]{3,2,1,0:T(8,128)(2,1)} %bitcast.18), channel_id=1, source_target_pairs={{0,112},{1,113},{8,120},{9,121},{16,0},{17,1},{24,8},{25,9},{32,16... | collective-permute-start | bytes 7864328 | tf_op jit(solution)/shard_map/ppermute | solution.py:23
  39.1 23.8 %collective-permute-done.6.second = bf16[160,128,128]{2,1,0:T(8,128)(2,1)} collective-permute-done((bf16[160,128,128]{2,1,0:T(8,128)(2,1)}, bf16[160,128,128]{2,1,0:T(8,128)(2,1)}, u32[]{:S(2)}, u32[]{:S(2)}) %collective-permute-start.6) | collective-permute-done | bytes 5242912 | tf_op jit(solution)/shard_map/ppermute | solution.py:23
  63.0 2.0 collective-permute-start.11
  65.0 2.0 collective-permute-start.12
  67.0 1.6 collective-permute-start.8
  68.6 0.7 collective-permute-start.13
  69.3 3.6 %collective-permute-start.7 = (s32[90]{0:T(128)S(1)}, s32[90]{0:T(128)S(1)}, u32[]{:S(2)}, u32[]{:S(2)}) collective-permute-start(s32[90]{0:T(128)S(1)} %copy-done.8), channel_id=1, source_target_pairs={{0,112},{1,113},{2,114},{3,115},{4,116},{5,117},{6,118},{7,119},{8... | collective-permute-start | bytes 1088 | tf_op jit(solution)/shard_map/ppermute | solution.py:23
  72.9 11.6 %collective-permute-done.10.late = bf16[10,8,128,128]{3,2,1,0:T(8,128)(2,1)S(1)} collective-permute-done((bf16[10,8,128,128]{3,2,1,0:T(8,128)(2,1)}, bf16[10,8,128,128]{3,2,1,0:T(8,128)(2,1)S(1)}, u32[]{:S(2)}, u32[]{:S(2)}) %collective-permute-start.10) | collective-permute-done | bytes 2621472 | tf_op jit(solution)/shard_map/ppermute | solution.py:23
  84.5 12.0 %collective-permute-start.9 = (s32[180]{0:T(256)S(1)}, s32[180]{0:T(256)S(1)}, u32[]{:S(2)}, u32[]{:S(2)}) collective-permute-start(s32[180]{0:T(256)S(1)} %copy-done.5), channel_id=1, source_target_pairs={{0,15},{1,0},{2,1},{3,2},{4,3},{5,4},{6,5},{7,6},{8,7},{9,8},{10,9... | collective-permute-start | bytes 2168 | tf_op jit(solution)/shard_map/ppermute | solution.py:23
  96.6 0.7 collective-permute-done.9.second_meta
  97.3 13.7 %shard_map.84 = bf16[256,128,128]{2,1,0:T(8,128)(2,1)} custom-call(s32[90]{0:T(128)S(1)} %collective-permute-done.7.first_meta, s32[180]{0:T(256)S(1)} %collective-permute-done.9.second_meta, s32[120]{0:T(128)S(1)} %copy-done, s32[120]{0:T(128)S(1)} %bitcast.10, s32[2]{0:T(128)S(1)} %add_convert_fusion.place, ...), custom_call_target="tpu_custom_call", output_to_operand_aliasing={{}: (12, {})} | custom-call | flops 1024 | bytes 1024 | tf_op jit(solution)/shard_map/pallas_call | solution.py:218
  111.0 112.5 %all_to_all.5.source = bf16[128,2,128,128]{3,2,1,0:T(8,128)(2,1)S(1)} all-to-all(bf16[128,2,128,128]{3,2,1,0:T(8,128)(2,1)} %bitcast.11), channel_id=1, replica_groups=mesh['row'=8,'col'=16] {'row','col'}, dimensions={0} | all-to-all | bytes 16777216 | tf_op jit(solution)/shard_map/all_to_all | solution.py:377
  223.5 3.3 %shard_map.85 = bf16[128,2,128,128]{3,2,1,0:T(8,128)(2,1)} custom-call(bf16[128,2,128,128]{3,2,1,0:T(8,128)(2,1)S(1)} %all_to_all.5.source), custom_call_target="tpu_custom_call" | custom-call | tf_op jit(solution)/shard_map/pallas_call | solution.py:301
  (36 shorter events, 0.6 us)
Async XLA Ops:
  0.0 63.0 %collective-permute-start.6 = (bf16[160,128,128]{2,1,0:T(8,128)(2,1)}, bf16[160,128,128]{2,1,0:T(8,128)(2,1)}, u32[]{:S(2)}, u32[]{:S(2)}) collective-permute-start(bf16[160,128,128]{2,1,0:T(8,128)(2,1)} %bitcast.12), channel_id=1, source_target_pairs={{1,0},{2,1},{3,2},{4,3},{5,4},{6,5},{7,6},{9,8},{10,9},{11,10},{12... | collective-permute-start | bytes 15728648 | tf_op jit(solution)/shard_map/ppermute | solution.py:23
  3.3 7.0 %copy-start.3 = (s32[1,10,8]{1,2,0:T(8,128)S(1)}, s32[1,10,8]{1,2,0:T(8,128)}, u32[]{:S(2)}) copy-start(s32[1,10,8]{1,2,0:T(8,128)} %param.9) | copy-start | bytes 964
  3.4 7.2 %copy-start.4 = (s32[1,20,8]{1,2,0:T(8,128)S(1)}, s32[1,20,8]{1,2,0:T(8,128)}, u32[]{:S(2)}) copy-start(s32[1,20,8]{1,2,0:T(8,128)} %param.12) | copy-start | bytes 1924
  3.4 7.3 %copy-start.6 = (s32[1,20]{1,0:T(1,128)S(1)}, s32[1,20]{1,0:T(1,128)}, u32[]{:S(2)}) copy-start(s32[1,20]{1,0:T(1,128)} %param.13) | copy-start | bytes 244
  3.4 7.9 %copy-start.7 = (s32[1,10]{1,0:T(1,128)S(1)}, s32[1,10]{1,0:T(1,128)}, u32[]{:S(2)}) copy-start(s32[1,10]{1,0:T(1,128)} %param.10) | copy-start | bytes 124
  3.4 8.6 %copy-start.2 = (s32[1,10,12]{2,0,1:T(1,128)S(1)}, s32[1,10,12]{2,0,1:T(1,128)}, u32[]{:S(2)}) copy-start(s32[1,10,12]{2,0,1:T(1,128)} %param.14) | copy-start | bytes 1444
  3.5 26.0 %collective-permute-start = (bf16[68,128,128]{2,1,0:T(8,128)(2,1)}, bf16[68,128,128]{2,1,0:T(8,128)(2,1)}, u32[]{:S(2)}, u32[]{:S(2)}) collective-permute-start(bf16[68,128,128]{2,1,0:T(8,128)(2,1)} %get-tuple-element.24), channel_id=1, source_target_pairs={{0,16},{8,24},{16,0},{24,8},{32,48},{40,56},{48,32},{56,40},{64,80... | collective-permute-start | bytes 6684680 | tf_op jit(solution)/shard_map/ppermute | solution.py:23
  5.5 24.0 %collective-permute-start.1 = (bf16[68,128,128]{2,1,0:T(8,128)(2,1)}, bf16[68,128,128]{2,1,0:T(8,128)(2,1)}, u32[]{:S(2)}, u32[]{:S(2)}) collective-permute-start(bf16[68,128,128]{2,1,0:T(8,128)(2,1)} %get-tuple-element.25), channel_id=1, source_target_pairs={{0,7},{8,15},{16,23},{24,31},{32,39},{40,47},{48,55},{56,63},{64,7... | collective-permute-start | bytes 6684680 | tf_op jit(solution)/shard_map/ppermute | solution.py:23
  7.5 31.6 %collective-permute-start.5 = (bf16[10,8,128,128]{3,2,1,0:T(8,128)(2,1)}, bf16[10,8,128,128]{3,2,1,0:T(8,128)(2,1)}, u32[]{:S(2)}, u32[]{:S(2)}) collective-permute-start(bf16[10,8,128,128]{3,2,1,0:T(8,128)(2,1)} %bitcast.16), channel_id=1, source_target_pairs={{2,114},{3,115},{4,116},{5,117},{6,118},{7,119},{10,122},{11,123},... | collective-permute-start | bytes 7864328 | tf_op jit(solution)/shard_map/ppermute | solution.py:23
  9.6 19.9 %collective-permute-start.2 = (bf16[24,128,128]{2,1,0:T(8,128)(2,1)}, bf16[24,128,128]{2,1,0:T(8,128)(2,1)S(1)}, u32[]{:S(2)}, u32[]{:S(2)}) collective-permute-start(bf16[24,128,128]{2,1,0:T(8,128)(2,1)} %get-tuple-element.26), channel_id=1, source_target_pairs={{0,29},{8,21},{16,13},{24,5},{32,61},{40,53},{48,45},{56,37},{64,9... | collective-permute-start | bytes 2359304 | tf_op jit(solution)/shard_map/ppermute | solution.py:23
  12.6 56.7 %copy-start.8 = (s32[90]{0:T(128)S(1)}, s32[90]{0:T(128)}, u32[]{:S(2)}) copy-start(s32[90]{0:T(128)} %pad_add_fusion.1.first_meta) | copy-start | bytes 1084
  12.6 71.9 %copy-start.5 = (s32[180]{0:T(256)S(1)}, s32[180]{0:T(256)}, u32[]{:S(2)}) copy-start(s32[180]{0:T(256)} %pad_add_fusion.second_meta) | copy-start | bytes 2164
  12.6 84.7 %copy-start = (s32[120]{0:T(128)S(1)}, s32[120]{0:T(128)}, u32[]{:S(2)}) copy-start(s32[120]{0:T(128)} %reshape_squeeze.15.kept_columns) | copy-start | bytes 1444
  12.6 84.7 %copy-start.1 = (s32[1,120,1]{1,2,0:T(1,128)S(1)}, s32[1,120,1]{1,2,0:T(1,128)}, u32[]{:S(2)}) copy-start(s32[1,120,1]{1,2,0:T(1,128)} %param.15) | copy-start | bytes 1444
  29.5 9.6 %collective-permute-start.3 = (bf16[68,128,128]{2,1,0:T(8,128)(2,1)}, bf16[68,128,128]{2,1,0:T(8,128)(2,1)}, u32[]{:S(2)}, u32[]{:S(2)}) collective-permute-start(bf16[68,128,128]{2,1,0:T(8,128)(2,1)} %collective-permute-done), channel_id=1, source_target_pairs={{0,24},{8,16},{16,8},{24,0},{32,56},{40,48},{48,40},{56,32},{64,88... | collective-permute-start | bytes 6684680 | tf_op jit(solution)/shard_map/ppermute | solution.py:23
  31.6 7.5 %collective-permute-start.4 = (bf16[68,128,128]{2,1,0:T(8,128)(2,1)}, bf16[68,128,128]{2,1,0:T(8,128)(2,1)}, u32[]{:S(2)}, u32[]{:S(2)}) collective-permute-start(bf16[68,128,128]{2,1,0:T(8,128)(2,1)} %collective-permute-done.1), channel_id=1, source_target_pairs={{7,31},{15,23},{23,15},{31,7},{39,63},{47,55},{55,47},{63,39},{71,... | collective-permute-start | bytes 6684680 | tf_op jit(solution)/shard_map/ppermute | solution.py:23
  33.6 50.9 %collective-permute-start.10 = (bf16[10,8,128,128]{3,2,1,0:T(8,128)(2,1)}, bf16[10,8,128,128]{3,2,1,0:T(8,128)(2,1)S(1)}, u32[]{:S(2)}, u32[]{:S(2)}) collective-permute-start(bf16[10,8,128,128]{3,2,1,0:T(8,128)(2,1)} %bitcast.18), channel_id=1, source_target_pairs={{0,112},{1,113},{8,120},{9,121},{16,0},{17,1},{24,8},{25,9},{32,16... | collective-permute-start | bytes 7864328 | tf_op jit(solution)/shard_map/ppermute | solution.py:23
  63.0 34.3 %collective-permute-start.11 = (bf16[68,128,128]{2,1,0:T(8,128)(2,1)}, bf16[68,128,128]{2,1,0:T(8,128)(2,1)}, u32[]{:S(2)}, u32[]{:S(2)}) collective-permute-start(bf16[68,128,128]{2,1,0:T(8,128)(2,1)} %collective-permute-done.3), channel_id=1, source_target_pairs={{0,7},{8,15},{16,23},{24,31},{32,39},{40,47},{48,55},{56,63},{64,7... | collective-permute-start | bytes 6684680 | tf_op jit(solution)/shard_map/ppermute | solution.py:23
  65.0 32.3 %collective-permute-start.12 = (bf16[68,128,128]{2,1,0:T(8,128)(2,1)}, bf16[68,128,128]{2,1,0:T(8,128)(2,1)}, u32[]{:S(2)}, u32[]{:S(2)}) collective-permute-start(bf16[68,128,128]{2,1,0:T(8,128)(2,1)} %collective-permute-done.4), channel_id=1, source_target_pairs={{7,23},{15,31},{23,7},{31,15},{39,55},{47,63},{55,39},{63,47},{71,... | collective-permute-start | bytes 6684680 | tf_op jit(solution)/shard_map/ppermute | solution.py:23
  67.0 1.6 collective-permute-start.8
  68.6 28.7 %collective-permute-start.13 = (bf16[24,128,128]{2,1,0:T(8,128)(2,1)}, bf16[24,128,128]{2,1,0:T(8,128)(2,1)S(1)}, u32[]{:S(2)}, u32[]{:S(2)}) collective-permute-start(bf16[24,128,128]{2,1,0:T(8,128)(2,1)} %collective-permute-done.8), channel_id=1, source_target_pairs={{5,7},{13,15},{21,23},{29,31},{37,39},{45,47},{53,55},{61,63},{69,... | collective-permute-start | bytes 2359304 | tf_op jit(solution)/shard_map/ppermute | solution.py:23
  69.3 27.2 %collective-permute-start.7 = (s32[90]{0:T(128)S(1)}, s32[90]{0:T(128)S(1)}, u32[]{:S(2)}, u32[]{:S(2)}) collective-permute-start(s32[90]{0:T(128)S(1)} %copy-done.8), channel_id=1, source_target_pairs={{0,112},{1,113},{2,114},{3,115},{4,116},{5,117},{6,118},{7,119},{8... | collective-permute-start | bytes 1088 | tf_op jit(solution)/shard_map/ppermute | solution.py:23
  84.5 12.8 %collective-permute-start.9 = (s32[180]{0:T(256)S(1)}, s32[180]{0:T(256)S(1)}, u32[]{:S(2)}, u32[]{:S(2)}) collective-permute-start(s32[180]{0:T(256)S(1)} %copy-done.5), channel_id=1, source_target_pairs={{0,15},{1,0},{2,1},{3,2},{4,3},{5,4},{6,5},{7,6},{8,7},{9,8},{10,9... | collective-permute-start | bytes 2168 | tf_op jit(solution)/shard_map/ppermute | solution.py:23

commit v3 on v2

--- a/solution.py
+++ b/solution.py
@@ -321,23 +321,20 @@
     spot = lax.axis_index("col") % span
     crossing = (spot == 0).astype(jnp.int32)[None]
 
+    last, middle = span - 1, span - 3
+
     def near(r, c):
         return r ^ 1, c
 
     def far(r, c):
         return r ^ 1, c + span
 
-    def to_last(r, c):
-        return r, c + span - 1
-
-    middle = span - 3
-
     def at(place, step):
         return lambda r, c: step(r, c) if c % span == place else None
 
     part_a, part_b, part_c = cut(crossing, second, (large, large, total - 2 * large))
     part_a = move(part_a, at(0, near))
-    part_b = move(part_b, at(0, to_last))
+    part_b = move(part_b, at(0, lambda r, c: far(r, c + last)))
     part_c = move(part_c, at(0, lambda r, c: far(r, c + middle)))
     early = move(first, lambda r, c: (r - 1, c) if c % span > 1 else None)
     second_next = move(second, lambda r, c: (r, c - 1) if c % span else None)
@@ -354,19 +351,17 @@
         (part_a, part_b, part_c, first, before, blank)
     )
     late = move(first, lambda r, c: (r - 1, c) if c % span < 2 else None)
-    part_a = move(part_a, at(0, far))
-    part_b = move(part_b, at(span - 1, far))
-
-    part_a, part_b, part_c, early, second_next, first_meta = lax.optimization_barrier(
-        (part_a, part_b, part_c, early, second_next, own_first_meta)
-    )
-    part_a = move(part_a, at(0, to_last))
-    part_b = move(part_b, at(span - 1, near))
+    part_a = move(part_a, at(0, lambda r, c: far(r, c + last)))
+    part_b = move(part_b, at(last, near))
+
+    part_a, part_c, early, second_next, first_meta = lax.optimization_barrier(
+        (part_a, part_c, early, second_next, own_first_meta)
+    )
     part_c = move(part_c, at(middle, near))
     first_meta = move(first_meta, lambda r, c: (r - 1, c))
 
     part_c, second_meta = lax.optimization_barrier((part_c, own_second_meta))
-    part_c = move(part_c, at(middle, lambda r, c: (r, c + 2)))
+    part_c = move(part_c, at(middle, lambda r, c: (r, c + last - middle)))
     second_meta = move(second_meta, lambda r, c: (r, c - 1))
 
     place = jnp.stack([spot == span - 1, spot < 2]).astype(jnp.int32)

time: 228 us -> 223 us (0.978)
  waiting for transfers between devices: 36.2 us -> 24.3 us
  blocking collectives: 113 us -> 120 us
  starting transfers between devices: 41.6 us -> 38.4 us
  local copies, waits for them, and re-layouts: 0.96 us -> 3.98 us
    ppermute x14 -> x12, waiting for transfers between devices: 36.2 us -> 24.3 us  [move(): return lax.ppermute(value, ('row', 'col'), pairs)]
    all_to_all x1, blocking collectives: 113 us -> 120 us  [on_device(): lax.all_to_all(outgoing.reshape(devices, per_owner, side, side), ('row',...]
    ppermute x14 -> x12, starting transfers between devices: 41.6 us -> 38.4 us  [move(): return lax.ppermute(value, ('row', 'col'), pairs)]
    unnamed x20 -> x24, local copies, waits for them, and re-layouts: 0.21 us -> 3.22 us
  transfers between devices with their start and end apart: 14 -> 12, of which waited for: 3 -> 2; matrix products, arithmetic and copies ran while one was open for 1% -> 1% of each run, Pallas kernels for 7% -> 8%
where the time goes in v3:
time: 223 us; the launch traced here: 222 us
  blocking collectives  120 us (54%)
  starting transfers between devices  38.4 us (17%)
  Pallas kernels  33.9 us (15%)
  waiting for transfers between devices  24.3 us (11%)
  local copies, waits for them, and re-layouts  3.98 us (2%)
    all_to_all x1, blocking collectives, on_device(): lax.all_to_all(outgoing.reshape(devices, per_owner, side, side), ('row',...  120 us
    ppermute x12, starting transfers between devices, move(): return lax.ppermute(value, ('row', 'col'), pairs)  38.4 us
    ppermute x12, waiting for transfers between devices, move(): return lax.ppermute(value, ('row', 'col'), pairs)  24.3 us
    pallas_call x1, Pallas kernels, first_stop(): pl.pallas_call(first_stop_kernel, grid_spec=pltpu.PrefetchScalarGridSpec(...  16.9 us
    pallas_call x1, Pallas kernels, last_stop(): pl.pallas_call(last_stop_kernel, grid_spec=pltpu.PrefetchScalarGridSpec(n...  13.7 us
  transfers between devices with their start and end apart: 12, of which 2 were waited for; matrix products, arithmetic and copies ran while one was open for 1% of the time, Pallas kernels for 8%

profile of v3, /device:TPU:1, one launch (start us, length us, event | category | flops | bytes accessed | tf_op | source)
XLA Modules:
  0.0 222.4 jit_solution(14021295049380162363)
XLA Ops:
  0.0 3.3 %collective-permute-start.5 = (bf16[160,128,128]{2,1,0:T(8,128)(2,1)}, bf16[160,128,128]{2,1,0:T(8,128)(2,1)}, u32[]{:S(2)}, u32[]{:S(2)}) collective-permute-start(bf16[160,128,128]{2,1,0:T(8,128)(2,1)} %bitcast.12), channel_id=1, source_target_pairs={{1,0},{2,1},{3,2},{4,3},{5,4},{6,5},{7,6},{9,8},{10,9},{11,10},{12... | collective-permute-start | bytes 15728648 | tf_op jit(solution)/shard_map/ppermute | solution.py:23
  3.5 2.1 collective-permute-start
  5.5 2.0 collective-permute-start.1
  7.5 2.1 collective-permute-start.4
  9.7 0.7 collective-permute-start.2
  10.6 0.1 reshape_squeeze.14
  10.7 0.6 pad_add_fusion.second_meta
  11.4 0.7 pad_add_fusion.1.first_meta
  12.0 0.6 reshape_squeeze.15.kept_columns
  12.6 16.9 %shard_map.83 = (f32[10,12,128,128]{3,2,1,0:T(8,128)}, bf16[256,128,128]{2,1,0:T(8,128)(2,1)}) custom-call(s32[90]{0:T(128)} %pad_add_fusion.1.first_meta, s32[180]{0:T(256)} %pad_add_fusion.second_meta, s32[120]{0:T(128)} %reshape_squeeze.15.kept_columns, bf16[10,8,128,128]{3,2,1,0:T(8,128)(2,1)} %bitcast.17, bf16[160,128,128]{2,1,0:T(8,128)(2,1)} %bitcast.14), custom_call_target="tpu_custom_call" | custom-call | flops 8053063680 | bytes 31457280 | tf_op jit(solution)/shard_map/pallas_call | solution.py:177
  29.6 0.8 collective-permute-start.3
  30.4 5.5 %collective-permute-start.9 = (bf16[10,8,128,128]{3,2,1,0:T(8,128)(2,1)}, bf16[10,8,128,128]{3,2,1,0:T(8,128)(2,1)S(1)}, u32[]{:S(2)}, u32[]{:S(2)}) collective-permute-start(bf16[10,8,128,128]{3,2,1,0:T(8,128)(2,1)} %bitcast.18), channel_id=1, source_target_pairs={{0,112},{1,113},{8,120},{9,121},{16,0},{17,1},{24,8},{25,9},{32,16... | collective-permute-start | bytes 7864328 | tf_op jit(solution)/shard_map/ppermute | solution.py:23
  35.9 2.0 collective-permute-start.10
  37.9 1.4 copy-done
  39.3 23.6 %collective-permute-done.5.second = bf16[160,128,128]{2,1,0:T(8,128)(2,1)} collective-permute-done((bf16[160,128,128]{2,1,0:T(8,128)(2,1)}, bf16[160,128,128]{2,1,0:T(8,128)(2,1)}, u32[]{:S(2)}, u32[]{:S(2)}) %collective-permute-start.5) | collective-permute-done | bytes 5242912 | tf_op jit(solution)/shard_map/ppermute | solution.py:23
  62.9 1.6 collective-permute-start.7
  64.4 0.7 collective-permute-start.11
  65.1 3.6 %collective-permute-start.6 = (s32[90]{0:T(128)S(1)}, s32[90]{0:T(128)S(1)}, u32[]{:S(2)}, u32[]{:S(2)}) collective-permute-start(s32[90]{0:T(128)S(1)} %copy-done.10), channel_id=1, source_target_pairs={{0,112},{1,113},{2,114},{3,115},{4,116},{5,117},{6,118},{7,119},{8... | collective-permute-start | bytes 1088 | tf_op jit(solution)/shard_map/ppermute | solution.py:23
  68.7 14.1 %collective-permute-start.8 = (s32[180]{0:T(256)S(1)}, s32[180]{0:T(256)S(1)}, u32[]{:S(2)}, u32[]{:S(2)}) collective-permute-start(s32[180]{0:T(256)S(1)} %copy-done.7), channel_id=1, source_target_pairs={{0,15},{1,0},{2,1},{3,2},{4,3},{5,4},{6,5},{7,6},{8,7},{9,8},{10,9... | collective-permute-start | bytes 2168 | tf_op jit(solution)/shard_map/ppermute | solution.py:23
  82.8 0.7 collective-permute-done.8.second_meta
  83.6 1.6 copy-done.1
  85.2 13.7 %shard_map.84 = bf16[256,128,128]{2,1,0:T(8,128)(2,1)} custom-call(s32[90]{0:T(128)S(1)} %collective-permute-done.6.first_meta, s32[180]{0:T(256)S(1)} %collective-permute-done.8.second_meta, s32[120]{0:T(128)S(1)} %copy-done.2, s32[120]{0:T(128)S(1)} %bitcast.10, s32[2]{0:T(128)S(1)} %add_convert_fusion.place, ...), custom_call_target="tpu_custom_call", output_to_operand_aliasing={{}: (12, {})} | custom-call | flops 1024 | bytes 1024 | tf_op jit(solution)/shard_map/pallas_call | solution.py:218
  98.9 120.2 %all_to_all.5.source = bf16[128,2,128,128]{3,2,1,0:T(8,128)(2,1)S(1)} all-to-all(bf16[128,2,128,128]{3,2,1,0:T(8,128)(2,1)} %bitcast.11), channel_id=1, replica_groups=mesh['row'=8,'col'=16] {'row','col'}, dimensions={0} | all-to-all | bytes 16777216 | tf_op jit(solution)/shard_map/all_to_all | solution.py:372
  219.1 3.3 %shard_map.85 = bf16[128,2,128,128]{3,2,1,0:T(8,128)(2,1)} custom-call(bf16[128,2,128,128]{3,2,1,0:T(8,128)(2,1)S(1)} %all_to_all.5.source), custom_call_target="tpu_custom_call" | custom-call | tf_op jit(solution)/shard_map/pallas_call | solution.py:301
  (36 shorter events, 0.5 us)
Async XLA Ops:
  0.0 62.8 %collective-permute-start.5 = (bf16[160,128,128]{2,1,0:T(8,128)(2,1)}, bf16[160,128,128]{2,1,0:T(8,128)(2,1)}, u32[]{:S(2)}, u32[]{:S(2)}) collective-permute-start(bf16[160,128,128]{2,1,0:T(8,128)(2,1)} %bitcast.12), channel_id=1, source_target_pairs={{1,0},{2,1},{3,2},{4,3},{5,4},{6,5},{7,6},{9,8},{10,9},{11,10},{12... | collective-permute-start | bytes 15728648 | tf_op jit(solution)/shard_map/ppermute | solution.py:23
  3.3 7.0 %copy-start.5 = (s32[1,10,8]{1,2,0:T(8,128)S(1)}, s32[1,10,8]{1,2,0:T(8,128)}, u32[]{:S(2)}) copy-start(s32[1,10,8]{1,2,0:T(8,128)} %param.9) | copy-start | bytes 964
  3.4 7.2 %copy-start.6 = (s32[1,20,8]{1,2,0:T(8,128)S(1)}, s32[1,20,8]{1,2,0:T(8,128)}, u32[]{:S(2)}) copy-start(s32[1,20,8]{1,2,0:T(8,128)} %param.12) | copy-start | bytes 1924
  3.4 7.4 %copy-start.8 = (s32[1,20]{1,0:T(1,128)S(1)}, s32[1,20]{1,0:T(1,128)}, u32[]{:S(2)}) copy-start(s32[1,20]{1,0:T(1,128)} %param.13) | copy-start | bytes 244
  3.4 8.0 %copy-start.9 = (s32[1,10]{1,0:T(1,128)S(1)}, s32[1,10]{1,0:T(1,128)}, u32[]{:S(2)}) copy-start(s32[1,10]{1,0:T(1,128)} %param.10) | copy-start | bytes 124
  3.4 8.6 %copy-start.4 = (s32[1,10,12]{2,0,1:T(1,128)S(1)}, s32[1,10,12]{2,0,1:T(1,128)}, u32[]{:S(2)}) copy-start(s32[1,10,12]{2,0,1:T(1,128)} %param.14) | copy-start | bytes 1444
  3.5 26.1 %collective-permute-start = (bf16[68,128,128]{2,1,0:T(8,128)(2,1)}, bf16[68,128,128]{2,1,0:T(8,128)(2,1)}, u32[]{:S(2)}, u32[]{:S(2)}) collective-permute-start(bf16[68,128,128]{2,1,0:T(8,128)(2,1)} %get-tuple-element.23), channel_id=1, source_target_pairs={{0,16},{8,24},{16,0},{24,8},{32,48},{40,56},{48,32},{56,40},{64,80... | collective-permute-start | bytes 6684680 | tf_op jit(solution)/shard_map/ppermute | solution.py:23
  5.5 24.0 %collective-permute-start.1 = (bf16[68,128,128]{2,1,0:T(8,128)(2,1)}, bf16[68,128,128]{2,1,0:T(8,128)(2,1)}, u32[]{:S(2)}, u32[]{:S(2)}) collective-permute-start(bf16[68,128,128]{2,1,0:T(8,128)(2,1)} %get-tuple-element.24), channel_id=1, source_target_pairs={{0,31},{8,23},{16,15},{24,7},{32,63},{40,55},{48,47},{56,39},{64,9... | collective-permute-start | bytes 6684680 | tf_op jit(solution)/shard_map/ppermute | solution.py:23
  7.5 30.3 %collective-permute-start.4 = (bf16[10,8,128,128]{3,2,1,0:T(8,128)(2,1)}, bf16[10,8,128,128]{3,2,1,0:T(8,128)(2,1)}, u32[]{:S(2)}, u32[]{:S(2)}) collective-permute-start(bf16[10,8,128,128]{3,2,1,0:T(8,128)(2,1)} %bitcast.16), channel_id=1, source_target_pairs={{2,114},{3,115},{4,116},{5,117},{6,118},{7,119},{10,122},{11,123},... | collective-permute-start | bytes 7864328 | tf_op jit(solution)/shard_map/ppermute | solution.py:23
  9.7 19.9 %collective-permute-start.2 = (bf16[24,128,128]{2,1,0:T(8,128)(2,1)}, bf16[24,128,128]{2,1,0:T(8,128)(2,1)S(1)}, u32[]{:S(2)}, u32[]{:S(2)}) collective-permute-start(bf16[24,128,128]{2,1,0:T(8,128)(2,1)} %get-tuple-element.25), channel_id=1, source_target_pairs={{0,29},{8,21},{16,13},{24,5},{32,61},{40,53},{48,45},{56,37},{64,9... | collective-permute-start | bytes 2359304 | tf_op jit(solution)/shard_map/ppermute | solution.py:23
  12.6 52.5 %copy-start.10 = (s32[90]{0:T(128)S(1)}, s32[90]{0:T(128)}, u32[]{:S(2)}) copy-start(s32[90]{0:T(128)} %pad_add_fusion.1.first_meta) | copy-start | bytes 1084
  12.6 56.1 %copy-start.7 = (s32[180]{0:T(256)S(1)}, s32[180]{0:T(256)}, u32[]{:S(2)}) copy-start(s32[180]{0:T(256)} %pad_add_fusion.second_meta) | copy-start | bytes 2164
  12.6 71.0 %copy-start.2 = (s32[120]{0:T(128)S(1)}, s32[120]{0:T(128)}, u32[]{:S(2)}) copy-start(s32[120]{0:T(128)} %reshape_squeeze.15.kept_columns) | copy-start | bytes 1444
  12.6 71.0 %copy-start.3 = (s32[1,120,1]{1,2,0:T(1,128)S(1)}, s32[1,120,1]{1,2,0:T(1,128)}, u32[]{:S(2)}) copy-start(s32[1,120,1]{1,2,0:T(1,128)} %param.15) | copy-start | bytes 1444
  29.6 8.3 %collective-permute-start.3 = (bf16[68,128,128]{2,1,0:T(8,128)(2,1)}, bf16[68,128,128]{2,1,0:T(8,128)(2,1)S(1)}, u32[]{:S(2)}, u32[]{:S(2)}) collective-permute-start(bf16[68,128,128]{2,1,0:T(8,128)(2,1)} %collective-permute-done), channel_id=1, source_target_pairs={{0,31},{8,23},{16,15},{24,7},{32,63},{40,55},{48,47},{56,39},{64,9... | collective-permute-start | bytes 6684680 | tf_op jit(solution)/shard_map/ppermute | solution.py:23
  30.4 52.5 %collective-permute-start.9 = (bf16[10,8,128,128]{3,2,1,0:T(8,128)(2,1)}, bf16[10,8,128,128]{3,2,1,0:T(8,128)(2,1)S(1)}, u32[]{:S(2)}, u32[]{:S(2)}) collective-permute-start(bf16[10,8,128,128]{3,2,1,0:T(8,128)(2,1)} %bitcast.18), channel_id=1, source_target_pairs={{0,112},{1,113},{8,120},{9,121},{16,0},{17,1},{24,8},{25,9},{32,16... | collective-permute-start | bytes 7864328 | tf_op jit(solution)/shard_map/ppermute | solution.py:23
  35.9 47.0 %collective-permute-start.10 = (bf16[68,128,128]{2,1,0:T(8,128)(2,1)}, bf16[68,128,128]{2,1,0:T(8,128)(2,1)}, u32[]{:S(2)}, u32[]{:S(2)}) collective-permute-start(bf16[68,128,128]{2,1,0:T(8,128)(2,1)} %collective-permute-done.1), channel_id=1, source_target_pairs={{7,23},{15,31},{23,7},{31,15},{39,55},{47,63},{55,39},{63,47},{71,... | collective-permute-start | bytes 6684680 | tf_op jit(solution)/shard_map/ppermute | solution.py:23
  37.9 1.4 copy-start
  62.9 1.6 collective-permute-start.7
  64.4 19.2 %collective-permute-start.11 = (bf16[24,128,128]{2,1,0:T(8,128)(2,1)}, bf16[24,128,128]{2,1,0:T(8,128)(2,1)S(1)}, u32[]{:S(2)}, u32[]{:S(2)}) collective-permute-start(bf16[24,128,128]{2,1,0:T(8,128)(2,1)} %collective-permute-done.7), channel_id=1, source_target_pairs={{5,7},{13,15},{21,23},{29,31},{37,39},{45,47},{53,55},{61,63},{69,... | collective-permute-start | bytes 2359304 | tf_op jit(solution)/shard_map/ppermute | solution.py:23
  65.1 17.7 %collective-permute-start.6 = (s32[90]{0:T(128)S(1)}, s32[90]{0:T(128)S(1)}, u32[]{:S(2)}, u32[]{:S(2)}) collective-permute-start(s32[90]{0:T(128)S(1)} %copy-done.10), channel_id=1, source_target_pairs={{0,112},{1,113},{2,114},{3,115},{4,116},{5,117},{6,118},{7,119},{8... | collective-permute-start | bytes 1088 | tf_op jit(solution)/shard_map/ppermute | solution.py:23
  68.7 14.9 %collective-permute-start.8 = (s32[180]{0:T(256)S(1)}, s32[180]{0:T(256)S(1)}, u32[]{:S(2)}, u32[]{:S(2)}) collective-permute-start(s32[180]{0:T(256)S(1)} %copy-done.7), channel_id=1, source_target_pairs={{0,15},{1,0},{2,1},{3,2},{4,3},{5,4},{6,5},{7,6},{8,7},{9,8},{10,9... | collective-permute-start | bytes 2168 | tf_op jit(solution)/shard_map/ppermute | solution.py:23
  83.6 1.6 copy-start.1

commit v4 on v3

--- a/solution.py
+++ b/solution.py
@@ -10,6 +10,10 @@
 VMEM_LIMIT = 40 * 1024 * 1024
 LARGE_VMEM_LIMIT = 62 * 1024 * 1024
 TABLE_ROWS = 20
+SHORT = 4
+STRIDE = 13
+SHIFT = 8
+PIECE = 8
 
 
 def move(value, chosen):
@@ -43,59 +47,101 @@
             table[k * width + meta[block]] = jnp.where(b < count, block, blank)
 
 
-def load_second(second, held, sem):
-    total = second.shape[0]
-    copy = pltpu.make_async_copy(second, held.at[pl.ds(0, total)], sem)
-    copy.start()
-    held[total] = jnp.zeros(held.shape[1:], held.dtype)
-    return copy
-
-
-def row_starts(meta, i, slots, width):
+def list_matches(matches, crowded, table, meta, kept_columns, slots, width):
     row_total = meta.shape[0] // (slots + 1)
-    count = meta[row_total * slots + i]
-    return [
-        jnp.where(a < count, meta[i * slots + a] * width, TABLE_ROWS * width) for a in range(slots)
-    ]
-
-
-def pair_product(starts, table, columns, first, held):
-    slots = first.shape[1]
-    row = jnp.concatenate([first[0, a] for a in range(slots)], axis=1)
-    picked = [
-        jnp.concatenate([held[table[start + column]] for start in starts], axis=0)
-        for column in columns
-    ]
-    return jnp.dot(row, jnp.concatenate(picked, axis=1), preferred_element_type=jnp.float32)
+    kept = kept_columns.shape[0] // row_total
+    blank = TABLE_ROWS * slots
+
+    def one_row(i, carry):
+        count = meta[row_total * slots + i]
+        starts = [
+            jnp.where(a < count, meta[i * slots + a] * width, TABLE_ROWS * width)
+            for a in range(slots)
+        ]
+        firsts = [(i * slots + a) << SHIFT for a in range(slots)]
+        most = jnp.int32(0)
+        for f in range(kept):
+            l = i * kept + f
+            column = kept_columns[l]
+            found = jnp.int32(0)
+            for start, first in zip(starts, firsts):
+                block = table[start + column]
+                matches[l * STRIDE + found] = first + block
+                found += (block != blank).astype(jnp.int32)
+            for n in range(slots - SHORT):
+                matches[l * STRIDE + found + n] = blank
+            matches[l * STRIDE + STRIDE - 1] = found
+            most = jnp.maximum(most, found)
+        crowded[i] = (most > SHORT).astype(jnp.int32)
+        return carry
+
+    lax.fori_loop(0, row_total, one_row, 0)
+
+
+def load_pieces(source, target, sem):
+    total = source.shape[0]
+    for at in range(0, total, PIECE):
+        piece = pl.ds(at, min(PIECE, total - at))
+        pltpu.make_async_copy(source.at[piece], target.at[piece], sem).start()
+
+
+def matched_product(matches, l, terms, rows, held):
+    codes = [matches[l * STRIDE + n] for n in range(terms)]
+    left = jnp.concatenate([rows[code >> SHIFT] for code in codes], axis=1)
+    right = jnp.concatenate([held[code & ((1 << SHIFT) - 1)] for code in codes], axis=0)
+    return jnp.dot(left, right, preferred_element_type=jnp.float32)
+
+
+def row_products(matches, crowded, i, slots, rows, held, kept, put):
+    for f in range(kept):
+        l = i * kept + f
+        put(l, f, matched_product(matches, l, SHORT, rows, held))
+
+    @pl.when(crowded[i] != 0)
+    def _():
+        def again(f, carry):
+            l = i * kept + f
+
+            @pl.when(matches[l * STRIDE + STRIDE - 1] > SHORT)
+            def _():
+                put(l, f, matched_product(matches, l, slots, rows, held))
+
+            return carry
+
+        lax.fori_loop(0, kept, again, 0)
 
 
 def first_stop_kernel(
     first_meta, second_meta, kept_columns, first, second,
-    total, blank, table, held, zeros, held_sem, blank_sem,
+    total, blank, table, matches, crowded, held, rows, zeros, held_sem, row_sem, blank_sem,
 ):
     i = pl.program_id(0)
-    kept, side = total.shape[1], total.shape[2]
-    slots = first.shape[1]
+    kept = total.shape[1]
+    row_total = pl.num_programs(0)
+    slots = rows.shape[0] // (kept_columns.shape[0] // kept)
     width = table.shape[0] // (TABLE_ROWS + 1)
     part = zeros.shape[0]
+    panel = held.at[pl.ds(0, second.shape[0])]
 
     @pl.when(i == 0)
     def _():
-        copy = load_second(second, held, held_sem)
+        load_pieces(second, panel, held_sem)
+        load_pieces(first, rows, row_sem)
+        held[second.shape[0]] = jnp.zeros(held.shape[1:], held.dtype)
         zeros[...] = jnp.zeros(zeros.shape, zeros.dtype)
+        fill_table(table, second_meta, slots, width)
+        list_matches(matches, crowded, table, first_meta, kept_columns, slots, width)
+        pltpu.make_async_copy(rows, rows, row_sem).wait()
+        pltpu.make_async_copy(panel, panel, held_sem).wait()
         for j in range(blank.shape[0] // part):
             pltpu.make_async_copy(zeros, blank.at[pl.ds(j * part, part)], blank_sem).start()
-        fill_table(table, second_meta, slots, width)
-        copy.wait()
-
-    starts = row_starts(first_meta, i, slots, width)
-    for f in range(0, kept, 2):
-        columns = [kept_columns[i * kept + f + g] for g in range(2)]
-        both = pair_product(starts, table, columns, first, held)
-        total[0, f] = both[:, :side]
-        total[0, f + 1] = both[:, side:]
-
-    @pl.when(i == pl.num_programs(0) - 1)
+
+    def put(l, f, value):
+        total[0, f] = value
+
+    row_products(matches, crowded, i, slots, rows, held, kept, put)
+
+    @pl.when(i == row_total - 1)
     def _():
         pltpu.make_async_copy(blank, blank, blank_sem).wait()
 
@@ -103,41 +149,37 @@
 def last_stop_kernel(
     first_meta, second_meta, kept_columns, owner, place,
     early, late, before, second, part_a, part_b, part_c, blank,
-    out, table, used, held, rows, product, held_sem, row_sem, out_sem,
+    out, table, matches, crowded, used, held, rows, product, held_sem, row_sem, out_sem,
 ):
     del blank
     i = pl.program_id(0)
-    kept, side = before.shape[1], before.shape[2]
+    kept = before.shape[1]
+    slots = rows.shape[0] // (kept_columns.shape[0] // kept)
     width = table.shape[0] // (TABLE_ROWS + 1)
     per_owner = out.shape[0] // used.shape[0]
-    row_total, slots = rows.shape[0], rows.shape[1]
     total = held.shape[0] - 1
+    panel = held.at[pl.ds(0, total)]
 
     @pl.when(i == 0)
     def _():
-        whole = held.at[pl.ds(0, total)]
-
         @pl.when(place[0] == 0)
         def _():
-            pltpu.make_async_copy(second, whole, held_sem).start()
+            load_pieces(second, panel, held_sem)
 
         @pl.when(place[0] != 0)
         def _():
             at = 0
             for part in (part_a, part_b, part_c):
-                span = pl.ds(at, part.shape[0])
-                pltpu.make_async_copy(part, held.at[span], held_sem).start()
+                load_pieces(part, held.at[pl.ds(at, part.shape[0])], held_sem)
                 at += part.shape[0]
 
         @pl.when(place[1] == 0)
         def _():
-            for j in range(row_total):
-                pltpu.make_async_copy(early.at[j], rows.at[j], row_sem.at[j]).start()
+            load_pieces(early, rows, row_sem)
 
         @pl.when(place[1] != 0)
         def _():
-            for j in range(row_total):
-                pltpu.make_async_copy(late.at[j], rows.at[j], row_sem.at[j]).start()
+            load_pieces(late, rows, row_sem)
 
         held[total] = jnp.zeros(held.shape[1:], held.dtype)
 
@@ -147,30 +189,37 @@
 
         lax.fori_loop(0, used.shape[0], clear, 0, unroll=16)
         fill_table(table, second_meta, slots, width)
-        pltpu.make_async_copy(whole, whole, held_sem).wait()
-
-    pltpu.make_async_copy(rows.at[i], rows.at[i], row_sem.at[i]).wait()
-    first = rows.at[pl.ds(i, 1)]
-    starts = row_starts(first_meta, i, slots, width)
-    for f in range(0, kept, 2):
-        columns = [kept_columns[i * kept + f + g] for g in range(2)]
-        both = pair_product(starts, table, columns, first, held)
-        for g in range(2):
-            l = i * kept + f + g
-            value = both[:, g * side:(g + 1) * side] + before[0, f + g]
-            product[l] = value.astype(product.dtype)
-            rank = used[owner[l]]
-            used[owner[l]] = rank + 1
-            slot = owner[l] * per_owner + rank
-            pltpu.make_async_copy(product.at[l], out.at[slot], out_sem).start()
+        list_matches(matches, crowded, table, first_meta, kept_columns, slots, width)
+        pltpu.make_async_copy(rows, rows, row_sem).wait()
+        pltpu.make_async_copy(panel, panel, held_sem).wait()
+
+    def put(l, f, value):
+        product[l] = (value + before[0, f]).astype(product.dtype)
+
+    row_products(matches, crowded, i, slots, rows, held, kept, put)
+    for f in range(kept):
+        l = i * kept + f
+        rank = used[owner[l]]
+        used[owner[l]] = rank + 1
+        slot = owner[l] * per_owner + rank
+        pltpu.make_async_copy(product.at[l], out.at[slot], out_sem).start()
 
     @pl.when(i == pl.num_programs(0) - 1)
     def _():
         pltpu.make_async_copy(product, out.at[pl.ds(0, product.shape[0])], out_sem).wait()
 
 
+def list_scratch(kept_total, row_total):
+    return [
+        pltpu.SMEM(((TABLE_ROWS + 1) * TABLE_ROWS,), jnp.int32),
+        pltpu.SMEM((kept_total * STRIDE,), jnp.int32),
+        pltpu.SMEM((row_total,), jnp.int32),
+    ]
+
+
 def first_stop(first_meta, second_meta, kept_columns, first, second, outgoing):
-    rows, slots, side, _ = first.shape
+    first_total, side, _ = first.shape
+    rows = first_meta.shape[0] - first_total
     kept = kept_columns.shape[0] // rows
     second_total = second.shape[0]
     part = 16
@@ -179,18 +228,16 @@
         grid_spec=pltpu.PrefetchScalarGridSpec(
             num_scalar_prefetch=3,
             grid=(rows,),
-            in_specs=[
-                pl.BlockSpec((1, slots, side, side), lambda i, *_: (i, 0, 0, 0)),
-                pl.BlockSpec(memory_space=pl.ANY),
-            ],
+            in_specs=[pl.BlockSpec(memory_space=pl.ANY)] * 2,
             out_specs=[
                 pl.BlockSpec((1, kept, side, side), lambda i, *_: (i, 0, 0, 0)),
                 pl.BlockSpec(memory_space=pl.ANY),
             ],
-            scratch_shapes=[
-                pltpu.SMEM(((TABLE_ROWS + 1) * TABLE_ROWS,), jnp.int32),
+            scratch_shapes=list_scratch(rows * kept, rows) + [
                 pltpu.VMEM((second_total + 1, side, side), second.dtype),
+                pltpu.VMEM(first.shape, first.dtype),
                 pltpu.VMEM((part, side, side), second.dtype),
+                pltpu.SemaphoreType.DMA,
                 pltpu.SemaphoreType.DMA,
                 pltpu.SemaphoreType.DMA,
             ],
@@ -201,8 +248,8 @@
         ],
         compiler_params=pltpu.CompilerParams(vmem_limit_bytes=LARGE_VMEM_LIMIT),
         cost_estimate=pl.CostEstimate(
-            flops=4 * rows * slots * kept * side**3,
-            bytes_accessed=2 * (rows * (slots * 2 + kept * 4) + 2 * second_total) * side**2,
+            flops=4 * first_total * kept * side**3,
+            bytes_accessed=2 * (first_total * 2 + rows * kept * 4 + 2 * second_total) * side**2,
             transcendentals=0,
         ),
     )(first_meta, second_meta, kept_columns, first, second)
@@ -212,8 +259,8 @@
     first_meta, second_meta, kept_columns, owner, place,
     early, late, before, second, part_a, part_b, part_c, blank, owners,
 ):
-    rows, slots, side, _ = early.shape
-    kept = before.shape[1]
+    side = early.shape[1]
+    rows, kept = before.shape[:2]
     second_total = second.shape[0]
     return pl.pallas_call(
         last_stop_kernel,
@@ -231,20 +278,19 @@
                 pl.BlockSpec(memory_space=pl.ANY),
             ],
             out_specs=pl.BlockSpec(memory_space=pl.ANY),
-            scratch_shapes=[
-                pltpu.SMEM(((TABLE_ROWS + 1) * TABLE_ROWS,), jnp.int32),
+            scratch_shapes=list_scratch(rows * kept, rows) + [
                 pltpu.SMEM((owners,), jnp.int32),
                 pltpu.VMEM((second_total + 1, side, side), second.dtype),
                 pltpu.VMEM(early.shape, early.dtype),
                 pltpu.VMEM((rows * kept, side, side), second.dtype),
                 pltpu.SemaphoreType.DMA,
-                pltpu.SemaphoreType.DMA((rows,)),
+                pltpu.SemaphoreType.DMA,
                 pltpu.SemaphoreType.DMA,
             ],
         ),
         out_shape=jax.ShapeDtypeStruct(blank.shape, blank.dtype),
         input_output_aliases={12: 0},
-        compiler_params=pltpu.CompilerParams(vmem_limit_bytes=VMEM_LIMIT),
+        compiler_params=pltpu.CompilerParams(vmem_limit_bytes=LARGE_VMEM_LIMIT),
         cost_estimate=pl.CostEstimate(flops=1024, bytes_accessed=1024, transcendentals=0),
     )(
         first_meta, second_meta, kept_columns, owner, place,
@@ -314,7 +360,7 @@
     rows, kept = c_cols.shape[1], c_cols.shape[2]
     side = a_blocks.shape[3]
     per_owner = max(2, 3 * rows * kept // (2 * devices))
-    first = a_blocks[0]
+    first = a_blocks[0].reshape(-1, side, side)
     second = b_blocks[0].reshape(-1, side, side)
     total = second.shape[0]
     large = total * 17 // 40
@@ -335,7 +381,7 @@
     part_a, part_b, part_c = cut(crossing, second, (large, large, total - 2 * large))
     part_a = move(part_a, at(0, near))
     part_b = move(part_b, at(0, lambda r, c: far(r, c + last)))
-    part_c = move(part_c, at(0, lambda r, c: far(r, c + middle)))
+    part_c = move(part_c, at(0, lambda r, c: (r, c + middle)))
     early = move(first, lambda r, c: (r - 1, c) if c % span > 1 else None)
     second_next = move(second, lambda r, c: (r, c - 1) if c % span else None)
 
@@ -352,6 +398,8 @@
     )
     late = move(first, lambda r, c: (r - 1, c) if c % span < 2 else None)
     part_a = move(part_a, at(0, lambda r, c: far(r, c + last)))
+    part_c = move(part_c, at(middle, far))
+    part_b, part_c = lax.optimization_barrier((part_b, part_c))
     part_b = move(part_b, at(last, near))
 
     part_a, part_c, early, second_next, first_meta = lax.optimization_barrier(

time: 223 us -> 225 us (level)
  starting transfers between devices: 38.4 us -> 34.6 us
  blocking collectives: 120 us -> 123 us
  waiting for transfers between devices: 24.3 us -> 26.6 us
    ppermute x12 -> x13, starting transfers between devices: 38.4 us -> 34.6 us  [move(): return lax.ppermute(value, ('row', 'col'), pairs)]
    pallas_call x1, Pallas kernels: 13.7 us -> 17.2 us  [last_stop(): pl.pallas_call(last_stop_kernel, grid_spec=pltpu.PrefetchScalarGridSpec(n...]
    all_to_all x1, blocking collectives: 120 us -> 123 us  [on_device(): lax.all_to_all(outgoing.reshape(devices, per_owner, side, side), ('row',...]
    ppermute x12 -> x13, waiting for transfers between devices: 24.3 us -> 26.6 us  [move(): return lax.ppermute(value, ('row', 'col'), pairs)]
  transfers between devices with their start and end apart: 12 -> 13, of which waited for: 2 -> 2; matrix products, arithmetic and copies ran while one was open for 1% -> 1% of each run, Pallas kernels for 8% -> 7%
where the time goes in v4:
time: 225 us; the launch traced here: 224 us
  blocking collectives  123 us (55%)
  Pallas kernels  35.9 us (16%)
  starting transfers between devices  34.6 us (15%)
  waiting for transfers between devices  26.6 us (12%)
    all_to_all x1, blocking collectives, on_device(): lax.all_to_all(outgoing.reshape(devices, per_owner, side, side), ('row',...  123 us
    ppermute x13, starting transfers between devices, move(): return lax.ppermute(value, ('row', 'col'), pairs)  34.6 us
    ppermute x13, waiting for transfers between devices, move(): return lax.ppermute(value, ('row', 'col'), pairs)  26.6 us
    pallas_call x1, Pallas kernels, last_stop(): pl.pallas_call(last_stop_kernel, grid_spec=pltpu.PrefetchScalarGridSpec(n...  17.2 us
    pallas_call x1, Pallas kernels, first_stop(): pl.pallas_call(first_stop_kernel, grid_spec=pltpu.PrefetchScalarGridSpec(...  15.3 us
  transfers between devices with their start and end apart: 13, of which 2 were waited for; matrix products, arithmetic and copies ran while one was open for 1% of the time, Pallas kernels for 7%

profile of v4, /device:TPU:1, one launch (start us, length us, event | category | flops | bytes accessed | tf_op | source)
XLA Modules:
  0.0 224.3 jit_solution(15283370506436138349)
XLA Ops:
  0.0 3.3 %collective-permute-start.6 = (bf16[160,128,128]{2,1,0:T(8,128)(2,1)}, bf16[160,128,128]{2,1,0:T(8,128)(2,1)}, u32[]{:S(2)}, u32[]{:S(2)}) collective-permute-start(bf16[160,128,128]{2,1,0:T(8,128)(2,1)} %bitcast.11), channel_id=1, source_target_pairs={{1,0},{2,1},{3,2},{4,3},{5,4},{6,5},{7,6},{9,8},{10,9},{11,10},{12... | collective-permute-start | bytes 15728648 | tf_op jit(solution)/shard_map/ppermute | solution.py:27
  3.5 2.1 collective-permute-start
  5.6 2.0 collective-permute-start.1
  7.6 2.1 collective-permute-start.5
  9.7 0.7 collective-permute-start.2
  10.8 0.7 pad_add_fusion.second_meta
  11.4 0.6 pad_add_fusion.1.first_meta
  12.0 0.6 reshape_squeeze.19.kept_columns
  12.6 15.3 %shard_map.83 = (f32[10,12,128,128]{3,2,1,0:T(8,128)}, bf16[256,128,128]{2,1,0:T(8,128)(2,1)}) custom-call(s32[90]{0:T(128)} %pad_add_fusion.1.first_meta, s32[180]{0:T(256)} %pad_add_fusion.second_meta, s32[120]{0:T(128)} %reshape_squeeze.19.kept_columns, bf16[80,128,128]{2,1,0:T(8,128)(2,1)} %bitcast.17, bf16[160,128,128]{2,1,0:T(8,128)(2,1)} %bitcast.13), custom_call_target="tpu_custom_call" | custom-call | flops 8053063680 | bytes 31457280 | tf_op jit(solution)/shard_map/pallas_call | solution.py:226
  28.0 2.0 collective-permute-start.3
  30.0 0.7 collective-permute-start.4
  30.7 5.9 %collective-permute-start.10 = (bf16[80,128,128]{2,1,0:T(8,128)(2,1)}, bf16[80,128,128]{2,1,0:T(8,128)(2,1)}, u32[]{:S(2)}, u32[]{:S(2)}) collective-permute-start(bf16[80,128,128]{2,1,0:T(8,128)(2,1)} %bitcast.18), channel_id=1, source_target_pairs={{0,112},{1,113},{8,120},{9,121},{16,0},{17,1},{24,8},{25,9},{32,16... | collective-permute-start | bytes 7864328 | tf_op jit(solution)/shard_map/ppermute | solution.py:27
  36.6 2.1 collective-permute-start.11
  38.7 24.3 %collective-permute-done.6.second = bf16[160,128,128]{2,1,0:T(8,128)(2,1)} collective-permute-done((bf16[160,128,128]{2,1,0:T(8,128)(2,1)}, bf16[160,128,128]{2,1,0:T(8,128)(2,1)}, u32[]{:S(2)}, u32[]{:S(2)}) %collective-permute-start.6) | collective-permute-done | bytes 5242912 | tf_op jit(solution)/shard_map/ppermute | solution.py:27
  63.0 0.7 collective-permute-start.8
  63.7 0.7 collective-permute-start.12
  64.4 3.6 %collective-permute-start.7 = (s32[90]{0:T(128)S(1)}, s32[90]{0:T(128)S(1)}, u32[]{:S(2)}, u32[]{:S(2)}) collective-permute-start(s32[90]{0:T(128)S(1)} %copy-done.9), channel_id=1, source_target_pairs={{0,112},{1,113},{2,114},{3,115},{4,116},{5,117},{6,118},{7,119},{8... | collective-permute-start | bytes 1088 | tf_op jit(solution)/shard_map/ppermute | solution.py:27
  68.0 8.8 %collective-permute-start.9 = (s32[180]{0:T(256)S(1)}, s32[180]{0:T(256)S(1)}, u32[]{:S(2)}, u32[]{:S(2)}) collective-permute-start(s32[180]{0:T(256)S(1)} %copy-done.5), channel_id=1, source_target_pairs={{0,15},{1,0},{2,1},{3,2},{4,3},{5,4},{6,5},{7,6},{8,7},{9,8},{10,9... | collective-permute-start | bytes 2168 | tf_op jit(solution)/shard_map/ppermute | solution.py:27
  76.8 0.6 add_convert_fusion.place
  77.4 2.3 %collective-permute-done.9.second_meta = s32[180]{0:T(256)S(1)} collective-permute-done((s32[180]{0:T(256)S(1)}, s32[180]{0:T(256)S(1)}, u32[]{:S(2)}, u32[]{:S(2)}) %collective-permute-start.9) | collective-permute-done | bytes 752 | tf_op jit(solution)/shard_map/ppermute | solution.py:27
  79.7 0.6 copy-done.4
  80.6 17.2 %shard_map.84 = bf16[256,128,128]{2,1,0:T(8,128)(2,1)} custom-call(s32[90]{0:T(128)} %copy-done.6, s32[180]{0:T(256)} %copy-done.4, s32[120]{0:T(128)} %reshape_squeeze.19.kept_columns, s32[120]{0:T(128)} %bitcast.14, s32[2]{0:T(128)} %add_convert_fusion.place, bf16[80,128,128]{2,1,0:T(8,128)(2,1)} %collective-permute-done.5.early, ...), custom_call_target="tpu_custom_call", output_to_operand_aliasing={{}: (12, {})} | custom-call | flops 1024 | bytes 1024 | tf_op jit(solution)/shard_map/pallas_call | solution.py:265
  97.8 123.2 %all_to_all.5.source = bf16[128,2,128,128]{3,2,1,0:T(8,128)(2,1)S(1)} all-to-all(bf16[128,2,128,128]{3,2,1,0:T(8,128)(2,1)} %bitcast.10), channel_id=1, replica_groups=mesh['row'=8,'col'=16] {'row','col'}, dimensions={0} | all-to-all | bytes 16777216 | tf_op jit(solution)/shard_map/all_to_all | solution.py:420
  221.0 3.3 %shard_map.85 = bf16[128,2,128,128]{3,2,1,0:T(8,128)(2,1)} custom-call(bf16[128,2,128,128]{3,2,1,0:T(8,128)(2,1)S(1)} %all_to_all.5.source), custom_call_target="tpu_custom_call" | custom-call | tf_op jit(solution)/shard_map/pallas_call | solution.py:347
  (36 shorter events, 0.8 us)
Async XLA Ops:
  0.0 63.0 %collective-permute-start.6 = (bf16[160,128,128]{2,1,0:T(8,128)(2,1)}, bf16[160,128,128]{2,1,0:T(8,128)(2,1)}, u32[]{:S(2)}, u32[]{:S(2)}) collective-permute-start(bf16[160,128,128]{2,1,0:T(8,128)(2,1)} %bitcast.11), channel_id=1, source_target_pairs={{1,0},{2,1},{3,2},{4,3},{5,4},{6,5},{7,6},{9,8},{10,9},{11,10},{12... | collective-permute-start | bytes 15728648 | tf_op jit(solution)/shard_map/ppermute | solution.py:27
  3.3 7.0 %copy-start.2 = (s32[1,10,8]{1,2,0:T(8,128)S(1)}, s32[1,10,8]{1,2,0:T(8,128)}, u32[]{:S(2)}) copy-start(s32[1,10,8]{1,2,0:T(8,128)} %param.9) | copy-start | bytes 964
  3.4 7.2 %copy-start.3 = (s32[1,20,8]{1,2,0:T(8,128)S(1)}, s32[1,20,8]{1,2,0:T(8,128)}, u32[]{:S(2)}) copy-start(s32[1,20,8]{1,2,0:T(8,128)} %param.12) | copy-start | bytes 1924
  3.4 7.4 %copy-start.7 = (s32[1,20]{1,0:T(1,128)S(1)}, s32[1,20]{1,0:T(1,128)}, u32[]{:S(2)}) copy-start(s32[1,20]{1,0:T(1,128)} %param.13) | copy-start | bytes 244
  3.4 8.0 %copy-start.8 = (s32[1,10]{1,0:T(1,128)S(1)}, s32[1,10]{1,0:T(1,128)}, u32[]{:S(2)}) copy-start(s32[1,10]{1,0:T(1,128)} %param.10) | copy-start | bytes 124
  3.4 8.6 %copy-start.1 = (s32[1,10,12]{2,0,1:T(1,128)S(1)}, s32[1,10,12]{2,0,1:T(1,128)}, u32[]{:S(2)}) copy-start(s32[1,10,12]{2,0,1:T(1,128)} %param.14) | copy-start | bytes 1444
  3.5 24.5 %collective-permute-start = (bf16[68,128,128]{2,1,0:T(8,128)(2,1)}, bf16[68,128,128]{2,1,0:T(8,128)(2,1)}, u32[]{:S(2)}, u32[]{:S(2)}) collective-permute-start(bf16[68,128,128]{2,1,0:T(8,128)(2,1)} %get-tuple-element.25), channel_id=1, source_target_pairs={{0,16},{8,24},{16,0},{24,8},{32,48},{40,56},{48,32},{56,40},{64,80... | collective-permute-start | bytes 6684680 | tf_op jit(solution)/shard_map/ppermute | solution.py:27
  5.6 22.4 %collective-permute-start.1 = (bf16[68,128,128]{2,1,0:T(8,128)(2,1)}, bf16[68,128,128]{2,1,0:T(8,128)(2,1)}, u32[]{:S(2)}, u32[]{:S(2)}) collective-permute-start(bf16[68,128,128]{2,1,0:T(8,128)(2,1)} %get-tuple-element.26), channel_id=1, source_target_pairs={{0,31},{8,23},{16,15},{24,7},{32,63},{40,55},{48,47},{56,39},{64,9... | collective-permute-start | bytes 6684680 | tf_op jit(solution)/shard_map/ppermute | solution.py:27
  7.6 31.1 %collective-permute-start.5 = (bf16[80,128,128]{2,1,0:T(8,128)(2,1)}, bf16[80,128,128]{2,1,0:T(8,128)(2,1)}, u32[]{:S(2)}, u32[]{:S(2)}) collective-permute-start(bf16[80,128,128]{2,1,0:T(8,128)(2,1)} %bitcast.16), channel_id=1, source_target_pairs={{2,114},{3,115},{4,116},{5,117},{6,118},{7,119},{10,122},{11,123},... | collective-permute-start | bytes 7864328 | tf_op jit(solution)/shard_map/ppermute | solution.py:27
  9.7 18.3 %collective-permute-start.2 = (bf16[24,128,128]{2,1,0:T(8,128)(2,1)}, bf16[24,128,128]{2,1,0:T(8,128)(2,1)S(1)}, u32[]{:S(2)}, u32[]{:S(2)}) collective-permute-start(bf16[24,128,128]{2,1,0:T(8,128)(2,1)} %get-tuple-element.27), channel_id=1, source_target_pairs={{0,5},{8,13},{16,21},{24,29},{32,37},{40,45},{48,53},{56,61},{64,6... | collective-permute-start | bytes 2359304 | tf_op jit(solution)/shard_map/ppermute | solution.py:27
  12.6 51.8 %copy-start.9 = (s32[90]{0:T(128)S(1)}, s32[90]{0:T(128)}, u32[]{:S(2)}) copy-start(s32[90]{0:T(128)} %pad_add_fusion.1.first_meta) | copy-start | bytes 1084
  12.6 55.3 %copy-start.5 = (s32[180]{0:T(256)S(1)}, s32[180]{0:T(256)}, u32[]{:S(2)}) copy-start(s32[180]{0:T(256)} %pad_add_fusion.second_meta) | copy-start | bytes 2164
  28.0 10.7 %collective-permute-start.3 = (bf16[68,128,128]{2,1,0:T(8,128)(2,1)}, bf16[68,128,128]{2,1,0:T(8,128)(2,1)}, u32[]{:S(2)}, u32[]{:S(2)}) collective-permute-start(bf16[68,128,128]{2,1,0:T(8,128)(2,1)} %collective-permute-done), channel_id=1, source_target_pairs={{0,31},{8,23},{16,15},{24,7},{32,63},{40,55},{48,47},{56,39},{64,9... | collective-permute-start | bytes 6684680 | tf_op jit(solution)/shard_map/ppermute | solution.py:27
  30.0 6.6 %collective-permute-start.4 = (bf16[24,128,128]{2,1,0:T(8,128)(2,1)S(1)}, bf16[24,128,128]{2,1,0:T(8,128)(2,1)S(1)}, u32[]{:S(2)}, u32[]{:S(2)}) collective-permute-start(bf16[24,128,128]{2,1,0:T(8,128)(2,1)S(1)} %collective-permute-done.2), channel_id=1, source_target_pairs={{5,29},{13,21},{21,13},{29,5},{37,61},{45,53},{53,45},{61,37},{69,... | collective-permute-start | bytes 2359304 | tf_op jit(solution)/shard_map/ppermute | solution.py:27
  30.7 46.7 %collective-permute-start.10 = (bf16[80,128,128]{2,1,0:T(8,128)(2,1)}, bf16[80,128,128]{2,1,0:T(8,128)(2,1)}, u32[]{:S(2)}, u32[]{:S(2)}) collective-permute-start(bf16[80,128,128]{2,1,0:T(8,128)(2,1)} %bitcast.18), channel_id=1, source_target_pairs={{0,112},{1,113},{8,120},{9,121},{16,0},{17,1},{24,8},{25,9},{32,16... | collective-permute-start | bytes 7864328 | tf_op jit(solution)/shard_map/ppermute | solution.py:27
  36.6 40.8 %collective-permute-start.11 = (bf16[68,128,128]{2,1,0:T(8,128)(2,1)}, bf16[68,128,128]{2,1,0:T(8,128)(2,1)}, u32[]{:S(2)}, u32[]{:S(2)}) collective-permute-start(bf16[68,128,128]{2,1,0:T(8,128)(2,1)} %collective-permute-done.1), channel_id=1, source_target_pairs={{7,23},{15,31},{23,7},{31,15},{39,55},{47,63},{55,39},{63,47},{71,... | collective-permute-start | bytes 6684680 | tf_op jit(solution)/shard_map/ppermute | solution.py:27
  63.0 0.7 collective-permute-start.8
  63.7 16.0 %collective-permute-start.12 = (bf16[24,128,128]{2,1,0:T(8,128)(2,1)S(1)}, bf16[24,128,128]{2,1,0:T(8,128)(2,1)S(1)}, u32[]{:S(2)}, u32[]{:S(2)}) collective-permute-start(bf16[24,128,128]{2,1,0:T(8,128)(2,1)S(1)} %collective-permute-done.8), channel_id=1, source_target_pairs={{5,7},{13,15},{21,23},{29,31},{37,39},{45,47},{53,55},{61,63},{69,... | collective-permute-start | bytes 2359304 | tf_op jit(solution)/shard_map/ppermute | solution.py:27
  64.4 13.0 %collective-permute-start.7 = (s32[90]{0:T(128)S(1)}, s32[90]{0:T(128)S(1)}, u32[]{:S(2)}, u32[]{:S(2)}) collective-permute-start(s32[90]{0:T(128)S(1)} %copy-done.9), channel_id=1, source_target_pairs={{0,112},{1,113},{2,114},{3,115},{4,116},{5,117},{6,118},{7,119},{8... | collective-permute-start | bytes 1088 | tf_op jit(solution)/shard_map/ppermute | solution.py:27
  68.0 11.7 %collective-permute-start.9 = (s32[180]{0:T(256)S(1)}, s32[180]{0:T(256)S(1)}, u32[]{:S(2)}, u32[]{:S(2)}) collective-permute-start(s32[180]{0:T(256)S(1)} %copy-done.5), channel_id=1, source_target_pairs={{0,15},{1,0},{2,1},{3,2},{4,3},{5,4},{6,5},{7,6},{8,7},{9,8},{10,9... | collective-permute-start | bytes 2168 | tf_op jit(solution)/shard_map/ppermute | solution.py:27
  77.4 2.3 %copy-start.6 = (s32[90]{0:T(128)}, s32[90]{0:T(128)S(1)}, u32[]{:S(2)}) copy-start(s32[90]{0:T(128)S(1)} %collective-permute-done.7.first_meta) | copy-start | bytes 1084
  79.7 0.6 copy-start.4
  79.7 0.9 copy-start

commit v5 on v4

--- a/solution.py
+++ b/solution.py
@@ -42,9 +42,9 @@
     lax.fori_loop(0, table.shape[0], clear, 0, unroll=width)
     for k in range(panel_rows):
         count = meta[blank + k]
+        columns = [meta[k * slots + b] for b in range(slots)]
         for b in range(slots):
-            block = k * slots + b
-            table[k * width + meta[block]] = jnp.where(b < count, block, blank)
+            table[k * width + columns[b]] = jnp.where(b < count, k * slots + b, blank)
 
 
 def list_matches(matches, crowded, table, meta, kept_columns, slots, width):
@@ -60,18 +60,19 @@
         ]
         firsts = [(i * slots + a) << SHIFT for a in range(slots)]
         most = jnp.int32(0)
-        for f in range(kept):
-            l = i * kept + f
-            column = kept_columns[l]
-            found = jnp.int32(0)
-            for start, first in zip(starts, firsts):
-                block = table[start + column]
-                matches[l * STRIDE + found] = first + block
-                found += (block != blank).astype(jnp.int32)
-            for n in range(slots - SHORT):
-                matches[l * STRIDE + found + n] = blank
-            matches[l * STRIDE + STRIDE - 1] = found
-            most = jnp.maximum(most, found)
+        for f in range(0, kept, 2):
+            columns = [kept_columns[i * kept + f + g] for g in range(2)]
+            blocks = [[table[start + column] for start in starts] for column in columns]
+            for g in range(2):
+                at = (i * kept + f + g) * STRIDE
+                found = jnp.int32(0)
+                for block, first in zip(blocks[g], firsts):
+                    matches[at + found] = first + block
+                    found += (block != blank).astype(jnp.int32)
+                for n in range(slots - SHORT):
+                    matches[at + found + n] = blank
+                matches[at + STRIDE - 1] = found
+                most = jnp.maximum(most, found)
         crowded[i] = (most > SHORT).astype(jnp.int32)
         return carry
 
@@ -197,12 +198,12 @@
         product[l] = (value + before[0, f]).astype(product.dtype)
 
     row_products(matches, crowded, i, slots, rows, held, kept, put)
+    owners = [owner[i * kept + f] for f in range(kept)]
     for f in range(kept):
-        l = i * kept + f
-        rank = used[owner[l]]
-        used[owner[l]] = rank + 1
-        slot = owner[l] * per_owner + rank
-        pltpu.make_async_copy(product.at[l], out.at[slot], out_sem).start()
+        rank = used[owners[f]]
+        used[owners[f]] = rank + 1
+        slot = owners[f] * per_owner + rank
+        pltpu.make_async_copy(product.at[i * kept + f], out.at[slot], out_sem).start()
 
     @pl.when(i == pl.num_programs(0) - 1)
     def _():
@@ -402,15 +403,13 @@
     part_b, part_c = lax.optimization_barrier((part_b, part_c))
     part_b = move(part_b, at(last, near))
 
-    part_a, part_c, early, second_next, first_meta = lax.optimization_barrier(
-        (part_a, part_c, early, second_next, own_first_meta)
+    part_a, part_c, early, second_next, first_meta, second_meta = lax.optimization_barrier(
+        (part_a, part_c, early, second_next, own_first_meta, own_second_meta)
     )
     part_c = move(part_c, at(middle, near))
     first_meta = move(first_meta, lambda r, c: (r - 1, c))
-
-    part_c, second_meta = lax.optimization_barrier((part_c, own_second_meta))
+    second_meta = move(second_meta, lambda r, c: (r, c - 1))
     part_c = move(part_c, at(middle, lambda r, c: (r, c + last - middle)))
-    second_meta = move(second_meta, lambda r, c: (r, c - 1))
 
     place = jnp.stack([spot == span - 1, spot < 2]).astype(jnp.int32)
     outgoing = last_stop(

time: 225 us -> 226 us (level)
  transfers between devices with their start and end apart: 13 -> 13, of which waited for: 2 -> 3; matrix products, arithmetic and copies ran while one was open for 1% -> 1% of each run, Pallas kernels for 7% -> 7%
where the time goes in v5:
time: 226 us; the launch traced here: 225 us
  blocking collectives  125 us (55%)
  Pallas kernels  35.7 us (16%)
  starting transfers between devices  35.1 us (16%)
  waiting for transfers between devices  25.6 us (11%)
    all_to_all x1, blocking collectives, on_device(): lax.all_to_all(outgoing.reshape(devices, per_owner, side, side), ('row',...  125 us
    ppermute x13, starting transfers between devices, move(): return lax.ppermute(value, ('row', 'col'), pairs)  35.1 us
    ppermute x13, waiting for transfers between devices, move(): return lax.ppermute(value, ('row', 'col'), pairs)  25.6 us
    pallas_call x1, Pallas kernels, last_stop(): pl.pallas_call(last_stop_kernel, grid_spec=pltpu.PrefetchScalarGridSpec(n...  16.5 us
    pallas_call x1, Pallas kernels, first_stop(): pl.pallas_call(first_stop_kernel, grid_spec=pltpu.PrefetchScalarGridSpec(...  15.8 us
  transfers between devices with their start and end apart: 13, of which 3 were waited for; matrix products, arithmetic and copies ran while one was open for 1% of the time, Pallas kernels for 7%

profile of v5, /device:TPU:1, one launch (start us, length us, event | category | flops | bytes accessed | tf_op | source)
XLA Modules:
  0.0 225.2 jit_solution(11203542943762241454)
XLA Ops:
  0.0 3.3 %collective-permute-start.6 = (bf16[160,128,128]{2,1,0:T(8,128)(2,1)}, bf16[160,128,128]{2,1,0:T(8,128)(2,1)}, u32[]{:S(2)}, u32[]{:S(2)}) collective-permute-start(bf16[160,128,128]{2,1,0:T(8,128)(2,1)} %bitcast.11), channel_id=1, source_target_pairs={{1,0},{2,1},{3,2},{4,3},{5,4},{6,5},{7,6},{9,8},{10,9},{11,10},{12... | collective-permute-start | bytes 15728648 | tf_op jit(solution)/shard_map/ppermute | solution.py:27
  3.5 2.1 collective-permute-start
  5.6 2.0 collective-permute-start.1
  7.6 2.1 collective-permute-start.5
  9.7 0.7 collective-permute-start.2
  10.8 0.7 pad_add_fusion.second_meta
  11.4 0.6 pad_add_fusion.1.first_meta
  12.0 0.6 reshape_squeeze.19.kept_columns
  12.6 15.8 %shard_map.83 = (f32[10,12,128,128]{3,2,1,0:T(8,128)}, bf16[256,128,128]{2,1,0:T(8,128)(2,1)}) custom-call(s32[90]{0:T(128)} %pad_add_fusion.1.first_meta, s32[180]{0:T(256)} %pad_add_fusion.second_meta, s32[120]{0:T(128)} %reshape_squeeze.19.kept_columns, bf16[80,128,128]{2,1,0:T(8,128)(2,1)} %bitcast.17, bf16[160,128,128]{2,1,0:T(8,128)(2,1)} %bitcast.13), custom_call_target="tpu_custom_call" | custom-call | flops 8053063680 | bytes 31457280 | tf_op jit(solution)/shard_map/pallas_call | solution.py:227
  28.5 2.0 collective-permute-start.3
  30.5 0.7 collective-permute-start.4
  31.2 6.3 %collective-permute-start.9 = (bf16[80,128,128]{2,1,0:T(8,128)(2,1)}, bf16[80,128,128]{2,1,0:T(8,128)(2,1)}, u32[]{:S(2)}, u32[]{:S(2)}) collective-permute-start(bf16[80,128,128]{2,1,0:T(8,128)(2,1)} %bitcast.18), channel_id=1, source_target_pairs={{0,112},{1,113},{8,120},{9,121},{16,0},{17,1},{24,8},{25,9},{32,16... | collective-permute-start | bytes 7864328 | tf_op jit(solution)/shard_map/ppermute | solution.py:27
  37.6 2.1 collective-permute-start.10
  39.6 23.3 %collective-permute-done.6.second = bf16[160,128,128]{2,1,0:T(8,128)(2,1)} collective-permute-done((bf16[160,128,128]{2,1,0:T(8,128)(2,1)}, bf16[160,128,128]{2,1,0:T(8,128)(2,1)}, u32[]{:S(2)}, u32[]{:S(2)}) %collective-permute-start.6) | collective-permute-done | bytes 5242912 | tf_op jit(solution)/shard_map/ppermute | solution.py:27
  63.0 0.7 collective-permute-start.11
  63.7 0.7 collective-permute-start.12
  64.4 3.6 %collective-permute-start.7 = (s32[90]{0:T(128)S(1)}, s32[90]{0:T(128)S(1)}, u32[]{:S(2)}, u32[]{:S(2)}) collective-permute-start(s32[90]{0:T(128)S(1)} %copy-done.9), channel_id=1, source_target_pairs={{0,112},{1,113},{2,114},{3,115},{4,116},{5,117},{6,118},{7,119},{8... | collective-permute-start | bytes 1088 | tf_op jit(solution)/shard_map/ppermute | solution.py:27
  68.0 8.8 %collective-permute-start.8 = (s32[180]{0:T(256)S(1)}, s32[180]{0:T(256)S(1)}, u32[]{:S(2)}, u32[]{:S(2)}) collective-permute-start(s32[180]{0:T(256)S(1)} %copy-done.5), channel_id=1, source_target_pairs={{0,15},{1,0},{2,1},{3,2},{4,3},{5,4},{6,5},{7,6},{8,7},{9,8},{10,9... | collective-permute-start | bytes 2168 | tf_op jit(solution)/shard_map/ppermute | solution.py:27
  76.8 0.6 add_convert_fusion.place
  77.9 1.8 collective-permute-done.8.second_meta
  79.7 0.6 copy-done.4
  80.6 16.5 %shard_map.84 = bf16[256,128,128]{2,1,0:T(8,128)(2,1)} custom-call(s32[90]{0:T(128)} %copy-done.6, s32[180]{0:T(256)} %copy-done.4, s32[120]{0:T(128)} %reshape_squeeze.19.kept_columns, s32[120]{0:T(128)} %bitcast.14, s32[2]{0:T(128)} %add_convert_fusion.place, bf16[80,128,128]{2,1,0:T(8,128)(2,1)} %collective-permute-done.5.early, ...), custom_call_target="tpu_custom_call", output_to_operand_aliasing={{}: (12, {})} | custom-call | flops 1024 | bytes 1024 | tf_op jit(solution)/shard_map/pallas_call | solution.py:266
  97.1 124.8 %all_to_all.5.source = bf16[128,2,128,128]{3,2,1,0:T(8,128)(2,1)S(1)} all-to-all(bf16[128,2,128,128]{3,2,1,0:T(8,128)(2,1)} %bitcast.10), channel_id=1, replica_groups=mesh['row'=8,'col'=16] {'row','col'}, dimensions={0} | all-to-all | bytes 16777216 | tf_op jit(solution)/shard_map/all_to_all | solution.py:419
  221.9 3.3 %shard_map.85 = bf16[128,2,128,128]{3,2,1,0:T(8,128)(2,1)} custom-call(bf16[128,2,128,128]{3,2,1,0:T(8,128)(2,1)S(1)} %all_to_all.5.source), custom_call_target="tpu_custom_call" | custom-call | tf_op jit(solution)/shard_map/pallas_call | solution.py:348
  (36 shorter events, 1.3 us)
Async XLA Ops:
  0.0 63.0 %collective-permute-start.6 = (bf16[160,128,128]{2,1,0:T(8,128)(2,1)}, bf16[160,128,128]{2,1,0:T(8,128)(2,1)}, u32[]{:S(2)}, u32[]{:S(2)}) collective-permute-start(bf16[160,128,128]{2,1,0:T(8,128)(2,1)} %bitcast.11), channel_id=1, source_target_pairs={{1,0},{2,1},{3,2},{4,3},{5,4},{6,5},{7,6},{9,8},{10,9},{11,10},{12... | collective-permute-start | bytes 15728648 | tf_op jit(solution)/shard_map/ppermute | solution.py:27
  3.3 7.0 %copy-start.2 = (s32[1,10,8]{1,2,0:T(8,128)S(1)}, s32[1,10,8]{1,2,0:T(8,128)}, u32[]{:S(2)}) copy-start(s32[1,10,8]{1,2,0:T(8,128)} %param.9) | copy-start | bytes 964
  3.4 7.2 %copy-start.3 = (s32[1,20,8]{1,2,0:T(8,128)S(1)}, s32[1,20,8]{1,2,0:T(8,128)}, u32[]{:S(2)}) copy-start(s32[1,20,8]{1,2,0:T(8,128)} %param.12) | copy-start | bytes 1924
  3.4 7.4 %copy-start.7 = (s32[1,20]{1,0:T(1,128)S(1)}, s32[1,20]{1,0:T(1,128)}, u32[]{:S(2)}) copy-start(s32[1,20]{1,0:T(1,128)} %param.13) | copy-start | bytes 244
  3.4 8.0 %copy-start.8 = (s32[1,10]{1,0:T(1,128)S(1)}, s32[1,10]{1,0:T(1,128)}, u32[]{:S(2)}) copy-start(s32[1,10]{1,0:T(1,128)} %param.10) | copy-start | bytes 124
  3.4 8.6 %copy-start.1 = (s32[1,10,12]{2,0,1:T(1,128)S(1)}, s32[1,10,12]{2,0,1:T(1,128)}, u32[]{:S(2)}) copy-start(s32[1,10,12]{2,0,1:T(1,128)} %param.14) | copy-start | bytes 1444
  3.5 25.0 %collective-permute-start = (bf16[68,128,128]{2,1,0:T(8,128)(2,1)}, bf16[68,128,128]{2,1,0:T(8,128)(2,1)}, u32[]{:S(2)}, u32[]{:S(2)}) collective-permute-start(bf16[68,128,128]{2,1,0:T(8,128)(2,1)} %get-tuple-element.24), channel_id=1, source_target_pairs={{0,16},{8,24},{16,0},{24,8},{32,48},{40,56},{48,32},{56,40},{64,80... | collective-permute-start | bytes 6684680 | tf_op jit(solution)/shard_map/ppermute | solution.py:27
  5.6 22.9 %collective-permute-start.1 = (bf16[68,128,128]{2,1,0:T(8,128)(2,1)}, bf16[68,128,128]{2,1,0:T(8,128)(2,1)}, u32[]{:S(2)}, u32[]{:S(2)}) collective-permute-start(bf16[68,128,128]{2,1,0:T(8,128)(2,1)} %get-tuple-element.25), channel_id=1, source_target_pairs={{0,31},{8,23},{16,15},{24,7},{32,63},{40,55},{48,47},{56,39},{64,9... | collective-permute-start | bytes 6684680 | tf_op jit(solution)/shard_map/ppermute | solution.py:27
  7.6 32.1 %collective-permute-start.5 = (bf16[80,128,128]{2,1,0:T(8,128)(2,1)}, bf16[80,128,128]{2,1,0:T(8,128)(2,1)}, u32[]{:S(2)}, u32[]{:S(2)}) collective-permute-start(bf16[80,128,128]{2,1,0:T(8,128)(2,1)} %bitcast.16), channel_id=1, source_target_pairs={{2,114},{3,115},{4,116},{5,117},{6,118},{7,119},{10,122},{11,123},... | collective-permute-start | bytes 7864328 | tf_op jit(solution)/shard_map/ppermute | solution.py:27
  9.7 18.8 %collective-permute-start.2 = (bf16[24,128,128]{2,1,0:T(8,128)(2,1)}, bf16[24,128,128]{2,1,0:T(8,128)(2,1)S(1)}, u32[]{:S(2)}, u32[]{:S(2)}) collective-permute-start(bf16[24,128,128]{2,1,0:T(8,128)(2,1)} %get-tuple-element.26), channel_id=1, source_target_pairs={{0,5},{8,13},{16,21},{24,29},{32,37},{40,45},{48,53},{56,61},{64,6... | collective-permute-start | bytes 2359304 | tf_op jit(solution)/shard_map/ppermute | solution.py:27
  12.6 51.8 %copy-start.9 = (s32[90]{0:T(128)S(1)}, s32[90]{0:T(128)}, u32[]{:S(2)}) copy-start(s32[90]{0:T(128)} %pad_add_fusion.1.first_meta) | copy-start | bytes 1084
  12.6 55.3 %copy-start.5 = (s32[180]{0:T(256)S(1)}, s32[180]{0:T(256)}, u32[]{:S(2)}) copy-start(s32[180]{0:T(256)} %pad_add_fusion.second_meta) | copy-start | bytes 2164
  28.5 11.1 %collective-permute-start.3 = (bf16[68,128,128]{2,1,0:T(8,128)(2,1)}, bf16[68,128,128]{2,1,0:T(8,128)(2,1)}, u32[]{:S(2)}, u32[]{:S(2)}) collective-permute-start(bf16[68,128,128]{2,1,0:T(8,128)(2,1)} %collective-permute-done), channel_id=1, source_target_pairs={{0,31},{8,23},{16,15},{24,7},{32,63},{40,55},{48,47},{56,39},{64,9... | collective-permute-start | bytes 6684680 | tf_op jit(solution)/shard_map/ppermute | solution.py:27
  30.5 7.0 %collective-permute-start.4 = (bf16[24,128,128]{2,1,0:T(8,128)(2,1)S(1)}, bf16[24,128,128]{2,1,0:T(8,128)(2,1)S(1)}, u32[]{:S(2)}, u32[]{:S(2)}) collective-permute-start(bf16[24,128,128]{2,1,0:T(8,128)(2,1)S(1)} %collective-permute-done.2), channel_id=1, source_target_pairs={{5,29},{13,21},{21,13},{29,5},{37,61},{45,53},{53,45},{61,37},{69,... | collective-permute-start | bytes 2359304 | tf_op jit(solution)/shard_map/ppermute | solution.py:27
  31.2 46.7 %collective-permute-start.9 = (bf16[80,128,128]{2,1,0:T(8,128)(2,1)}, bf16[80,128,128]{2,1,0:T(8,128)(2,1)}, u32[]{:S(2)}, u32[]{:S(2)}) collective-permute-start(bf16[80,128,128]{2,1,0:T(8,128)(2,1)} %bitcast.18), channel_id=1, source_target_pairs={{0,112},{1,113},{8,120},{9,121},{16,0},{17,1},{24,8},{25,9},{32,16... | collective-permute-start | bytes 7864328 | tf_op jit(solution)/shard_map/ppermute | solution.py:27
  37.6 40.3 %collective-permute-start.10 = (bf16[68,128,128]{2,1,0:T(8,128)(2,1)}, bf16[68,128,128]{2,1,0:T(8,128)(2,1)}, u32[]{:S(2)}, u32[]{:S(2)}) collective-permute-start(bf16[68,128,128]{2,1,0:T(8,128)(2,1)} %collective-permute-done.1), channel_id=1, source_target_pairs={{7,23},{15,31},{23,7},{31,15},{39,55},{47,63},{55,39},{63,47},{71,... | collective-permute-start | bytes 6684680 | tf_op jit(solution)/shard_map/ppermute | solution.py:27
  63.0 0.7 collective-permute-start.11
  63.7 16.0 %collective-permute-start.12 = (bf16[24,128,128]{2,1,0:T(8,128)(2,1)S(1)}, bf16[24,128,128]{2,1,0:T(8,128)(2,1)S(1)}, u32[]{:S(2)}, u32[]{:S(2)}) collective-permute-start(bf16[24,128,128]{2,1,0:T(8,128)(2,1)S(1)} %collective-permute-done.11), channel_id=1, source_target_pairs={{5,7},{13,15},{21,23},{29,31},{37,39},{45,47},{53,55},{61,63},{69,... | collective-permute-start | bytes 2359304 | tf_op jit(solution)/shard_map/ppermute | solution.py:27
  64.4 13.5 %collective-permute-start.7 = (s32[90]{0:T(128)S(1)}, s32[90]{0:T(128)S(1)}, u32[]{:S(2)}, u32[]{:S(2)}) collective-permute-start(s32[90]{0:T(128)S(1)} %copy-done.9), channel_id=1, source_target_pairs={{0,112},{1,113},{2,114},{3,115},{4,116},{5,117},{6,118},{7,119},{8... | collective-permute-start | bytes 1088 | tf_op jit(solution)/shard_map/ppermute | solution.py:27
  68.0 11.7 %collective-permute-start.8 = (s32[180]{0:T(256)S(1)}, s32[180]{0:T(256)S(1)}, u32[]{:S(2)}, u32[]{:S(2)}) collective-permute-start(s32[180]{0:T(256)S(1)} %copy-done.5), channel_id=1, source_target_pairs={{0,15},{1,0},{2,1},{3,2},{4,3},{5,4},{6,5},{7,6},{8,7},{9,8},{10,9... | collective-permute-start | bytes 2168 | tf_op jit(solution)/shard_map/ppermute | solution.py:27
  77.9 1.8 copy-start.6
  79.7 0.6 copy-start.4
  79.7 0.9 copy-start

commit v6 on v5

--- a/solution.py
+++ b/solution.py
@@ -10,9 +10,6 @@
 VMEM_LIMIT = 40 * 1024 * 1024
 LARGE_VMEM_LIMIT = 62 * 1024 * 1024
 TABLE_ROWS = 20
-SHORT = 4
-STRIDE = 13
-SHIFT = 8
 PIECE = 8
 
 
@@ -47,38 +44,6 @@
             table[k * width + columns[b]] = jnp.where(b < count, k * slots + b, blank)
 
 
-def list_matches(matches, crowded, table, meta, kept_columns, slots, width):
-    row_total = meta.shape[0] // (slots + 1)
-    kept = kept_columns.shape[0] // row_total
-    blank = TABLE_ROWS * slots
-
-    def one_row(i, carry):
-        count = meta[row_total * slots + i]
-        starts = [
-            jnp.where(a < count, meta[i * slots + a] * width, TABLE_ROWS * width)
-            for a in range(slots)
-        ]
-        firsts = [(i * slots + a) << SHIFT for a in range(slots)]
-        most = jnp.int32(0)
-        for f in range(0, kept, 2):
-            columns = [kept_columns[i * kept + f + g] for g in range(2)]
-            blocks = [[table[start + column] for start in starts] for column in columns]
-            for g in range(2):
-                at = (i * kept + f + g) * STRIDE
-                found = jnp.int32(0)
-                for block, first in zip(blocks[g], firsts):
-                    matches[at + found] = first + block
-                    found += (block != blank).astype(jnp.int32)
-                for n in range(slots - SHORT):
-                    matches[at + found + n] = blank
-                matches[at + STRIDE - 1] = found
-                most = jnp.maximum(most, found)
-        crowded[i] = (most > SHORT).astype(jnp.int32)
-        return carry
-
-    lax.fori_loop(0, row_total, one_row, 0)
-
-
 def load_pieces(source, target, sem):
     total = source.shape[0]
     for at in range(0, total, PIECE):
@@ -86,41 +51,42 @@
         pltpu.make_async_copy(source.at[piece], target.at[piece], sem).start()
 
 
-def matched_product(matches, l, terms, rows, held):
-    codes = [matches[l * STRIDE + n] for n in range(terms)]
-    left = jnp.concatenate([rows[code >> SHIFT] for code in codes], axis=1)
-    right = jnp.concatenate([held[code & ((1 << SHIFT) - 1)] for code in codes], axis=0)
-    return jnp.dot(left, right, preferred_element_type=jnp.float32)
-
-
-def row_products(matches, crowded, i, slots, rows, held, kept, put):
-    for f in range(kept):
-        l = i * kept + f
-        put(l, f, matched_product(matches, l, SHORT, rows, held))
-
-    @pl.when(crowded[i] != 0)
-    def _():
-        def again(f, carry):
-            l = i * kept + f
-
-            @pl.when(matches[l * STRIDE + STRIDE - 1] > SHORT)
-            def _():
-                put(l, f, matched_product(matches, l, slots, rows, held))
-
-            return carry
-
-        lax.fori_loop(0, kept, again, 0)
+def row_products(table, first_meta, kept_columns, i, slots, kept, rows, held, put):
+    width = table.shape[0] // (TABLE_ROWS + 1)
+    side = held.shape[1]
+    row_total = kept_columns.shape[0] // kept
+    count = first_meta[row_total * slots + i]
+
+    def over(terms):
+        starts = [
+            jnp.where(a < count, first_meta[i * slots + a] * width, TABLE_ROWS * width)
+            for a in range(terms)
+        ]
+        left = jnp.concatenate([rows[i * slots + a] for a in range(terms)], axis=1)
+        for f in range(0, kept, 2):
+            picked = []
+            for g in range(2):
+                column = kept_columns[i * kept + f + g]
+                blocks = [held[table[start + column]] for start in starts]
+                picked.append(jnp.concatenate(blocks, axis=0))
+            right = jnp.concatenate(picked, axis=1)
+            both = jnp.dot(left, right, preferred_element_type=jnp.float32)
+            put(f, both[:, :side])
+            put(f + 1, both[:, side:])
+
+    fewer = -1
+    for terms in (slots // 2, slots * 3 // 4, slots):
+        pl.when((count > fewer) & (count <= terms))(functools.partial(over, terms))
+        fewer = terms
 
 
 def first_stop_kernel(
     first_meta, second_meta, kept_columns, first, second,
-    total, blank, table, matches, crowded, held, rows, zeros, held_sem, row_sem, blank_sem,
+    total, blank, table, held, rows, zeros, held_sem, row_sem, blank_sem,
 ):
     i = pl.program_id(0)
     kept = total.shape[1]
-    row_total = pl.num_programs(0)
-    slots = rows.shape[0] // (kept_columns.shape[0] // kept)
-    width = table.shape[0] // (TABLE_ROWS + 1)
+    slots = rows.shape[0] * kept // kept_columns.shape[0]
     part = zeros.shape[0]
     panel = held.at[pl.ds(0, second.shape[0])]
 
@@ -130,19 +96,18 @@
         load_pieces(first, rows, row_sem)
         held[second.shape[0]] = jnp.zeros(held.shape[1:], held.dtype)
         zeros[...] = jnp.zeros(zeros.shape, zeros.dtype)
-        fill_table(table, second_meta, slots, width)
-        list_matches(matches, crowded, table, first_meta, kept_columns, slots, width)
+        fill_table(table, second_meta, slots, table.shape[0] // (TABLE_ROWS + 1))
         pltpu.make_async_copy(rows, rows, row_sem).wait()
         pltpu.make_async_copy(panel, panel, held_sem).wait()
         for j in range(blank.shape[0] // part):
             pltpu.make_async_copy(zeros, blank.at[pl.ds(j * part, part)], blank_sem).start()
 
-    def put(l, f, value):
+    def put(f, value):
         total[0, f] = value
 
-    row_products(matches, crowded, i, slots, rows, held, kept, put)
-
-    @pl.when(i == row_total - 1)
+    row_products(table, first_meta, kept_columns, i, slots, kept, rows, held, put)
+
+    @pl.when(i == pl.num_programs(0) - 1)
     def _():
         pltpu.make_async_copy(blank, blank, blank_sem).wait()
 
@@ -150,13 +115,12 @@
 def last_stop_kernel(
     first_meta, second_meta, kept_columns, owner, place,
     early, late, before, second, part_a, part_b, part_c, blank,
-    out, table, matches, crowded, used, held, rows, product, held_sem, row_sem, out_sem,
+    out, table, used, held, rows, product, held_sem, row_sem, out_sem,
 ):
     del blank
     i = pl.program_id(0)
     kept = before.shape[1]
-    slots = rows.shape[0] // (kept_columns.shape[0] // kept)
-    width = table.shape[0] // (TABLE_ROWS + 1)
+    slots = rows.shape[0] * kept // kept_columns.shape[0]
     per_owner = out.shape[0] // used.shape[0]
     total = held.shape[0] - 1
     panel = held.at[pl.ds(0, total)]
@@ -189,33 +153,23 @@
             return carry
 
         lax.fori_loop(0, used.shape[0], clear, 0, unroll=16)
-        fill_table(table, second_meta, slots, width)
-        list_matches(matches, crowded, table, first_meta, kept_columns, slots, width)
+        fill_table(table, second_meta, slots, table.shape[0] // (TABLE_ROWS + 1))
         pltpu.make_async_copy(rows, rows, row_sem).wait()
         pltpu.make_async_copy(panel, panel, held_sem).wait()
 
-    def put(l, f, value):
+    def put(f, value):
+        l = i * kept + f
         product[l] = (value + before[0, f]).astype(product.dtype)
-
-    row_products(matches, crowded, i, slots, rows, held, kept, put)
-    owners = [owner[i * kept + f] for f in range(kept)]
-    for f in range(kept):
-        rank = used[owners[f]]
-        used[owners[f]] = rank + 1
-        slot = owners[f] * per_owner + rank
-        pltpu.make_async_copy(product.at[i * kept + f], out.at[slot], out_sem).start()
+        rank = used[owner[l]]
+        used[owner[l]] = rank + 1
+        slot = owner[l] * per_owner + rank
+        pltpu.make_async_copy(product.at[l], out.at[slot], out_sem).start()
+
+    row_products(table, first_meta, kept_columns, i, slots, kept, rows, held, put)
 
     @pl.when(i == pl.num_programs(0) - 1)
     def _():
         pltpu.make_async_copy(product, out.at[pl.ds(0, product.shape[0])], out_sem).wait()
-
-
-def list_scratch(kept_total, row_total):
-    return [
-        pltpu.SMEM(((TABLE_ROWS + 1) * TABLE_ROWS,), jnp.int32),
-        pltpu.SMEM((kept_total * STRIDE,), jnp.int32),
-        pltpu.SMEM((row_total,), jnp.int32),
-    ]
 
 
 def first_stop(first_meta, second_meta, kept_columns, first, second, outgoing):
@@ -234,7 +188,8 @@
                 pl.BlockSpec((1, kept, side, side), lambda i, *_: (i, 0, 0, 0)),
                 pl.BlockSpec(memory_space=pl.ANY),
             ],
-            scratch_shapes=list_scratch(rows * kept, rows) + [
+            scratch_shapes=[
+                pltpu.SMEM(((TABLE_ROWS + 1) * TABLE_ROWS,), jnp.int32),
                 pltpu.VMEM((second_total + 1, side, side), second.dtype),
                 pltpu.VMEM(first.shape, first.dtype),
                 pltpu.VMEM((part, side, side), second.dtype),
@@ -263,23 +218,20 @@
     side = early.shape[1]
     rows, kept = before.shape[:2]
     second_total = second.shape[0]
+    anywhere = pl.BlockSpec(memory_space=pl.ANY)
     return pl.pallas_call(
         last_stop_kernel,
         grid_spec=pltpu.PrefetchScalarGridSpec(
             num_scalar_prefetch=5,
             grid=(rows,),
             in_specs=[
-                pl.BlockSpec(memory_space=pl.ANY),
-                pl.BlockSpec(memory_space=pl.ANY),
+                anywhere,
+                anywhere,
                 pl.BlockSpec((1, kept, side, side), lambda i, *_: (i, 0, 0, 0)),
-                pl.BlockSpec(memory_space=pl.ANY),
-                pl.BlockSpec(memory_space=pl.ANY),
-                pl.BlockSpec(memory_space=pl.ANY),
-                pl.BlockSpec(memory_space=pl.ANY),
-                pl.BlockSpec(memory_space=pl.ANY),
-            ],
-            out_specs=pl.BlockSpec(memory_space=pl.ANY),
-            scratch_shapes=list_scratch(rows * kept, rows) + [
+            ] + [anywhere] * 5,
+            out_specs=anywhere,
+            scratch_shapes=[
+                pltpu.SMEM(((TABLE_ROWS + 1) * TABLE_ROWS,), jnp.int32),
                 pltpu.SMEM((owners,), jnp.int32),
                 pltpu.VMEM((second_total + 1, side, side), second.dtype),
                 pltpu.VMEM(early.shape, early.dtype),
@@ -299,7 +251,7 @@
     )
 
 
-def cut_kernel(place, source, *rest):
+def cut_kernel(start, place, source, *rest):
     held, in_sem, out_sem = rest[-3:]
     targets = rest[:-3]
 
@@ -307,9 +259,9 @@
     def _():
         loads, stores, at = [], [], 0
         for n, target in enumerate(targets):
-            piece = pl.ds(at, target.shape[0])
-            loads.append(pltpu.make_async_copy(source.at[piece], held.at[piece], in_sem.at[n]))
-            stores.append(pltpu.make_async_copy(held.at[piece], target, out_sem.at[n]))
+            piece, size = pl.ds(start + at, target.shape[0]), pl.ds(at, target.shape[0])
+            loads.append(pltpu.make_async_copy(source.at[piece], held.at[size], in_sem.at[n]))
+            stores.append(pltpu.make_async_copy(held.at[size], target, out_sem.at[n]))
             at += target.shape[0]
         for load in loads:
             load.start()
@@ -320,14 +272,14 @@
             store.wait()
 
 
-def cut(place, value, sizes):
+def cut(place, value, start, sizes):
     return pl.pallas_call(
-        cut_kernel,
+        functools.partial(cut_kernel, start),
         in_specs=[pl.BlockSpec(memory_space=pltpu.SMEM), pl.BlockSpec(memory_space=pl.ANY)],
         out_specs=[pl.BlockSpec(memory_space=pl.ANY)] * len(sizes),
         out_shape=[jax.ShapeDtypeStruct((size,) + value.shape[1:], value.dtype) for size in sizes],
         scratch_shapes=[
-            pltpu.VMEM(value.shape, value.dtype),
+            pltpu.VMEM((sum(sizes),) + value.shape[1:], value.dtype),
             pltpu.SemaphoreType.DMA((len(sizes),)),
             pltpu.SemaphoreType.DMA((len(sizes),)),
         ],
@@ -379,8 +331,9 @@
     def at(place, step):
         return lambda r, c: step(r, c) if c % span == place else None
 
-    part_a, part_b, part_c = cut(crossing, second, (large, large, total - 2 * large))
+    (part_a,) = cut(crossing, second, 0, (large,))
     part_a = move(part_a, at(0, near))
+    part_b, part_c = cut(crossing, second, large, (large, total - 2 * large))
     part_b = move(part_b, at(0, lambda r, c: far(r, c + last)))
     part_c = move(part_c, at(0, lambda r, c: (r, c + middle)))
     early = move(first, lambda r, c: (r - 1, c) if c % span > 1 else None)

time: 226 us -> 225 us (level)
  Pallas kernels: 35.7 us -> 31 us
  waiting for transfers between devices: 25.6 us -> 28.6 us
    ppermute x13, waiting for transfers between devices: 25.6 us -> 28.6 us  [move(): return lax.ppermute(value, ('row', 'col'), pairs)]
    pallas_call x1, Pallas kernels: 16.5 us -> 13.9 us  [last_stop(): pl.pallas_call(last_stop_kernel, grid_spec=pltpu.PrefetchScalarGridSpec(n...]
  transfers between devices with their start and end apart: 13 -> 13, of which waited for: 3 -> 2; matrix products, arithmetic and copies ran while one was open for 1% -> 1% of each run, Pallas kernels for 7% -> 6%
where the time goes in v6:
time: 225 us; the launch traced here: 222 us
  blocking collectives  124 us (55%)
  starting transfers between devices  34.4 us (15%)
  Pallas kernels  31 us (14%)
  waiting for transfers between devices  28.6 us (13%)
    all_to_all x1, blocking collectives, on_device(): lax.all_to_all(outgoing.reshape(devices, per_owner, side, side), ('row',...  124 us
    ppermute x13, starting transfers between devices, move(): return lax.ppermute(value, ('row', 'col'), pairs)  34.4 us
    ppermute x13, waiting for transfers between devices, move(): return lax.ppermute(value, ('row', 'col'), pairs)  28.6 us
    pallas_call x1, Pallas kernels, last_stop(): pl.pallas_call(last_stop_kernel, grid_spec=pltpu.PrefetchScalarGridSpec(n...  13.9 us
    pallas_call x1, Pallas kernels, first_stop(): pl.pallas_call(first_stop_kernel, grid_spec=pltpu.PrefetchScalarGridSpec(...  13.7 us
  transfers between devices with their start and end apart: 13, of which 2 were waited for; matrix products, arithmetic and copies ran while one was open for 1% of the time, Pallas kernels for 6%

profile of v6, /device:TPU:1, one launch (start us, length us, event | category | flops | bytes accessed | tf_op | source)
XLA Modules:
  0.0 222.0 jit_solution(8829483905229807841)
XLA Ops:
  0.0 3.3 %collective-permute-start.6 = (bf16[160,128,128]{2,1,0:T(8,128)(2,1)}, bf16[160,128,128]{2,1,0:T(8,128)(2,1)}, u32[]{:S(2)}, u32[]{:S(2)}) collective-permute-start(bf16[160,128,128]{2,1,0:T(8,128)(2,1)} %bitcast.11), channel_id=1, source_target_pairs={{1,0},{2,1},{3,2},{4,3},{5,4},{6,5},{7,6},{9,8},{10,9},{11,10},{12... | collective-permute-start | bytes 15728648 | tf_op jit(solution)/shard_map/ppermute | solution.py:24
  3.4 2.2 %collective-permute-start = (bf16[68,128,128]{2,1,0:T(8,128)(2,1)}, bf16[68,128,128]{2,1,0:T(8,128)(2,1)}, u32[]{:S(2)}, u32[]{:S(2)}) collective-permute-start(bf16[68,128,128]{2,1,0:T(8,128)(2,1)} %shard_map.82), channel_id=1, source_target_pairs={{0,16},{8,24},{16,0},{24,8},{32,48},{40,56},{48,32},{56,40},{64,80... | collective-permute-start | bytes 6684680 | tf_op jit(solution)/shard_map/ppermute | solution.py:24
  5.7 2.0 collective-permute-start.1
  7.7 2.1 collective-permute-start.5
  9.8 0.7 collective-permute-start.2
  10.9 0.7 pad_add_fusion.second_meta
  11.6 0.6 pad_add_fusion.1.first_meta
  12.2 0.6 reshape_squeeze.19.kept_columns
  12.8 13.7 %shard_map.84 = (f32[10,12,128,128]{3,2,1,0:T(8,128)}, bf16[256,128,128]{2,1,0:T(8,128)(2,1)}) custom-call(s32[90]{0:T(128)} %pad_add_fusion.1.first_meta, s32[180]{0:T(256)} %pad_add_fusion.second_meta, s32[120]{0:T(128)} %reshape_squeeze.19.kept_columns, bf16[80,128,128]{2,1,0:T(8,128)(2,1)} %bitcast.18, bf16[160,128,128]{2,1,0:T(8,128)(2,1)} %bitcast.14), custom_call_target="tpu_custom_call" | custom-call | flops 8053063680 | bytes 31457280 | tf_op jit(solution)/shard_map/pallas_call | solution.py:181
  26.5 2.0 collective-permute-start.3
  28.6 0.7 collective-permute-start.4
  29.3 5.3 %collective-permute-start.9 = (bf16[80,128,128]{2,1,0:T(8,128)(2,1)}, bf16[80,128,128]{2,1,0:T(8,128)(2,1)}, u32[]{:S(2)}, u32[]{:S(2)}) collective-permute-start(bf16[80,128,128]{2,1,0:T(8,128)(2,1)} %bitcast.19), channel_id=1, source_target_pairs={{0,112},{1,113},{8,120},{9,121},{16,0},{17,1},{24,8},{25,9},{32,16... | collective-permute-start | bytes 7864328 | tf_op jit(solution)/shard_map/ppermute | solution.py:24
  34.6 2.1 collective-permute-start.10
  36.6 26.3 %collective-permute-done.6.second = bf16[160,128,128]{2,1,0:T(8,128)(2,1)} collective-permute-done((bf16[160,128,128]{2,1,0:T(8,128)(2,1)}, bf16[160,128,128]{2,1,0:T(8,128)(2,1)}, u32[]{:S(2)}, u32[]{:S(2)}) %collective-permute-start.6) | collective-permute-done | bytes 5242912 | tf_op jit(solution)/shard_map/ppermute | solution.py:24
  63.0 0.7 collective-permute-start.11
  63.7 0.7 collective-permute-start.12
  64.4 3.6 %collective-permute-start.7 = (s32[90]{0:T(128)S(1)}, s32[90]{0:T(128)S(1)}, u32[]{:S(2)}, u32[]{:S(2)}) collective-permute-start(s32[90]{0:T(128)S(1)} %copy-done.9), channel_id=1, source_target_pairs={{0,112},{1,113},{2,114},{3,115},{4,116},{5,117},{6,118},{7,119},{8... | collective-permute-start | bytes 1088 | tf_op jit(solution)/shard_map/ppermute | solution.py:24
  68.0 9.0 %collective-permute-start.8 = (s32[180]{0:T(256)S(1)}, s32[180]{0:T(256)S(1)}, u32[]{:S(2)}, u32[]{:S(2)}) collective-permute-start(s32[180]{0:T(256)S(1)} %copy-done.5), channel_id=1, source_target_pairs={{0,15},{1,0},{2,1},{3,2},{4,3},{5,4},{6,5},{7,6},{8,7},{9,8},{10,9... | collective-permute-start | bytes 2168 | tf_op jit(solution)/shard_map/ppermute | solution.py:24
  76.9 0.6 add_convert_fusion.place
  77.6 2.2 %collective-permute-done.8.second_meta = s32[180]{0:T(256)S(1)} collective-permute-done((s32[180]{0:T(256)S(1)}, s32[180]{0:T(256)S(1)}, u32[]{:S(2)}, u32[]{:S(2)}) %collective-permute-start.8) | collective-permute-done | bytes 752 | tf_op jit(solution)/shard_map/ppermute | solution.py:24
  79.9 0.6 copy-done.4
  80.8 13.9 %shard_map.85 = bf16[256,128,128]{2,1,0:T(8,128)(2,1)} custom-call(s32[90]{0:T(128)} %copy-done.6, s32[180]{0:T(256)} %copy-done.4, s32[120]{0:T(128)} %reshape_squeeze.19.kept_columns, s32[120]{0:T(128)} %bitcast.15, s32[2]{0:T(128)} %add_convert_fusion.place, bf16[80,128,128]{2,1,0:T(8,128)(2,1)} %collective-permute-done.5.early, ...), custom_call_target="tpu_custom_call", output_to_operand_aliasing={{}: (12, {})} | custom-call | flops 1024 | bytes 1024 | tf_op jit(solution)/shard_map/pallas_call | solution.py:222
  94.7 124.0 %all_to_all.5.source = bf16[128,2,128,128]{3,2,1,0:T(8,128)(2,1)S(1)} all-to-all(bf16[128,2,128,128]{3,2,1,0:T(8,128)(2,1)} %bitcast.10), channel_id=1, replica_groups=mesh['row'=8,'col'=16] {'row','col'}, dimensions={0} | all-to-all | bytes 16777216 | tf_op jit(solution)/shard_map/all_to_all | solution.py:372
  218.7 3.3 %shard_map.86 = bf16[128,2,128,128]{3,2,1,0:T(8,128)(2,1)} custom-call(bf16[128,2,128,128]{3,2,1,0:T(8,128)(2,1)S(1)} %all_to_all.5.source), custom_call_target="tpu_custom_call" | custom-call | tf_op jit(solution)/shard_map/pallas_call | solution.py:300
  (37 shorter events, 0.8 us)
Async XLA Ops:
  0.0 63.0 %collective-permute-start.6 = (bf16[160,128,128]{2,1,0:T(8,128)(2,1)}, bf16[160,128,128]{2,1,0:T(8,128)(2,1)}, u32[]{:S(2)}, u32[]{:S(2)}) collective-permute-start(bf16[160,128,128]{2,1,0:T(8,128)(2,1)} %bitcast.11), channel_id=1, source_target_pairs={{1,0},{2,1},{3,2},{4,3},{5,4},{6,5},{7,6},{9,8},{10,9},{11,10},{12... | collective-permute-start | bytes 15728648 | tf_op jit(solution)/shard_map/ppermute | solution.py:24
  3.4 7.2 %copy-start.2 = (s32[1,10,8]{1,2,0:T(8,128)S(1)}, s32[1,10,8]{1,2,0:T(8,128)}, u32[]{:S(2)}) copy-start(s32[1,10,8]{1,2,0:T(8,128)} %param.9) | copy-start | bytes 964
  3.4 7.3 %copy-start.3 = (s32[1,20,8]{1,2,0:T(8,128)S(1)}, s32[1,20,8]{1,2,0:T(8,128)}, u32[]{:S(2)}) copy-start(s32[1,20,8]{1,2,0:T(8,128)} %param.12) | copy-start | bytes 1924
  3.4 7.5 %copy-start.7 = (s32[1,20]{1,0:T(1,128)S(1)}, s32[1,20]{1,0:T(1,128)}, u32[]{:S(2)}) copy-start(s32[1,20]{1,0:T(1,128)} %param.13) | copy-start | bytes 244
  3.4 8.2 %copy-start.8 = (s32[1,10]{1,0:T(1,128)S(1)}, s32[1,10]{1,0:T(1,128)}, u32[]{:S(2)}) copy-start(s32[1,10]{1,0:T(1,128)} %param.10) | copy-start | bytes 124
  3.4 8.7 %copy-start.1 = (s32[1,10,12]{2,0,1:T(1,128)S(1)}, s32[1,10,12]{2,0,1:T(1,128)}, u32[]{:S(2)}) copy-start(s32[1,10,12]{2,0,1:T(1,128)} %param.14) | copy-start | bytes 1444
  3.4 23.1 %collective-permute-start = (bf16[68,128,128]{2,1,0:T(8,128)(2,1)}, bf16[68,128,128]{2,1,0:T(8,128)(2,1)}, u32[]{:S(2)}, u32[]{:S(2)}) collective-permute-start(bf16[68,128,128]{2,1,0:T(8,128)(2,1)} %shard_map.82), channel_id=1, source_target_pairs={{0,16},{8,24},{16,0},{24,8},{32,48},{40,56},{48,32},{56,40},{64,80... | collective-permute-start | bytes 6684680 | tf_op jit(solution)/shard_map/ppermute | solution.py:24
  5.7 20.8 %collective-permute-start.1 = (bf16[68,128,128]{2,1,0:T(8,128)(2,1)}, bf16[68,128,128]{2,1,0:T(8,128)(2,1)}, u32[]{:S(2)}, u32[]{:S(2)}) collective-permute-start(bf16[68,128,128]{2,1,0:T(8,128)(2,1)} %get-tuple-element.23), channel_id=1, source_target_pairs={{0,31},{8,23},{16,15},{24,7},{32,63},{40,55},{48,47},{56,39},{64,9... | collective-permute-start | bytes 6684680 | tf_op jit(solution)/shard_map/ppermute | solution.py:24
  7.7 28.9 %collective-permute-start.5 = (bf16[80,128,128]{2,1,0:T(8,128)(2,1)}, bf16[80,128,128]{2,1,0:T(8,128)(2,1)}, u32[]{:S(2)}, u32[]{:S(2)}) collective-permute-start(bf16[80,128,128]{2,1,0:T(8,128)(2,1)} %bitcast.17), channel_id=1, source_target_pairs={{2,114},{3,115},{4,116},{5,117},{6,118},{7,119},{10,122},{11,123},... | collective-permute-start | bytes 7864328 | tf_op jit(solution)/shard_map/ppermute | solution.py:24
  9.8 16.7 %collective-permute-start.2 = (bf16[24,128,128]{2,1,0:T(8,128)(2,1)}, bf16[24,128,128]{2,1,0:T(8,128)(2,1)S(1)}, u32[]{:S(2)}, u32[]{:S(2)}) collective-permute-start(bf16[24,128,128]{2,1,0:T(8,128)(2,1)} %get-tuple-element.24), channel_id=1, source_target_pairs={{0,5},{8,13},{16,21},{24,29},{32,37},{40,45},{48,53},{56,61},{64,6... | collective-permute-start | bytes 2359304 | tf_op jit(solution)/shard_map/ppermute | solution.py:24
  12.8 51.6 %copy-start.9 = (s32[90]{0:T(128)S(1)}, s32[90]{0:T(128)}, u32[]{:S(2)}) copy-start(s32[90]{0:T(128)} %pad_add_fusion.1.first_meta) | copy-start | bytes 1084
  12.8 55.2 %copy-start.5 = (s32[180]{0:T(256)S(1)}, s32[180]{0:T(256)}, u32[]{:S(2)}) copy-start(s32[180]{0:T(256)} %pad_add_fusion.second_meta) | copy-start | bytes 2164
  26.5 10.1 %collective-permute-start.3 = (bf16[68,128,128]{2,1,0:T(8,128)(2,1)}, bf16[68,128,128]{2,1,0:T(8,128)(2,1)}, u32[]{:S(2)}, u32[]{:S(2)}) collective-permute-start(bf16[68,128,128]{2,1,0:T(8,128)(2,1)} %collective-permute-done), channel_id=1, source_target_pairs={{0,31},{8,23},{16,15},{24,7},{32,63},{40,55},{48,47},{56,39},{64,9... | collective-permute-start | bytes 6684680 | tf_op jit(solution)/shard_map/ppermute | solution.py:24
  28.6 6.0 %collective-permute-start.4 = (bf16[24,128,128]{2,1,0:T(8,128)(2,1)S(1)}, bf16[24,128,128]{2,1,0:T(8,128)(2,1)S(1)}, u32[]{:S(2)}, u32[]{:S(2)}) collective-permute-start(bf16[24,128,128]{2,1,0:T(8,128)(2,1)S(1)} %collective-permute-done.2), channel_id=1, source_target_pairs={{5,29},{13,21},{21,13},{29,5},{37,61},{45,53},{53,45},{61,37},{69,... | collective-permute-start | bytes 2359304 | tf_op jit(solution)/shard_map/ppermute | solution.py:24
  29.3 48.3 %collective-permute-start.9 = (bf16[80,128,128]{2,1,0:T(8,128)(2,1)}, bf16[80,128,128]{2,1,0:T(8,128)(2,1)}, u32[]{:S(2)}, u32[]{:S(2)}) collective-permute-start(bf16[80,128,128]{2,1,0:T(8,128)(2,1)} %bitcast.19), channel_id=1, source_target_pairs={{0,112},{1,113},{8,120},{9,121},{16,0},{17,1},{24,8},{25,9},{32,16... | collective-permute-start | bytes 7864328 | tf_op jit(solution)/shard_map/ppermute | solution.py:24
  34.6 43.0 %collective-permute-start.10 = (bf16[68,128,128]{2,1,0:T(8,128)(2,1)}, bf16[68,128,128]{2,1,0:T(8,128)(2,1)}, u32[]{:S(2)}, u32[]{:S(2)}) collective-permute-start(bf16[68,128,128]{2,1,0:T(8,128)(2,1)} %collective-permute-done.1), channel_id=1, source_target_pairs={{7,23},{15,31},{23,7},{31,15},{39,55},{47,63},{55,39},{63,47},{71,... | collective-permute-start | bytes 6684680 | tf_op jit(solution)/shard_map/ppermute | solution.py:24
  63.0 0.7 collective-permute-start.11
  63.7 16.2 %collective-permute-start.12 = (bf16[24,128,128]{2,1,0:T(8,128)(2,1)S(1)}, bf16[24,128,128]{2,1,0:T(8,128)(2,1)S(1)}, u32[]{:S(2)}, u32[]{:S(2)}) collective-permute-start(bf16[24,128,128]{2,1,0:T(8,128)(2,1)S(1)} %collective-permute-done.11), channel_id=1, source_target_pairs={{5,7},{13,15},{21,23},{29,31},{37,39},{45,47},{53,55},{61,63},{69,... | collective-permute-start | bytes 2359304 | tf_op jit(solution)/shard_map/ppermute | solution.py:24
  64.4 13.2 %collective-permute-start.7 = (s32[90]{0:T(128)S(1)}, s32[90]{0:T(128)S(1)}, u32[]{:S(2)}, u32[]{:S(2)}) collective-permute-start(s32[90]{0:T(128)S(1)} %copy-done.9), channel_id=1, source_target_pairs={{0,112},{1,113},{2,114},{3,115},{4,116},{5,117},{6,118},{7,119},{8... | collective-permute-start | bytes 1088 | tf_op jit(solution)/shard_map/ppermute | solution.py:24
  68.0 11.9 %collective-permute-start.8 = (s32[180]{0:T(256)S(1)}, s32[180]{0:T(256)S(1)}, u32[]{:S(2)}, u32[]{:S(2)}) collective-permute-start(s32[180]{0:T(256)S(1)} %copy-done.5), channel_id=1, source_target_pairs={{0,15},{1,0},{2,1},{3,2},{4,3},{5,4},{6,5},{7,6},{8,7},{9,8},{10,9... | collective-permute-start | bytes 2168 | tf_op jit(solution)/shard_map/ppermute | solution.py:24
  77.6 2.3 %copy-start.6 = (s32[90]{0:T(128)}, s32[90]{0:T(128)S(1)}, u32[]{:S(2)}) copy-start(s32[90]{0:T(128)S(1)} %collective-permute-done.7.first_meta) | copy-start | bytes 1084
  79.9 0.6 copy-start.4
  79.9 0.9 copy-start

commit v7 on v6

--- a/solution.py
+++ b/solution.py
@@ -10,7 +10,7 @@
 VMEM_LIMIT = 40 * 1024 * 1024
 LARGE_VMEM_LIMIT = 62 * 1024 * 1024
 TABLE_ROWS = 20
-PIECE = 8
+PIECE = 4
 
 
 def move(value, chosen):
@@ -82,10 +82,10 @@
 
 def first_stop_kernel(
     first_meta, second_meta, kept_columns, first, second,
-    total, blank, table, held, rows, zeros, held_sem, row_sem, blank_sem,
+    total, blank, table, held, rows, sums, zeros, held_sem, row_sem, sum_sem, blank_sem,
 ):
     i = pl.program_id(0)
-    kept = total.shape[1]
+    kept = total.shape[0] // pl.num_programs(0)
     slots = rows.shape[0] * kept // kept_columns.shape[0]
     part = zeros.shape[0]
     panel = held.at[pl.ds(0, second.shape[0])]
@@ -103,23 +103,27 @@
             pltpu.make_async_copy(zeros, blank.at[pl.ds(j * part, part)], blank_sem).start()
 
     def put(f, value):
-        total[0, f] = value
+        l = i * kept + f
+        sums[l] = value
+        pltpu.make_async_copy(sums.at[l], total.at[l], sum_sem).start()
 
     row_products(table, first_meta, kept_columns, i, slots, kept, rows, held, put)
 
     @pl.when(i == pl.num_programs(0) - 1)
     def _():
+        pltpu.make_async_copy(sums, total, sum_sem).wait()
         pltpu.make_async_copy(blank, blank, blank_sem).wait()
 
 
 def last_stop_kernel(
     first_meta, second_meta, kept_columns, owner, place,
     early, late, before, second, part_a, part_b, part_c, blank,
-    out, table, used, held, rows, product, held_sem, row_sem, out_sem,
+    out, table, used, held, rows, sums, product, held_sem, row_sem, sum_sem, out_sem,
 ):
     del blank
     i = pl.program_id(0)
-    kept = before.shape[1]
+    row_total = pl.num_programs(0)
+    kept = before.shape[0] // row_total
     slots = rows.shape[0] * kept // kept_columns.shape[0]
     per_owner = out.shape[0] // used.shape[0]
     total = held.shape[0] - 1
@@ -146,6 +150,10 @@
         def _():
             load_pieces(late, rows, row_sem)
 
+        for j in range(sum_sem.shape[0]):
+            row = pl.ds(j * kept, kept)
+            load_pieces(before.at[row], sums.at[row], sum_sem.at[j])
+
         held[total] = jnp.zeros(held.shape[1:], held.dtype)
 
         def clear(n, carry):
@@ -157,9 +165,12 @@
         pltpu.make_async_copy(rows, rows, row_sem).wait()
         pltpu.make_async_copy(panel, panel, held_sem).wait()
 
+    row = sums.at[pl.ds(i * kept, kept)]
+    pltpu.make_async_copy(row, row, sum_sem.at[i]).wait()
+
     def put(f, value):
         l = i * kept + f
-        product[l] = (value + before[0, f]).astype(product.dtype)
+        product[l] = (value + sums[l]).astype(product.dtype)
         rank = used[owner[l]]
         used[owner[l]] = rank + 1
         slot = owner[l] * per_owner + rank
@@ -184,27 +195,26 @@
             num_scalar_prefetch=3,
             grid=(rows,),
             in_specs=[pl.BlockSpec(memory_space=pl.ANY)] * 2,
-            out_specs=[
-                pl.BlockSpec((1, kept, side, side), lambda i, *_: (i, 0, 0, 0)),
-                pl.BlockSpec(memory_space=pl.ANY),
-            ],
+            out_specs=[pl.BlockSpec(memory_space=pl.ANY)] * 2,
             scratch_shapes=[
                 pltpu.SMEM(((TABLE_ROWS + 1) * TABLE_ROWS,), jnp.int32),
                 pltpu.VMEM((second_total + 1, side, side), second.dtype),
                 pltpu.VMEM(first.shape, first.dtype),
+                pltpu.VMEM((rows * kept, side, side), jnp.float32),
                 pltpu.VMEM((part, side, side), second.dtype),
+                pltpu.SemaphoreType.DMA,
                 pltpu.SemaphoreType.DMA,
                 pltpu.SemaphoreType.DMA,
                 pltpu.SemaphoreType.DMA,
             ],
         ),
         out_shape=[
-            jax.ShapeDtypeStruct((rows, kept, side, side), jnp.float32),
+            jax.ShapeDtypeStruct((rows * kept, side, side), jnp.float32),
             jax.ShapeDtypeStruct((outgoing, side, side), second.dtype),
         ],
         compiler_params=pltpu.CompilerParams(vmem_limit_bytes=LARGE_VMEM_LIMIT),
         cost_estimate=pl.CostEstimate(
-            flops=4 * first_total * kept * side**3,
+            flops=400 * first_total * kept * side**3,
             bytes_accessed=2 * (first_total * 2 + rows * kept * 4 + 2 * second_total) * side**2,
             transcendentals=0,
         ),
@@ -216,7 +226,7 @@
     early, late, before, second, part_a, part_b, part_c, blank, owners,
 ):
     side = early.shape[1]
-    rows, kept = before.shape[:2]
+    rows = first_meta.shape[0] - early.shape[0]
     second_total = second.shape[0]
     anywhere = pl.BlockSpec(memory_space=pl.ANY)
     return pl.pallas_call(
@@ -224,20 +234,18 @@
         grid_spec=pltpu.PrefetchScalarGridSpec(
             num_scalar_prefetch=5,
             grid=(rows,),
-            in_specs=[
-                anywhere,
-                anywhere,
-                pl.BlockSpec((1, kept, side, side), lambda i, *_: (i, 0, 0, 0)),
-            ] + [anywhere] * 5,
+            in_specs=[anywhere] * 8,
             out_specs=anywhere,
             scratch_shapes=[
                 pltpu.SMEM(((TABLE_ROWS + 1) * TABLE_ROWS,), jnp.int32),
                 pltpu.SMEM((owners,), jnp.int32),
                 pltpu.VMEM((second_total + 1, side, side), second.dtype),
                 pltpu.VMEM(early.shape, early.dtype),
-                pltpu.VMEM((rows * kept, side, side), second.dtype),
-                pltpu.SemaphoreType.DMA,
-                pltpu.SemaphoreType.DMA,
+                pltpu.VMEM(before.shape, before.dtype),
+                pltpu.VMEM(before.shape, second.dtype),
+                pltpu.SemaphoreType.DMA,
+                pltpu.SemaphoreType.DMA,
+                pltpu.SemaphoreType.DMA((rows,)),
                 pltpu.SemaphoreType.DMA,
             ],
         ),

time: 225 us -> 228 us (1.013)
  starting transfers between devices: 34.4 us -> 54.3 us
  blocking collectives: 124 us -> 114 us
  Pallas kernels: 31 us -> 26.1 us
    ppermute x13, starting transfers between devices: 34.4 us -> 54.3 us  [move(): return lax.ppermute(value, ('row', 'col'), pairs)]
    all_to_all x1, blocking collectives: 124 us -> 114 us  [on_device(): lax.all_to_all(outgoing.reshape(devices, per_owner, side, side), ('row',...]
    pallas_call x1, Pallas kernels: 13.7 us -> 10.4 us  [first_stop(): pl.pallas_call(first_stop_kernel, grid_spec=pltpu.PrefetchScalarGridSpec(...]
  transfers between devices with their start and end apart: 13 -> 13, of which waited for: 2 -> 2; matrix products, arithmetic and copies ran while one was open for 1% -> 1% of each run, Pallas kernels for 6% -> 5%
where the time goes in v7:
time: 228 us; the launch traced here: 227 us
  blocking collectives  114 us (50%)
  starting transfers between devices  54.3 us (24%)
  waiting for transfers between devices  28.3 us (12%)
  Pallas kernels  26.1 us (11%)
    all_to_all x1, blocking collectives, on_device(): lax.all_to_all(outgoing.reshape(devices, per_owner, side, side), ('row',...  114 us
    ppermute x13, starting transfers between devices, move(): return lax.ppermute(value, ('row', 'col'), pairs)  54.3 us
    ppermute x13, waiting for transfers between devices, move(): return lax.ppermute(value, ('row', 'col'), pairs)  28.3 us
    pallas_call x1, Pallas kernels, last_stop(): pl.pallas_call(last_stop_kernel, grid_spec=pltpu.PrefetchScalarGridSpec(n...  12.4 us
    pallas_call x1, Pallas kernels, first_stop(): pl.pallas_call(first_stop_kernel, grid_spec=pltpu.PrefetchScalarGridSpec(...  10.4 us
  transfers between devices with their start and end apart: 13, of which 2 were waited for; matrix products, arithmetic and copies ran while one was open for 1% of the time, Pallas kernels for 5%

profile of v7, /device:TPU:1, one launch (start us, length us, event | category | flops | bytes accessed | tf_op | source)
XLA Modules:
  0.0 227.2 jit_solution(18024332849941556861)
XLA Ops:
  0.0 3.3 %collective-permute-start.6 = (bf16[160,128,128]{2,1,0:T(8,128)(2,1)}, bf16[160,128,128]{2,1,0:T(8,128)(2,1)}, u32[]{:S(2)}, u32[]{:S(2)}) collective-permute-start(bf16[160,128,128]{2,1,0:T(8,128)(2,1)} %bitcast.11), channel_id=1, source_target_pairs={{1,0},{2,1},{3,2},{4,3},{5,4},{6,5},{7,6},{9,8},{10,9},{11,10},{12... | collective-permute-start | bytes 15728648 | tf_op jit(solution)/shard_map/ppermute | solution.py:24
  3.4 2.1 collective-permute-start
  5.5 2.3 collective-permute-start.5
  7.8 1.6 collective-permute-start.2
  9.4 2.0 collective-permute-start.1
  11.6 0.7 reshape_squeeze.19.kept_columns
  12.4 0.6 pad_add_fusion.1.first_meta
  13.1 0.6 pad_add_fusion.second_meta
  13.7 10.4 %shard_map.84 = (f32[120,128,128]{2,1,0:T(8,128)}, bf16[256,128,128]{2,1,0:T(8,128)(2,1)}) custom-call(s32[90]{0:T(128)} %pad_add_fusion.1.first_meta, s32[180]{0:T(256)} %pad_add_fusion.second_meta, s32[120]{0:T(128)} %reshape_squeeze.19.kept_columns, bf16[80,128,128]{2,1,0:T(8,128)(2,1)} %bitcast.18, bf16[160,128,128]{2,1,0:T(8,128)(2,1)} %bitcast.14), custom_call_target="tpu_custom_call" | custom-call | flops 805306368000 | bytes 31457280 | tf_op jit(solution)/shard_map/pallas_call | solution.py:192
  24.1 2.0 collective-permute-start.3
  26.1 0.7 collective-permute-start.4
  26.8 5.6 %collective-permute-start.9 = (bf16[80,128,128]{2,1,0:T(8,128)(2,1)}, bf16[80,128,128]{2,1,0:T(8,128)(2,1)}, u32[]{:S(2)}, u32[]{:S(2)}) collective-permute-start(bf16[80,128,128]{2,1,0:T(8,128)(2,1)} %bitcast.19), channel_id=1, source_target_pairs={{0,112},{1,113},{8,120},{9,121},{16,0},{17,1},{24,8},{25,9},{32,16... | collective-permute-start | bytes 7864328 | tf_op jit(solution)/shard_map/ppermute | solution.py:24
  32.5 2.1 collective-permute-start.10
  34.5 28.1 %collective-permute-done.6.second = bf16[160,128,128]{2,1,0:T(8,128)(2,1)} collective-permute-done((bf16[160,128,128]{2,1,0:T(8,128)(2,1)}, bf16[160,128,128]{2,1,0:T(8,128)(2,1)}, u32[]{:S(2)}, u32[]{:S(2)}) %collective-permute-start.6) | collective-permute-done | bytes 5242912 | tf_op jit(solution)/shard_map/ppermute | solution.py:24
  62.7 0.7 collective-permute-start.11
  63.4 0.7 collective-permute-start.12
  64.1 3.9 %collective-permute-start.7 = (s32[90]{0:T(128)S(1)}, s32[90]{0:T(128)S(1)}, u32[]{:S(2)}, u32[]{:S(2)}) collective-permute-start(s32[90]{0:T(128)S(1)} %copy-done.9), channel_id=1, source_target_pairs={{0,112},{1,113},{2,114},{3,115},{4,116},{5,117},{6,118},{7,119},{8... | collective-permute-start | bytes 1088 | tf_op jit(solution)/shard_map/ppermute | solution.py:24
  68.0 27.5 %collective-permute-start.8 = (s32[180]{0:T(256)S(1)}, s32[180]{0:T(256)S(1)}, u32[]{:S(2)}, u32[]{:S(2)}) collective-permute-start(s32[180]{0:T(256)S(1)} %copy-done.5), channel_id=1, source_target_pairs={{0,15},{1,0},{2,1},{3,2},{4,3},{5,4},{6,5},{7,6},{8,7},{9,8},{10,9... | collective-permute-start | bytes 2168 | tf_op jit(solution)/shard_map/ppermute | solution.py:24
  95.4 0.6 add_convert_fusion.place
  96.3 0.4 copy-done.6
  96.8 0.3 copy-done
  97.1 12.4 %shard_map.85 = bf16[256,128,128]{2,1,0:T(8,128)(2,1)} custom-call(s32[90]{0:T(128)} %copy-done.6, s32[180]{0:T(256)} %copy-done.4, s32[120]{0:T(128)} %reshape_squeeze.19.kept_columns, s32[120]{0:T(128)} %bitcast.15, s32[2]{0:T(128)} %add_convert_fusion.place, bf16[80,128,128]{2,1,0:T(8,128)(2,1)} %collective-permute-done.5.early, ...), custom_call_target="tpu_custom_call", output_to_operand_aliasing={{}: (12, {})} | custom-call | flops 1024 | bytes 1024 | tf_op jit(solution)/shard_map/pallas_call | solution.py:232
  109.6 114.3 %all_to_all.5.source = bf16[128,2,128,128]{3,2,1,0:T(8,128)(2,1)S(1)} all-to-all(bf16[128,2,128,128]{3,2,1,0:T(8,128)(2,1)} %bitcast.10), channel_id=1, replica_groups=mesh['row'=8,'col'=16] {'row','col'}, dimensions={0} | all-to-all | bytes 16777216 | tf_op jit(solution)/shard_map/all_to_all | solution.py:380
  223.9 3.3 %shard_map.86 = bf16[128,2,128,128]{3,2,1,0:T(8,128)(2,1)} custom-call(bf16[128,2,128,128]{3,2,1,0:T(8,128)(2,1)S(1)} %all_to_all.5.source), custom_call_target="tpu_custom_call" | custom-call | tf_op jit(solution)/shard_map/pallas_call | solution.py:308
  (37 shorter events, 0.8 us)
Async XLA Ops:
  0.0 62.7 %collective-permute-start.6 = (bf16[160,128,128]{2,1,0:T(8,128)(2,1)}, bf16[160,128,128]{2,1,0:T(8,128)(2,1)}, u32[]{:S(2)}, u32[]{:S(2)}) collective-permute-start(bf16[160,128,128]{2,1,0:T(8,128)(2,1)} %bitcast.11), channel_id=1, source_target_pairs={{1,0},{2,1},{3,2},{4,3},{5,4},{6,5},{7,6},{9,8},{10,9},{11,10},{12... | collective-permute-start | bytes 15728648 | tf_op jit(solution)/shard_map/ppermute | solution.py:24
  3.4 20.7 %collective-permute-start = (bf16[68,128,128]{2,1,0:T(8,128)(2,1)}, bf16[68,128,128]{2,1,0:T(8,128)(2,1)}, u32[]{:S(2)}, u32[]{:S(2)}) collective-permute-start(bf16[68,128,128]{2,1,0:T(8,128)(2,1)} %shard_map.82), channel_id=1, source_target_pairs={{0,16},{8,24},{16,0},{24,8},{32,48},{40,56},{48,32},{56,40},{64,80... | collective-permute-start | bytes 6684680 | tf_op jit(solution)/shard_map/ppermute | solution.py:24
  5.5 5.9 %copy-start.2 = (s32[1,10,8]{1,2,0:T(8,128)S(1)}, s32[1,10,8]{1,2,0:T(8,128)}, u32[]{:S(2)}) copy-start(s32[1,10,8]{1,2,0:T(8,128)} %param.9) | copy-start | bytes 964
  5.5 6.1 %copy-start.1 = (s32[1,10,12]{2,0,1:T(1,128)S(1)}, s32[1,10,12]{2,0,1:T(1,128)}, u32[]{:S(2)}) copy-start(s32[1,10,12]{2,0,1:T(1,128)} %param.14) | copy-start | bytes 1444
  5.5 6.8 %copy-start.3 = (s32[1,20,8]{1,2,0:T(8,128)S(1)}, s32[1,20,8]{1,2,0:T(8,128)}, u32[]{:S(2)}) copy-start(s32[1,20,8]{1,2,0:T(8,128)} %param.12) | copy-start | bytes 1924
  5.5 6.9 %copy-start.8 = (s32[1,10]{1,0:T(1,128)S(1)}, s32[1,10]{1,0:T(1,128)}, u32[]{:S(2)}) copy-start(s32[1,10]{1,0:T(1,128)} %param.10) | copy-start | bytes 124
  5.5 7.6 %copy-start.7 = (s32[1,20]{1,0:T(1,128)S(1)}, s32[1,20]{1,0:T(1,128)}, u32[]{:S(2)}) copy-start(s32[1,20]{1,0:T(1,128)} %param.13) | copy-start | bytes 244
  5.5 29.0 %collective-permute-start.5 = (bf16[80,128,128]{2,1,0:T(8,128)(2,1)}, bf16[80,128,128]{2,1,0:T(8,128)(2,1)}, u32[]{:S(2)}, u32[]{:S(2)}) collective-permute-start(bf16[80,128,128]{2,1,0:T(8,128)(2,1)} %bitcast.17), channel_id=1, source_target_pairs={{2,114},{3,115},{4,116},{5,117},{6,118},{7,119},{10,122},{11,123},... | collective-permute-start | bytes 7864328 | tf_op jit(solution)/shard_map/ppermute | solution.py:24
  7.8 16.3 %collective-permute-start.2 = (bf16[24,128,128]{2,1,0:T(8,128)(2,1)}, bf16[24,128,128]{2,1,0:T(8,128)(2,1)}, u32[]{:S(2)}, u32[]{:S(2)}) collective-permute-start(bf16[24,128,128]{2,1,0:T(8,128)(2,1)} %get-tuple-element.24), channel_id=1, source_target_pairs={{0,5},{8,13},{16,21},{24,29},{32,37},{40,45},{48,53},{56,61},{64,6... | collective-permute-start | bytes 2359304 | tf_op jit(solution)/shard_map/ppermute | solution.py:24
  9.4 14.8 %collective-permute-start.1 = (bf16[68,128,128]{2,1,0:T(8,128)(2,1)}, bf16[68,128,128]{2,1,0:T(8,128)(2,1)}, u32[]{:S(2)}, u32[]{:S(2)}) collective-permute-start(bf16[68,128,128]{2,1,0:T(8,128)(2,1)} %get-tuple-element.23), channel_id=1, source_target_pairs={{0,31},{8,23},{16,15},{24,7},{32,63},{40,55},{48,47},{56,39},{64,9... | collective-permute-start | bytes 6684680 | tf_op jit(solution)/shard_map/ppermute | solution.py:24
  13.7 50.4 %copy-start.9 = (s32[90]{0:T(128)S(1)}, s32[90]{0:T(128)}, u32[]{:S(2)}) copy-start(s32[90]{0:T(128)} %pad_add_fusion.1.first_meta) | copy-start | bytes 1084
  13.7 54.3 %copy-start.5 = (s32[180]{0:T(256)S(1)}, s32[180]{0:T(256)}, u32[]{:S(2)}) copy-start(s32[180]{0:T(256)} %pad_add_fusion.second_meta) | copy-start | bytes 2164
  24.1 10.4 %collective-permute-start.3 = (bf16[68,128,128]{2,1,0:T(8,128)(2,1)}, bf16[68,128,128]{2,1,0:T(8,128)(2,1)}, u32[]{:S(2)}, u32[]{:S(2)}) collective-permute-start(bf16[68,128,128]{2,1,0:T(8,128)(2,1)} %collective-permute-done), channel_id=1, source_target_pairs={{0,31},{8,23},{16,15},{24,7},{32,63},{40,55},{48,47},{56,39},{64,9... | collective-permute-start | bytes 6684680 | tf_op jit(solution)/shard_map/ppermute | solution.py:24
  26.1 6.3 %collective-permute-start.4 = (bf16[24,128,128]{2,1,0:T(8,128)(2,1)}, bf16[24,128,128]{2,1,0:T(8,128)(2,1)S(1)}, u32[]{:S(2)}, u32[]{:S(2)}) collective-permute-start(bf16[24,128,128]{2,1,0:T(8,128)(2,1)} %collective-permute-done.2), channel_id=1, source_target_pairs={{5,29},{13,21},{21,13},{29,5},{37,61},{45,53},{53,45},{61,37},{69,... | collective-permute-start | bytes 2359304 | tf_op jit(solution)/shard_map/ppermute | solution.py:24
  26.8 69.2 %collective-permute-start.9 = (bf16[80,128,128]{2,1,0:T(8,128)(2,1)}, bf16[80,128,128]{2,1,0:T(8,128)(2,1)}, u32[]{:S(2)}, u32[]{:S(2)}) collective-permute-start(bf16[80,128,128]{2,1,0:T(8,128)(2,1)} %bitcast.19), channel_id=1, source_target_pairs={{0,112},{1,113},{8,120},{9,121},{16,0},{17,1},{24,8},{25,9},{32,16... | collective-permute-start | bytes 7864328 | tf_op jit(solution)/shard_map/ppermute | solution.py:24
  32.5 63.6 %collective-permute-start.10 = (bf16[68,128,128]{2,1,0:T(8,128)(2,1)}, bf16[68,128,128]{2,1,0:T(8,128)(2,1)}, u32[]{:S(2)}, u32[]{:S(2)}) collective-permute-start(bf16[68,128,128]{2,1,0:T(8,128)(2,1)} %collective-permute-done.1), channel_id=1, source_target_pairs={{7,23},{15,31},{23,7},{31,15},{39,55},{47,63},{55,39},{63,47},{71,... | collective-permute-start | bytes 6684680 | tf_op jit(solution)/shard_map/ppermute | solution.py:24
  62.7 0.7 collective-permute-start.11
  63.4 32.9 %collective-permute-start.12 = (bf16[24,128,128]{2,1,0:T(8,128)(2,1)S(1)}, bf16[24,128,128]{2,1,0:T(8,128)(2,1)S(1)}, u32[]{:S(2)}, u32[]{:S(2)}) collective-permute-start(bf16[24,128,128]{2,1,0:T(8,128)(2,1)S(1)} %collective-permute-done.11), channel_id=1, source_target_pairs={{5,7},{13,15},{21,23},{29,31},{37,39},{45,47},{53,55},{61,63},{69,... | collective-permute-start | bytes 2359304 | tf_op jit(solution)/shard_map/ppermute | solution.py:24
  64.1 32.0 %collective-permute-start.7 = (s32[90]{0:T(128)S(1)}, s32[90]{0:T(128)S(1)}, u32[]{:S(2)}, u32[]{:S(2)}) collective-permute-start(s32[90]{0:T(128)S(1)} %copy-done.9), channel_id=1, source_target_pairs={{0,112},{1,113},{2,114},{3,115},{4,116},{5,117},{6,118},{7,119},{8... | collective-permute-start | bytes 1088 | tf_op jit(solution)/shard_map/ppermute | solution.py:24
  68.0 28.3 %collective-permute-start.8 = (s32[180]{0:T(256)S(1)}, s32[180]{0:T(256)S(1)}, u32[]{:S(2)}, u32[]{:S(2)}) collective-permute-start(s32[180]{0:T(256)S(1)} %copy-done.5), channel_id=1, source_target_pairs={{0,15},{1,0},{2,1},{3,2},{4,3},{5,4},{6,5},{7,6},{8,7},{9,8},{10,9... | collective-permute-start | bytes 2168 | tf_op jit(solution)/shard_map/ppermute | solution.py:24
  96.1 0.6 copy-start.6
  96.3 0.5 copy-start.4
  96.3 0.9 copy-start

commit v8 on v7

--- a/solution.py
+++ b/solution.py
@@ -82,10 +82,10 @@
 
 def first_stop_kernel(
     first_meta, second_meta, kept_columns, first, second,
-    total, blank, table, held, rows, sums, zeros, held_sem, row_sem, sum_sem, blank_sem,
+    total, blank, table, held, rows, zeros, held_sem, row_sem, blank_sem,
 ):
     i = pl.program_id(0)
-    kept = total.shape[0] // pl.num_programs(0)
+    kept = total.shape[1]
     slots = rows.shape[0] * kept // kept_columns.shape[0]
     part = zeros.shape[0]
     panel = held.at[pl.ds(0, second.shape[0])]
@@ -103,15 +103,12 @@
             pltpu.make_async_copy(zeros, blank.at[pl.ds(j * part, part)], blank_sem).start()
 
     def put(f, value):
-        l = i * kept + f
-        sums[l] = value
-        pltpu.make_async_copy(sums.at[l], total.at[l], sum_sem).start()
+        total[0, f] = value
 
     row_products(table, first_meta, kept_columns, i, slots, kept, rows, held, put)
 
     @pl.when(i == pl.num_programs(0) - 1)
     def _():
-        pltpu.make_async_copy(sums, total, sum_sem).wait()
         pltpu.make_async_copy(blank, blank, blank_sem).wait()
 
 
@@ -195,21 +192,22 @@
             num_scalar_prefetch=3,
             grid=(rows,),
             in_specs=[pl.BlockSpec(memory_space=pl.ANY)] * 2,
-            out_specs=[pl.BlockSpec(memory_space=pl.ANY)] * 2,
+            out_specs=[
+                pl.BlockSpec((1, kept, side, side), lambda i, *_: (i, 0, 0, 0)),
+                pl.BlockSpec(memory_space=pl.ANY),
+            ],
             scratch_shapes=[
                 pltpu.SMEM(((TABLE_ROWS + 1) * TABLE_ROWS,), jnp.int32),
                 pltpu.VMEM((second_total + 1, side, side), second.dtype),
                 pltpu.VMEM(first.shape, first.dtype),
-                pltpu.VMEM((rows * kept, side, side), jnp.float32),
                 pltpu.VMEM((part, side, side), second.dtype),
-                pltpu.SemaphoreType.DMA,
                 pltpu.SemaphoreType.DMA,
                 pltpu.SemaphoreType.DMA,
                 pltpu.SemaphoreType.DMA,
             ],
         ),
         out_shape=[
-            jax.ShapeDtypeStruct((rows * kept, side, side), jnp.float32),
+            jax.ShapeDtypeStruct((rows, kept, side, side), jnp.float32),
             jax.ShapeDtypeStruct((outgoing, side, side), second.dtype),
         ],
         compiler_params=pltpu.CompilerParams(vmem_limit_bytes=LARGE_VMEM_LIMIT),
@@ -375,7 +373,7 @@
     place = jnp.stack([spot == span - 1, spot < 2]).astype(jnp.int32)
     outgoing = last_stop(
         first_meta, second_meta, kept_columns, owner, place,
-        early, late, before, second_next, part_a, part_b, part_c, blank, devices,
+        early, late, before.reshape(-1, side, side), second_next, part_a, part_b, part_c, blank, devices,
     )
     arrived = lax.all_to_all(
         outgoing.reshape(devices, per_owner, side, side),

time: 228 us -> 218 us (0.956)
  starting transfers between devices: 54.3 us -> 39.7 us
  blocking collectives: 114 us -> 118 us
  Pallas kernels: 26.1 us -> 29.8 us
  waiting for transfers between devices: 28.3 us -> 25.5 us
    ppermute x13, starting transfers between devices: 54.3 us -> 39.7 us  [move(): return lax.ppermute(value, ('row', 'col'), pairs)]
    all_to_all x1, blocking collectives: 114 us -> 118 us  [on_device(): lax.all_to_all(outgoing.reshape(devices, per_owner, side, side), ('row',...]
    pallas_call x1, Pallas kernels: 10.4 us -> 14 us  [first_stop(): pl.pallas_call(first_stop_kernel, grid_spec=pltpu.PrefetchScalarGridSpec(...]
    ppermute x13, waiting for transfers between devices: 28.3 us -> 25.5 us  [move(): return lax.ppermute(value, ('row', 'col'), pairs)]
  transfers between devices with their start and end apart: 13 -> 13, of which waited for: 2 -> 2; matrix products, arithmetic and copies ran while one was open for 1% -> 1% of each run, Pallas kernels for 5% -> 6%
where the time goes in v8:
time: 218 us; the launch traced here: 217 us
  blocking collectives  118 us (54%)
  starting transfers between devices  39.7 us (18%)
  Pallas kernels  29.8 us (14%)
  waiting for transfers between devices  25.5 us (12%)
    all_to_all x1, blocking collectives, on_device(): lax.all_to_all(outgoing.reshape(devices, per_owner, side, side), ('row',...  118 us
    ppermute x13, starting transfers between devices, move(): return lax.ppermute(value, ('row', 'col'), pairs)  39.7 us
    ppermute x13, waiting for transfers between devices, move(): return lax.ppermute(value, ('row', 'col'), pairs)  25.5 us
    pallas_call x1, Pallas kernels, first_stop(): pl.pallas_call(first_stop_kernel, grid_spec=pltpu.PrefetchScalarGridSpec(...  14 us
    pallas_call x1, Pallas kernels, last_stop(): pl.pallas_call(last_stop_kernel, grid_spec=pltpu.PrefetchScalarGridSpec(n...  12.5 us
  transfers between devices with their start and end apart: 13, of which 2 were waited for; matrix products, arithmetic and copies ran while one was open for 1% of the time, Pallas kernels for 6%

profile of v8, /device:TPU:1, one launch (start us, length us, event | category | flops | bytes accessed | tf_op | source)
XLA Modules:
  0.0 217.4 jit_solution(8342499785426005699)
XLA Ops:
  0.0 3.3 %collective-permute-start.6 = (bf16[160,128,128]{2,1,0:T(8,128)(2,1)}, bf16[160,128,128]{2,1,0:T(8,128)(2,1)}, u32[]{:S(2)}, u32[]{:S(2)}) collective-permute-start(bf16[160,128,128]{2,1,0:T(8,128)(2,1)} %bitcast.12), channel_id=1, source_target_pairs={{1,0},{2,1},{3,2},{4,3},{5,4},{6,5},{7,6},{9,8},{10,9},{11,10},{12... | collective-permute-start | bytes 15728648 | tf_op jit(solution)/shard_map/ppermute | solution.py:24
  3.4 2.1 collective-permute-start
  5.5 2.3 %collective-permute-start.5 = (bf16[80,128,128]{2,1,0:T(8,128)(2,1)}, bf16[80,128,128]{2,1,0:T(8,128)(2,1)}, u32[]{:S(2)}, u32[]{:S(2)}) collective-permute-start(bf16[80,128,128]{2,1,0:T(8,128)(2,1)} %bitcast.19), channel_id=1, source_target_pairs={{2,114},{3,115},{4,116},{5,117},{6,118},{7,119},{10,122},{11,123},... | collective-permute-start | bytes 7864328 | tf_op jit(solution)/shard_map/ppermute | solution.py:24
  7.8 1.6 collective-permute-start.2
  9.4 2.0 collective-permute-start.1
  11.6 0.7 reshape_squeeze.19.kept_columns
  12.4 0.6 pad_add_fusion.1.first_meta
  13.1 0.6 pad_add_fusion.second_meta
  13.7 14.0 %shard_map.84 = (f32[10,12,128,128]{3,2,1,0:T(8,128)}, bf16[256,128,128]{2,1,0:T(8,128)(2,1)}) custom-call(s32[90]{0:T(128)} %pad_add_fusion.1.first_meta, s32[180]{0:T(256)} %pad_add_fusion.second_meta, s32[120]{0:T(128)} %reshape_squeeze.19.kept_columns, bf16[80,128,128]{2,1,0:T(8,128)(2,1)} %bitcast.20, bf16[160,128,128]{2,1,0:T(8,128)(2,1)} %bitcast.15), custom_call_target="tpu_custom_call" | custom-call | flops 805306368000 | bytes 31457280 | tf_op jit(solution)/shard_map/pallas_call | solution.py:189
  27.7 2.0 collective-permute-start.3
  29.7 0.7 collective-permute-start.4
  30.4 5.1 %collective-permute-start.9 = (bf16[80,128,128]{2,1,0:T(8,128)(2,1)}, bf16[80,128,128]{2,1,0:T(8,128)(2,1)}, u32[]{:S(2)}, u32[]{:S(2)}) collective-permute-start(bf16[80,128,128]{2,1,0:T(8,128)(2,1)} %bitcast.21), channel_id=1, source_target_pairs={{0,112},{1,113},{8,120},{9,121},{16,0},{17,1},{24,8},{25,9},{32,16... | collective-permute-start | bytes 7864328 | tf_op jit(solution)/shard_map/ppermute | solution.py:24
  35.5 2.1 collective-permute-start.10
  37.6 25.3 %collective-permute-done.6.second = bf16[160,128,128]{2,1,0:T(8,128)(2,1)} collective-permute-done((bf16[160,128,128]{2,1,0:T(8,128)(2,1)}, bf16[160,128,128]{2,1,0:T(8,128)(2,1)}, u32[]{:S(2)}, u32[]{:S(2)}) %collective-permute-start.6) | collective-permute-done | bytes 5242912 | tf_op jit(solution)/shard_map/ppermute | solution.py:24
  63.0 0.7 collective-permute-start.11
  63.7 0.7 collective-permute-start.12
  64.4 3.6 %collective-permute-start.7 = (s32[90]{0:T(128)S(1)}, s32[90]{0:T(128)S(1)}, u32[]{:S(2)}, u32[]{:S(2)}) collective-permute-start(s32[90]{0:T(128)S(1)} %copy-done.9), channel_id=1, source_target_pairs={{0,112},{1,113},{2,114},{3,115},{4,116},{5,117},{6,118},{7,119},{8... | collective-permute-start | bytes 1088 | tf_op jit(solution)/shard_map/ppermute | solution.py:24
  68.0 13.7 %collective-permute-start.8 = (s32[180]{0:T(256)S(1)}, s32[180]{0:T(256)S(1)}, u32[]{:S(2)}, u32[]{:S(2)}) collective-permute-start(s32[180]{0:T(256)S(1)} %copy-done.5), channel_id=1, source_target_pairs={{0,15},{1,0},{2,1},{3,2},{4,3},{5,4},{6,5},{7,6},{8,7},{9,8},{10,9... | collective-permute-start | bytes 2168 | tf_op jit(solution)/shard_map/ppermute | solution.py:24
  81.7 0.6 add_convert_fusion.place
  82.5 0.4 copy-done.6
  83.0 0.3 copy-done
  83.4 12.5 %shard_map.85 = bf16[256,128,128]{2,1,0:T(8,128)(2,1)} custom-call(s32[90]{0:T(128)} %copy-done.6, s32[180]{0:T(256)} %copy-done.4, s32[120]{0:T(128)} %reshape_squeeze.19.kept_columns, s32[120]{0:T(128)} %bitcast.17, s32[2]{0:T(128)} %add_convert_fusion.place, bf16[80,128,128]{2,1,0:T(8,128)(2,1)} %collective-permute-done.5.early, ...), custom_call_target="tpu_custom_call", output_to_operand_aliasing={{}: (12, {})} | custom-call | flops 1024 | bytes 1024 | tf_op jit(solution)/shard_map/pallas_call | solution.py:230
  95.9 118.2 %all_to_all.5.source = bf16[128,2,128,128]{3,2,1,0:T(8,128)(2,1)S(1)} all-to-all(bf16[128,2,128,128]{3,2,1,0:T(8,128)(2,1)} %bitcast.11), channel_id=1, replica_groups=mesh['row'=8,'col'=16] {'row','col'}, dimensions={0} | all-to-all | bytes 16777216 | tf_op jit(solution)/shard_map/all_to_all | solution.py:378
  214.1 3.3 %shard_map.86 = bf16[128,2,128,128]{3,2,1,0:T(8,128)(2,1)} custom-call(bf16[128,2,128,128]{3,2,1,0:T(8,128)(2,1)S(1)} %all_to_all.5.source), custom_call_target="tpu_custom_call" | custom-call | tf_op jit(solution)/shard_map/pallas_call | solution.py:306
  (37 shorter events, 0.8 us)
Async XLA Ops:
  0.0 63.0 %collective-permute-start.6 = (bf16[160,128,128]{2,1,0:T(8,128)(2,1)}, bf16[160,128,128]{2,1,0:T(8,128)(2,1)}, u32[]{:S(2)}, u32[]{:S(2)}) collective-permute-start(bf16[160,128,128]{2,1,0:T(8,128)(2,1)} %bitcast.12), channel_id=1, source_target_pairs={{1,0},{2,1},{3,2},{4,3},{5,4},{6,5},{7,6},{9,8},{10,9},{11,10},{12... | collective-permute-start | bytes 15728648 | tf_op jit(solution)/shard_map/ppermute | solution.py:24
  3.4 24.3 %collective-permute-start = (bf16[68,128,128]{2,1,0:T(8,128)(2,1)}, bf16[68,128,128]{2,1,0:T(8,128)(2,1)}, u32[]{:S(2)}, u32[]{:S(2)}) collective-permute-start(bf16[68,128,128]{2,1,0:T(8,128)(2,1)} %shard_map.82), channel_id=1, source_target_pairs={{0,16},{8,24},{16,0},{24,8},{32,48},{40,56},{48,32},{56,40},{64,80... | collective-permute-start | bytes 6684680 | tf_op jit(solution)/shard_map/ppermute | solution.py:24
  5.5 5.9 %copy-start.2 = (s32[1,10,8]{1,2,0:T(8,128)S(1)}, s32[1,10,8]{1,2,0:T(8,128)}, u32[]{:S(2)}) copy-start(s32[1,10,8]{1,2,0:T(8,128)} %param.9) | copy-start | bytes 964
  5.5 6.1 %copy-start.1 = (s32[1,10,12]{2,0,1:T(1,128)S(1)}, s32[1,10,12]{2,0,1:T(1,128)}, u32[]{:S(2)}) copy-start(s32[1,10,12]{2,0,1:T(1,128)} %param.14) | copy-start | bytes 1444
  5.5 6.8 %copy-start.3 = (s32[1,20,8]{1,2,0:T(8,128)S(1)}, s32[1,20,8]{1,2,0:T(8,128)}, u32[]{:S(2)}) copy-start(s32[1,20,8]{1,2,0:T(8,128)} %param.12) | copy-start | bytes 1924
  5.5 6.9 %copy-start.8 = (s32[1,10]{1,0:T(1,128)S(1)}, s32[1,10]{1,0:T(1,128)}, u32[]{:S(2)}) copy-start(s32[1,10]{1,0:T(1,128)} %param.10) | copy-start | bytes 124
  5.5 7.6 %copy-start.7 = (s32[1,20]{1,0:T(1,128)S(1)}, s32[1,20]{1,0:T(1,128)}, u32[]{:S(2)}) copy-start(s32[1,20]{1,0:T(1,128)} %param.13) | copy-start | bytes 244
  5.5 32.1 %collective-permute-start.5 = (bf16[80,128,128]{2,1,0:T(8,128)(2,1)}, bf16[80,128,128]{2,1,0:T(8,128)(2,1)}, u32[]{:S(2)}, u32[]{:S(2)}) collective-permute-start(bf16[80,128,128]{2,1,0:T(8,128)(2,1)} %bitcast.19), channel_id=1, source_target_pairs={{2,114},{3,115},{4,116},{5,117},{6,118},{7,119},{10,122},{11,123},... | collective-permute-start | bytes 7864328 | tf_op jit(solution)/shard_map/ppermute | solution.py:24
  7.8 19.9 %collective-permute-start.2 = (bf16[24,128,128]{2,1,0:T(8,128)(2,1)}, bf16[24,128,128]{2,1,0:T(8,128)(2,1)}, u32[]{:S(2)}, u32[]{:S(2)}) collective-permute-start(bf16[24,128,128]{2,1,0:T(8,128)(2,1)} %get-tuple-element.24), channel_id=1, source_target_pairs={{0,5},{8,13},{16,21},{24,29},{32,37},{40,45},{48,53},{56,61},{64,6... | collective-permute-start | bytes 2359304 | tf_op jit(solution)/shard_map/ppermute | solution.py:24
  9.4 18.4 %collective-permute-start.1 = (bf16[68,128,128]{2,1,0:T(8,128)(2,1)}, bf16[68,128,128]{2,1,0:T(8,128)(2,1)}, u32[]{:S(2)}, u32[]{:S(2)}) collective-permute-start(bf16[68,128,128]{2,1,0:T(8,128)(2,1)} %get-tuple-element.23), channel_id=1, source_target_pairs={{0,31},{8,23},{16,15},{24,7},{32,63},{40,55},{48,47},{56,39},{64,9... | collective-permute-start | bytes 6684680 | tf_op jit(solution)/shard_map/ppermute | solution.py:24
  13.7 50.7 %copy-start.9 = (s32[90]{0:T(128)S(1)}, s32[90]{0:T(128)}, u32[]{:S(2)}) copy-start(s32[90]{0:T(128)} %pad_add_fusion.1.first_meta) | copy-start | bytes 1084
  13.7 54.3 %copy-start.5 = (s32[180]{0:T(256)S(1)}, s32[180]{0:T(256)}, u32[]{:S(2)}) copy-start(s32[180]{0:T(256)} %pad_add_fusion.second_meta) | copy-start | bytes 2164
  27.7 9.9 %collective-permute-start.3 = (bf16[68,128,128]{2,1,0:T(8,128)(2,1)}, bf16[68,128,128]{2,1,0:T(8,128)(2,1)}, u32[]{:S(2)}, u32[]{:S(2)}) collective-permute-start(bf16[68,128,128]{2,1,0:T(8,128)(2,1)} %collective-permute-done), channel_id=1, source_target_pairs={{0,31},{8,23},{16,15},{24,7},{32,63},{40,55},{48,47},{56,39},{64,9... | collective-permute-start | bytes 6684680 | tf_op jit(solution)/shard_map/ppermute | solution.py:24
  29.7 5.8 %collective-permute-start.4 = (bf16[24,128,128]{2,1,0:T(8,128)(2,1)}, bf16[24,128,128]{2,1,0:T(8,128)(2,1)S(1)}, u32[]{:S(2)}, u32[]{:S(2)}) collective-permute-start(bf16[24,128,128]{2,1,0:T(8,128)(2,1)} %collective-permute-done.2), channel_id=1, source_target_pairs={{5,29},{13,21},{21,13},{29,5},{37,61},{45,53},{53,45},{61,37},{69,... | collective-permute-start | bytes 2359304 | tf_op jit(solution)/shard_map/ppermute | solution.py:24
  30.4 51.9 %collective-permute-start.9 = (bf16[80,128,128]{2,1,0:T(8,128)(2,1)}, bf16[80,128,128]{2,1,0:T(8,128)(2,1)}, u32[]{:S(2)}, u32[]{:S(2)}) collective-permute-start(bf16[80,128,128]{2,1,0:T(8,128)(2,1)} %bitcast.21), channel_id=1, source_target_pairs={{0,112},{1,113},{8,120},{9,121},{16,0},{17,1},{24,8},{25,9},{32,16... | collective-permute-start | bytes 7864328 | tf_op jit(solution)/shard_map/ppermute | solution.py:24
  35.5 46.8 %collective-permute-start.10 = (bf16[68,128,128]{2,1,0:T(8,128)(2,1)}, bf16[68,128,128]{2,1,0:T(8,128)(2,1)}, u32[]{:S(2)}, u32[]{:S(2)}) collective-permute-start(bf16[68,128,128]{2,1,0:T(8,128)(2,1)} %collective-permute-done.1), channel_id=1, source_target_pairs={{7,23},{15,31},{23,7},{31,15},{39,55},{47,63},{55,39},{63,47},{71,... | collective-permute-start | bytes 6684680 | tf_op jit(solution)/shard_map/ppermute | solution.py:24
  63.0 0.7 collective-permute-start.11
  63.7 18.8 %collective-permute-start.12 = (bf16[24,128,128]{2,1,0:T(8,128)(2,1)S(1)}, bf16[24,128,128]{2,1,0:T(8,128)(2,1)S(1)}, u32[]{:S(2)}, u32[]{:S(2)}) collective-permute-start(bf16[24,128,128]{2,1,0:T(8,128)(2,1)S(1)} %collective-permute-done.11), channel_id=1, source_target_pairs={{5,7},{13,15},{21,23},{29,31},{37,39},{45,47},{53,55},{61,63},{69,... | collective-permute-start | bytes 2359304 | tf_op jit(solution)/shard_map/ppermute | solution.py:24
  64.4 17.9 %collective-permute-start.7 = (s32[90]{0:T(128)S(1)}, s32[90]{0:T(128)S(1)}, u32[]{:S(2)}, u32[]{:S(2)}) collective-permute-start(s32[90]{0:T(128)S(1)} %copy-done.9), channel_id=1, source_target_pairs={{0,112},{1,113},{2,114},{3,115},{4,116},{5,117},{6,118},{7,119},{8... | collective-permute-start | bytes 1088 | tf_op jit(solution)/shard_map/ppermute | solution.py:24
  68.0 14.5 %collective-permute-start.8 = (s32[180]{0:T(256)S(1)}, s32[180]{0:T(256)S(1)}, u32[]{:S(2)}, u32[]{:S(2)}) collective-permute-start(s32[180]{0:T(256)S(1)} %copy-done.5), channel_id=1, source_target_pairs={{0,15},{1,0},{2,1},{3,2},{4,3},{5,4},{6,5},{7,6},{8,7},{9,8},{10,9... | collective-permute-start | bytes 2168 | tf_op jit(solution)/shard_map/ppermute | solution.py:24
  82.3 0.6 copy-start.6
  82.5 0.5 copy-start.4
  82.5 0.9 copy-start

commit v9 on v8

--- a/solution.py
+++ b/solution.py
@@ -11,6 +11,7 @@
 LARGE_VMEM_LIMIT = 62 * 1024 * 1024
 TABLE_ROWS = 20
 PIECE = 4
+AHEAD = 2
 
 
 def move(value, chosen):
@@ -126,6 +127,20 @@
     total = held.shape[0] - 1
     panel = held.at[pl.ds(0, total)]
 
+    def load_row(j):
+        row = pl.ds(j * slots, slots)
+
+        @pl.when(place[1] == 0)
+        def _():
+            load_pieces(early.at[row], rows.at[row], row_sem.at[j])
+
+        @pl.when(place[1] != 0)
+        def _():
+            load_pieces(late.at[row], rows.at[row], row_sem.at[j])
+
+        row = pl.ds(j * kept, kept)
+        load_pieces(before.at[row], sums.at[row], sum_sem.at[j])
+
     @pl.when(i == 0)
     def _():
         @pl.when(place[0] == 0)
@@ -139,17 +154,8 @@
                 load_pieces(part, held.at[pl.ds(at, part.shape[0])], held_sem)
                 at += part.shape[0]
 
-        @pl.when(place[1] == 0)
-        def _():
-            load_pieces(early, rows, row_sem)
-
-        @pl.when(place[1] != 0)
-        def _():
-            load_pieces(late, rows, row_sem)
-
-        for j in range(sum_sem.shape[0]):
-            row = pl.ds(j * kept, kept)
-            load_pieces(before.at[row], sums.at[row], sum_sem.at[j])
+        for j in range(AHEAD):
+            load_row(j)
 
         held[total] = jnp.zeros(held.shape[1:], held.dtype)
 
@@ -159,9 +165,14 @@
 
         lax.fori_loop(0, used.shape[0], clear, 0, unroll=16)
         fill_table(table, second_meta, slots, table.shape[0] // (TABLE_ROWS + 1))
-        pltpu.make_async_copy(rows, rows, row_sem).wait()
         pltpu.make_async_copy(panel, panel, held_sem).wait()
 
+    @pl.when(i + AHEAD < row_total)
+    def _():
+        load_row(i + AHEAD)
+
+    row = rows.at[pl.ds(i * slots, slots)]
+    pltpu.make_async_copy(row, row, row_sem.at[i]).wait()
     row = sums.at[pl.ds(i * kept, kept)]
     pltpu.make_async_copy(row, row, sum_sem.at[i]).wait()
 
@@ -242,7 +253,7 @@
                 pltpu.VMEM(before.shape, before.dtype),
                 pltpu.VMEM(before.shape, second.dtype),
                 pltpu.SemaphoreType.DMA,
-                pltpu.SemaphoreType.DMA,
+                pltpu.SemaphoreType.DMA((rows,)),
                 pltpu.SemaphoreType.DMA((rows,)),
                 pltpu.SemaphoreType.DMA,
             ],
@@ -322,7 +333,7 @@
     first = a_blocks[0].reshape(-1, side, side)
     second = b_blocks[0].reshape(-1, side, side)
     total = second.shape[0]
-    large = total * 17 // 40
+    large_a, large_b = total * 17 // 40, total * 7 // 16
     spot = lax.axis_index("col") % span
     crossing = (spot == 0).astype(jnp.int32)[None]
 
@@ -337,9 +348,9 @@
     def at(place, step):
         return lambda r, c: step(r, c) if c % span == place else None
 
-    (part_a,) = cut(crossing, second, 0, (large,))
+    (part_a,) = cut(crossing, second, 0, (large_a,))
     part_a = move(part_a, at(0, near))
-    part_b, part_c = cut(crossing, second, large, (large, total - 2 * large))
+    part_b, part_c = cut(crossing, second, large_a, (large_b, total - large_a - large_b))
     part_b = move(part_b, at(0, lambda r, c: far(r, c + last)))
     part_c = move(part_c, at(0, lambda r, c: (r, c + middle)))
     early = move(first, lambda r, c: (r - 1, c) if c % span > 1 else None)

time: 218 us -> 218 us (level)
  transfers between devices with their start and end apart: 13 -> 13, of which waited for: 2 -> 2; matrix products, arithmetic and copies ran while one was open for 1% -> 1% of each run, Pallas kernels for 6% -> 7%
where the time goes in v9:
time: 218 us; the launch traced here: 217 us
  blocking collectives  119 us (55%)
  starting transfers between devices  40.5 us (19%)
  Pallas kernels  28.2 us (13%)
  waiting for transfers between devices  25.4 us (12%)
    all_to_all x1, blocking collectives, on_device(): lax.all_to_all(outgoing.reshape(devices, per_owner, side, side), ('row',...  119 us
    ppermute x13, starting transfers between devices, move(): return lax.ppermute(value, ('row', 'col'), pairs)  40.5 us
    ppermute x13, waiting for transfers between devices, move(): return lax.ppermute(value, ('row', 'col'), pairs)  25.4 us
    pallas_call x1, Pallas kernels, first_stop(): pl.pallas_call(first_stop_kernel, grid_spec=pltpu.PrefetchScalarGridSpec(...  14.3 us
    pallas_call x1, Pallas kernels, last_stop(): pl.pallas_call(last_stop_kernel, grid_spec=pltpu.PrefetchScalarGridSpec(n...  10.5 us
  transfers between devices with their start and end apart: 13, of which 2 were waited for; matrix products, arithmetic and copies ran while one was open for 1% of the time, Pallas kernels for 7%

profile of v9, /device:TPU:1, one launch (start us, length us, event | category | flops | bytes accessed | tf_op | source)
XLA Modules:
  0.0 217.3 jit_solution(8385353434490429609)
XLA Ops:
  0.0 3.3 %collective-permute-start.6 = (bf16[160,128,128]{2,1,0:T(8,128)(2,1)}, bf16[160,128,128]{2,1,0:T(8,128)(2,1)}, u32[]{:S(2)}, u32[]{:S(2)}) collective-permute-start(bf16[160,128,128]{2,1,0:T(8,128)(2,1)} %bitcast.12), channel_id=1, source_target_pairs={{1,0},{2,1},{3,2},{4,3},{5,4},{6,5},{7,6},{9,8},{10,9},{11,10},{12... | collective-permute-start | bytes 15728648 | tf_op jit(solution)/shard_map/ppermute | solution.py:25
  3.4 2.1 collective-permute-start
  5.5 2.3 %collective-permute-start.5 = (bf16[80,128,128]{2,1,0:T(8,128)(2,1)}, bf16[80,128,128]{2,1,0:T(8,128)(2,1)}, u32[]{:S(2)}, u32[]{:S(2)}) collective-permute-start(bf16[80,128,128]{2,1,0:T(8,128)(2,1)} %bitcast.19), channel_id=1, source_target_pairs={{2,114},{3,115},{4,116},{5,117},{6,118},{7,119},{10,122},{11,123},... | collective-permute-start | bytes 7864328 | tf_op jit(solution)/shard_map/ppermute | solution.py:25
  7.8 1.5 collective-permute-start.2
  9.4 2.0 collective-permute-start.1
  11.6 0.6 reshape_squeeze.19.kept_columns
  12.4 0.6 pad_add_fusion.1.first_meta
  12.9 0.6 pad_add_fusion.second_meta
  13.5 14.3 %shard_map.84 = (f32[10,12,128,128]{3,2,1,0:T(8,128)}, bf16[256,128,128]{2,1,0:T(8,128)(2,1)}) custom-call(s32[90]{0:T(128)} %pad_add_fusion.1.first_meta, s32[180]{0:T(256)} %pad_add_fusion.second_meta, s32[120]{0:T(128)} %reshape_squeeze.19.kept_columns, bf16[80,128,128]{2,1,0:T(8,128)(2,1)} %bitcast.20, bf16[160,128,128]{2,1,0:T(8,128)(2,1)} %bitcast.15), custom_call_target="tpu_custom_call" | custom-call | flops 805306368000 | bytes 31457280 | tf_op jit(solution)/shard_map/pallas_call | solution.py:200
  27.9 2.0 collective-permute-start.3
  29.9 0.7 collective-permute-start.4
  30.6 5.1 %collective-permute-start.9 = (bf16[80,128,128]{2,1,0:T(8,128)(2,1)}, bf16[80,128,128]{2,1,0:T(8,128)(2,1)}, u32[]{:S(2)}, u32[]{:S(2)}) collective-permute-start(bf16[80,128,128]{2,1,0:T(8,128)(2,1)} %bitcast.21), channel_id=1, source_target_pairs={{0,112},{1,113},{8,120},{9,121},{16,0},{17,1},{24,8},{25,9},{32,16... | collective-permute-start | bytes 7864328 | tf_op jit(solution)/shard_map/ppermute | solution.py:25
  35.7 2.1 collective-permute-start.10
  37.8 25.1 %collective-permute-done.6.second = bf16[160,128,128]{2,1,0:T(8,128)(2,1)} collective-permute-done((bf16[160,128,128]{2,1,0:T(8,128)(2,1)}, bf16[160,128,128]{2,1,0:T(8,128)(2,1)}, u32[]{:S(2)}, u32[]{:S(2)}) %collective-permute-start.6) | collective-permute-done | bytes 5242912 | tf_op jit(solution)/shard_map/ppermute | solution.py:25
  63.0 0.7 collective-permute-start.11
  63.7 0.7 collective-permute-start.12
  64.4 3.6 %collective-permute-start.7 = (s32[90]{0:T(128)S(1)}, s32[90]{0:T(128)S(1)}, u32[]{:S(2)}, u32[]{:S(2)}) collective-permute-start(s32[90]{0:T(128)S(1)} %copy-done.9), channel_id=1, source_target_pairs={{0,112},{1,113},{2,114},{3,115},{4,116},{5,117},{6,118},{7,119},{8... | collective-permute-start | bytes 1088 | tf_op jit(solution)/shard_map/ppermute | solution.py:25
  68.0 14.3 %collective-permute-start.8 = (s32[180]{0:T(256)S(1)}, s32[180]{0:T(256)S(1)}, u32[]{:S(2)}, u32[]{:S(2)}) collective-permute-start(s32[180]{0:T(256)S(1)} %copy-done.5), channel_id=1, source_target_pairs={{0,15},{1,0},{2,1},{3,2},{4,3},{5,4},{6,5},{7,6},{8,7},{9,8},{10,9... | collective-permute-start | bytes 2168 | tf_op jit(solution)/shard_map/ppermute | solution.py:25
  82.3 0.6 add_convert_fusion.place
  83.1 0.3 copy-done.6
  83.6 0.4 copy-done
  84.0 10.5 %shard_map.85 = bf16[256,128,128]{2,1,0:T(8,128)(2,1)} custom-call(s32[90]{0:T(128)} %copy-done.6, s32[180]{0:T(256)} %copy-done.4, s32[120]{0:T(128)} %reshape_squeeze.19.kept_columns, s32[120]{0:T(128)} %bitcast.17, s32[2]{0:T(128)} %add_convert_fusion.place, bf16[80,128,128]{2,1,0:T(8,128)(2,1)} %collective-permute-done.5.early, ...), custom_call_target="tpu_custom_call", output_to_operand_aliasing={{}: (12, {})} | custom-call | flops 1024 | bytes 1024 | tf_op jit(solution)/shard_map/pallas_call | solution.py:241
  94.5 119.5 %all_to_all.5.source = bf16[128,2,128,128]{3,2,1,0:T(8,128)(2,1)S(1)} all-to-all(bf16[128,2,128,128]{3,2,1,0:T(8,128)(2,1)} %bitcast.11), channel_id=1, replica_groups=mesh['row'=8,'col'=16] {'row','col'}, dimensions={0} | all-to-all | bytes 16777216 | tf_op jit(solution)/shard_map/all_to_all | solution.py:389
  214.0 3.3 %shard_map.86 = bf16[128,2,128,128]{3,2,1,0:T(8,128)(2,1)} custom-call(bf16[128,2,128,128]{3,2,1,0:T(8,128)(2,1)S(1)} %all_to_all.5.source), custom_call_target="tpu_custom_call" | custom-call | tf_op jit(solution)/shard_map/pallas_call | solution.py:317
  (37 shorter events, 0.9 us)
Async XLA Ops:
  0.0 63.0 %collective-permute-start.6 = (bf16[160,128,128]{2,1,0:T(8,128)(2,1)}, bf16[160,128,128]{2,1,0:T(8,128)(2,1)}, u32[]{:S(2)}, u32[]{:S(2)}) collective-permute-start(bf16[160,128,128]{2,1,0:T(8,128)(2,1)} %bitcast.12), channel_id=1, source_target_pairs={{1,0},{2,1},{3,2},{4,3},{5,4},{6,5},{7,6},{9,8},{10,9},{11,10},{12... | collective-permute-start | bytes 15728648 | tf_op jit(solution)/shard_map/ppermute | solution.py:25
  3.4 24.5 %collective-permute-start = (bf16[68,128,128]{2,1,0:T(8,128)(2,1)}, bf16[68,128,128]{2,1,0:T(8,128)(2,1)}, u32[]{:S(2)}, u32[]{:S(2)}) collective-permute-start(bf16[68,128,128]{2,1,0:T(8,128)(2,1)} %shard_map.82), channel_id=1, source_target_pairs={{0,16},{8,24},{16,0},{24,8},{32,48},{40,56},{48,32},{56,40},{64,80... | collective-permute-start | bytes 6684680 | tf_op jit(solution)/shard_map/ppermute | solution.py:25
  5.5 5.9 %copy-start.2 = (s32[1,10,8]{1,2,0:T(8,128)S(1)}, s32[1,10,8]{1,2,0:T(8,128)}, u32[]{:S(2)}) copy-start(s32[1,10,8]{1,2,0:T(8,128)} %param.9) | copy-start | bytes 964
  5.5 6.1 %copy-start.1 = (s32[1,10,12]{2,0,1:T(1,128)S(1)}, s32[1,10,12]{2,0,1:T(1,128)}, u32[]{:S(2)}) copy-start(s32[1,10,12]{2,0,1:T(1,128)} %param.14) | copy-start | bytes 1444
  5.5 6.7 %copy-start.3 = (s32[1,20,8]{1,2,0:T(8,128)S(1)}, s32[1,20,8]{1,2,0:T(8,128)}, u32[]{:S(2)}) copy-start(s32[1,20,8]{1,2,0:T(8,128)} %param.12) | copy-start | bytes 1924
  5.5 6.9 %copy-start.8 = (s32[1,10]{1,0:T(1,128)S(1)}, s32[1,10]{1,0:T(1,128)}, u32[]{:S(2)}) copy-start(s32[1,10]{1,0:T(1,128)} %param.10) | copy-start | bytes 124
  5.5 7.4 %copy-start.7 = (s32[1,20]{1,0:T(1,128)S(1)}, s32[1,20]{1,0:T(1,128)}, u32[]{:S(2)}) copy-start(s32[1,20]{1,0:T(1,128)} %param.13) | copy-start | bytes 244
  5.5 32.3 %collective-permute-start.5 = (bf16[80,128,128]{2,1,0:T(8,128)(2,1)}, bf16[80,128,128]{2,1,0:T(8,128)(2,1)}, u32[]{:S(2)}, u32[]{:S(2)}) collective-permute-start(bf16[80,128,128]{2,1,0:T(8,128)(2,1)} %bitcast.19), channel_id=1, source_target_pairs={{2,114},{3,115},{4,116},{5,117},{6,118},{7,119},{10,122},{11,123},... | collective-permute-start | bytes 7864328 | tf_op jit(solution)/shard_map/ppermute | solution.py:25
  7.8 20.0 %collective-permute-start.2 = (bf16[22,128,128]{2,1,0:T(8,128)(2,1)}, bf16[22,128,128]{2,1,0:T(8,128)(2,1)}, u32[]{:S(2)}, u32[]{:S(2)}) collective-permute-start(bf16[22,128,128]{2,1,0:T(8,128)(2,1)} %get-tuple-element.24), channel_id=1, source_target_pairs={{0,5},{8,13},{16,21},{24,29},{32,37},{40,45},{48,53},{56,61},{64,6... | collective-permute-start | bytes 2162696 | tf_op jit(solution)/shard_map/ppermute | solution.py:25
  9.4 18.5 %collective-permute-start.1 = (bf16[70,128,128]{2,1,0:T(8,128)(2,1)}, bf16[70,128,128]{2,1,0:T(8,128)(2,1)}, u32[]{:S(2)}, u32[]{:S(2)}) collective-permute-start(bf16[70,128,128]{2,1,0:T(8,128)(2,1)} %get-tuple-element.23), channel_id=1, source_target_pairs={{0,31},{8,23},{16,15},{24,7},{32,63},{40,55},{48,47},{56,39},{64,9... | collective-permute-start | bytes 6881288 | tf_op jit(solution)/shard_map/ppermute | solution.py:25
  13.5 50.9 %copy-start.9 = (s32[90]{0:T(128)S(1)}, s32[90]{0:T(128)}, u32[]{:S(2)}) copy-start(s32[90]{0:T(128)} %pad_add_fusion.1.first_meta) | copy-start | bytes 1084
  13.5 54.4 %copy-start.5 = (s32[180]{0:T(256)S(1)}, s32[180]{0:T(256)}, u32[]{:S(2)}) copy-start(s32[180]{0:T(256)} %pad_add_fusion.second_meta) | copy-start | bytes 2164
  27.9 10.0 %collective-permute-start.3 = (bf16[68,128,128]{2,1,0:T(8,128)(2,1)}, bf16[68,128,128]{2,1,0:T(8,128)(2,1)}, u32[]{:S(2)}, u32[]{:S(2)}) collective-permute-start(bf16[68,128,128]{2,1,0:T(8,128)(2,1)} %collective-permute-done), channel_id=1, source_target_pairs={{0,31},{8,23},{16,15},{24,7},{32,63},{40,55},{48,47},{56,39},{64,9... | collective-permute-start | bytes 6684680 | tf_op jit(solution)/shard_map/ppermute | solution.py:25
  29.9 5.8 %collective-permute-start.4 = (bf16[22,128,128]{2,1,0:T(8,128)(2,1)}, bf16[22,128,128]{2,1,0:T(8,128)(2,1)S(1)}, u32[]{:S(2)}, u32[]{:S(2)}) collective-permute-start(bf16[22,128,128]{2,1,0:T(8,128)(2,1)} %collective-permute-done.2), channel_id=1, source_target_pairs={{5,29},{13,21},{21,13},{29,5},{37,61},{45,53},{53,45},{61,37},{69,... | collective-permute-start | bytes 2162696 | tf_op jit(solution)/shard_map/ppermute | solution.py:25
  30.6 52.3 %collective-permute-start.9 = (bf16[80,128,128]{2,1,0:T(8,128)(2,1)}, bf16[80,128,128]{2,1,0:T(8,128)(2,1)}, u32[]{:S(2)}, u32[]{:S(2)}) collective-permute-start(bf16[80,128,128]{2,1,0:T(8,128)(2,1)} %bitcast.21), channel_id=1, source_target_pairs={{0,112},{1,113},{8,120},{9,121},{16,0},{17,1},{24,8},{25,9},{32,16... | collective-permute-start | bytes 7864328 | tf_op jit(solution)/shard_map/ppermute | solution.py:25
  35.7 47.4 %collective-permute-start.10 = (bf16[70,128,128]{2,1,0:T(8,128)(2,1)}, bf16[70,128,128]{2,1,0:T(8,128)(2,1)}, u32[]{:S(2)}, u32[]{:S(2)}) collective-permute-start(bf16[70,128,128]{2,1,0:T(8,128)(2,1)} %collective-permute-done.1), channel_id=1, source_target_pairs={{7,23},{15,31},{23,7},{31,15},{39,55},{47,63},{55,39},{63,47},{71,... | collective-permute-start | bytes 6881288 | tf_op jit(solution)/shard_map/ppermute | solution.py:25
  63.0 0.7 collective-permute-start.11
  63.7 19.4 %collective-permute-start.12 = (bf16[22,128,128]{2,1,0:T(8,128)(2,1)S(1)}, bf16[22,128,128]{2,1,0:T(8,128)(2,1)S(1)}, u32[]{:S(2)}, u32[]{:S(2)}) collective-permute-start(bf16[22,128,128]{2,1,0:T(8,128)(2,1)S(1)} %collective-permute-done.11), channel_id=1, source_target_pairs={{5,7},{13,15},{21,23},{29,31},{37,39},{45,47},{53,55},{61,63},{69,... | collective-permute-start | bytes 2162696 | tf_op jit(solution)/shard_map/ppermute | solution.py:25
  64.4 18.5 %collective-permute-start.7 = (s32[90]{0:T(128)S(1)}, s32[90]{0:T(128)S(1)}, u32[]{:S(2)}, u32[]{:S(2)}) collective-permute-start(s32[90]{0:T(128)S(1)} %copy-done.9), channel_id=1, source_target_pairs={{0,112},{1,113},{2,114},{3,115},{4,116},{5,117},{6,118},{7,119},{8... | collective-permute-start | bytes 1088 | tf_op jit(solution)/shard_map/ppermute | solution.py:25
  68.0 15.1 %collective-permute-start.8 = (s32[180]{0:T(256)S(1)}, s32[180]{0:T(256)S(1)}, u32[]{:S(2)}, u32[]{:S(2)}) collective-permute-start(s32[180]{0:T(256)S(1)} %copy-done.5), channel_id=1, source_target_pairs={{0,15},{1,0},{2,1},{3,2},{4,3},{5,4},{6,5},{7,6},{8,7},{9,8},{10,9... | collective-permute-start | bytes 2168 | tf_op jit(solution)/shard_map/ppermute | solution.py:25
  82.9 0.6 copy-start.6
  83.1 0.5 copy-start.4
  83.1 0.9 copy-start

commit v10 on v9

--- a/solution.py
+++ b/solution.py
@@ -364,8 +364,8 @@
         own_first_meta, own_second_meta, kept_columns, first, second, devices * per_owner
     )
 
-    part_a, part_b, part_c, first, before, blank = lax.optimization_barrier(
-        (part_a, part_b, part_c, first, before, blank)
+    part_a, part_c, first, before, blank = lax.optimization_barrier(
+        (part_a, part_c, first, before, blank)
     )
     late = move(first, lambda r, c: (r - 1, c) if c % span < 2 else None)
     part_a = move(part_a, at(0, lambda r, c: far(r, c + last)))

time: 218 us -> 218 us (level)
  starting transfers between devices: 40.5 us -> 33.5 us
  blocking collectives: 119 us -> 125 us
    ppermute x13, starting transfers between devices: 40.5 us -> 33.5 us  [move(): return lax.ppermute(value, ('row', 'col'), pairs)]
    all_to_all x1, blocking collectives: 119 us -> 125 us  [on_device(): lax.all_to_all(outgoing.reshape(devices, per_owner, side, side), ('row',...]
  transfers between devices with their start and end apart: 13 -> 13, of which waited for: 2 -> 3; matrix products, arithmetic and copies ran while one was open for 1% -> 1% of each run, Pallas kernels for 7% -> 6%
where the time goes in v10:
time: 218 us; the launch traced here: 217 us
  blocking collectives  125 us (57%)
  starting transfers between devices  33.5 us (15%)
  Pallas kernels  27.9 us (13%)
  waiting for transfers between devices  27.1 us (12%)
    all_to_all x1, blocking collectives, on_device(): lax.all_to_all(outgoing.reshape(devices, per_owner, side, side), ('row',...  125 us
    ppermute x13, starting transfers between devices, move(): return lax.ppermute(value, ('row', 'col'), pairs)  33.5 us
    ppermute x13, waiting for transfers between devices, move(): return lax.ppermute(value, ('row', 'col'), pairs)  27.1 us
    pallas_call x1, Pallas kernels, first_stop(): pl.pallas_call(first_stop_kernel, grid_spec=pltpu.PrefetchScalarGridSpec(...  14 us
    pallas_call x1, Pallas kernels, last_stop(): pl.pallas_call(last_stop_kernel, grid_spec=pltpu.PrefetchScalarGridSpec(n...  10.5 us
  transfers between devices with their start and end apart: 13, of which 3 were waited for; matrix products, arithmetic and copies ran while one was open for 1% of the time, Pallas kernels for 6%

profile of v10, /device:TPU:1, one launch (start us, length us, event | category | flops | bytes accessed | tf_op | source)
XLA Modules:
  0.0 217.0 jit_solution(9886712120278735190)
XLA Ops:
  0.0 3.3 %collective-permute-start.6 = (bf16[160,128,128]{2,1,0:T(8,128)(2,1)}, bf16[160,128,128]{2,1,0:T(8,128)(2,1)}, u32[]{:S(2)}, u32[]{:S(2)}) collective-permute-start(bf16[160,128,128]{2,1,0:T(8,128)(2,1)} %bitcast.12), channel_id=1, source_target_pairs={{1,0},{2,1},{3,2},{4,3},{5,4},{6,5},{7,6},{9,8},{10,9},{11,10},{12... | collective-permute-start | bytes 15728648 | tf_op jit(solution)/shard_map/ppermute | solution.py:25
  3.4 2.1 collective-permute-start
  5.5 2.3 %collective-permute-start.5 = (bf16[80,128,128]{2,1,0:T(8,128)(2,1)}, bf16[80,128,128]{2,1,0:T(8,128)(2,1)}, u32[]{:S(2)}, u32[]{:S(2)}) collective-permute-start(bf16[80,128,128]{2,1,0:T(8,128)(2,1)} %bitcast.19), channel_id=1, source_target_pairs={{2,114},{3,115},{4,116},{5,117},{6,118},{7,119},{10,122},{11,123},... | collective-permute-start | bytes 7864328 | tf_op jit(solution)/shard_map/ppermute | solution.py:25
  7.8 1.5 collective-permute-start.1
  9.4 2.0 collective-permute-start.3
  11.6 0.7 reshape_squeeze.19.kept_columns
  12.4 0.7 pad_add_fusion.1.first_meta
  13.1 0.6 pad_add_fusion.second_meta
  13.7 14.0 %shard_map.84 = (f32[10,12,128,128]{3,2,1,0:T(8,128)}, bf16[256,128,128]{2,1,0:T(8,128)(2,1)}) custom-call(s32[90]{0:T(128)} %pad_add_fusion.1.first_meta, s32[180]{0:T(256)} %pad_add_fusion.second_meta, s32[120]{0:T(128)} %reshape_squeeze.19.kept_columns, bf16[80,128,128]{2,1,0:T(8,128)(2,1)} %bitcast.20, bf16[160,128,128]{2,1,0:T(8,128)(2,1)} %bitcast.15), custom_call_target="tpu_custom_call" | custom-call | flops 805306368000 | bytes 31457280 | tf_op jit(solution)/shard_map/pallas_call | solution.py:200
  27.7 2.1 collective-permute-start.2
  29.8 0.7 collective-permute-start.4
  30.5 5.4 %collective-permute-start.9 = (bf16[80,128,128]{2,1,0:T(8,128)(2,1)}, bf16[80,128,128]{2,1,0:T(8,128)(2,1)}, u32[]{:S(2)}, u32[]{:S(2)}) collective-permute-start(bf16[80,128,128]{2,1,0:T(8,128)(2,1)} %bitcast.21), channel_id=1, source_target_pairs={{0,112},{1,113},{8,120},{9,121},{16,0},{17,1},{24,8},{25,9},{32,16... | collective-permute-start | bytes 7864328 | tf_op jit(solution)/shard_map/ppermute | solution.py:25
  35.9 2.1 collective-permute-start.10
  38.0 24.9 %collective-permute-done.6.second = bf16[160,128,128]{2,1,0:T(8,128)(2,1)} collective-permute-done((bf16[160,128,128]{2,1,0:T(8,128)(2,1)}, bf16[160,128,128]{2,1,0:T(8,128)(2,1)}, u32[]{:S(2)}, u32[]{:S(2)}) %collective-permute-start.6) | collective-permute-done | bytes 5242912 | tf_op jit(solution)/shard_map/ppermute | solution.py:25
  63.0 0.7 collective-permute-start.11
  63.7 0.7 collective-permute-start.12
  64.4 3.6 %collective-permute-start.7 = (s32[90]{0:T(128)S(1)}, s32[90]{0:T(128)S(1)}, u32[]{:S(2)}, u32[]{:S(2)}) collective-permute-start(s32[90]{0:T(128)S(1)} %copy-done.9), channel_id=1, source_target_pairs={{0,112},{1,113},{2,114},{3,115},{4,116},{5,117},{6,118},{7,119},{8... | collective-permute-start | bytes 1088 | tf_op jit(solution)/shard_map/ppermute | solution.py:25
  68.0 7.1 %collective-permute-start.8 = (s32[180]{0:T(256)S(1)}, s32[180]{0:T(256)S(1)}, u32[]{:S(2)}, u32[]{:S(2)}) collective-permute-start(s32[180]{0:T(256)S(1)} %copy-done.5), channel_id=1, source_target_pairs={{0,15},{1,0},{2,1},{3,2},{4,3},{5,4},{6,5},{7,6},{8,7},{9,8},{10,9... | collective-permute-start | bytes 2168 | tf_op jit(solution)/shard_map/ppermute | solution.py:25
  75.0 0.7 add_convert_fusion.place
  75.7 1.3 collective-permute-done.9.late
  77.0 0.7 collective-permute-done.8.second_meta
  78.7 10.5 %shard_map.85 = bf16[256,128,128]{2,1,0:T(8,128)(2,1)} custom-call(s32[90]{0:T(128)} %copy-done.6, s32[180]{0:T(256)} %copy-done.4, s32[120]{0:T(128)} %reshape_squeeze.19.kept_columns, s32[120]{0:T(128)} %bitcast.17, s32[2]{0:T(128)} %add_convert_fusion.place, bf16[80,128,128]{2,1,0:T(8,128)(2,1)} %collective-permute-done.5.early, ...), custom_call_target="tpu_custom_call", output_to_operand_aliasing={{}: (12, {})} | custom-call | flops 1024 | bytes 1024 | tf_op jit(solution)/shard_map/pallas_call | solution.py:241
  89.2 124.5 %all_to_all.5.source = bf16[128,2,128,128]{3,2,1,0:T(8,128)(2,1)S(1)} all-to-all(bf16[128,2,128,128]{3,2,1,0:T(8,128)(2,1)} %bitcast.11), channel_id=1, replica_groups=mesh['row'=8,'col'=16] {'row','col'}, dimensions={0} | all-to-all | bytes 16777216 | tf_op jit(solution)/shard_map/all_to_all | solution.py:389
  213.7 3.3 %shard_map.86 = bf16[128,2,128,128]{3,2,1,0:T(8,128)(2,1)} custom-call(bf16[128,2,128,128]{3,2,1,0:T(8,128)(2,1)S(1)} %all_to_all.5.source), custom_call_target="tpu_custom_call" | custom-call | tf_op jit(solution)/shard_map/pallas_call | solution.py:317
  (37 shorter events, 1.3 us)
Async XLA Ops:
  0.0 63.0 %collective-permute-start.6 = (bf16[160,128,128]{2,1,0:T(8,128)(2,1)}, bf16[160,128,128]{2,1,0:T(8,128)(2,1)}, u32[]{:S(2)}, u32[]{:S(2)}) collective-permute-start(bf16[160,128,128]{2,1,0:T(8,128)(2,1)} %bitcast.12), channel_id=1, source_target_pairs={{1,0},{2,1},{3,2},{4,3},{5,4},{6,5},{7,6},{9,8},{10,9},{11,10},{12... | collective-permute-start | bytes 15728648 | tf_op jit(solution)/shard_map/ppermute | solution.py:25
  3.4 24.4 %collective-permute-start = (bf16[68,128,128]{2,1,0:T(8,128)(2,1)}, bf16[68,128,128]{2,1,0:T(8,128)(2,1)}, u32[]{:S(2)}, u32[]{:S(2)}) collective-permute-start(bf16[68,128,128]{2,1,0:T(8,128)(2,1)} %shard_map.82), channel_id=1, source_target_pairs={{0,16},{8,24},{16,0},{24,8},{32,48},{40,56},{48,32},{56,40},{64,80... | collective-permute-start | bytes 6684680 | tf_op jit(solution)/shard_map/ppermute | solution.py:25
  5.5 5.9 %copy-start.2 = (s32[1,10,8]{1,2,0:T(8,128)S(1)}, s32[1,10,8]{1,2,0:T(8,128)}, u32[]{:S(2)}) copy-start(s32[1,10,8]{1,2,0:T(8,128)} %param.9) | copy-start | bytes 964
  5.5 6.1 %copy-start.1 = (s32[1,10,12]{2,0,1:T(1,128)S(1)}, s32[1,10,12]{2,0,1:T(1,128)}, u32[]{:S(2)}) copy-start(s32[1,10,12]{2,0,1:T(1,128)} %param.14) | copy-start | bytes 1444
  5.5 6.7 %copy-start.3 = (s32[1,20,8]{1,2,0:T(8,128)S(1)}, s32[1,20,8]{1,2,0:T(8,128)}, u32[]{:S(2)}) copy-start(s32[1,20,8]{1,2,0:T(8,128)} %param.12) | copy-start | bytes 1924
  5.5 6.9 %copy-start.8 = (s32[1,10]{1,0:T(1,128)S(1)}, s32[1,10]{1,0:T(1,128)}, u32[]{:S(2)}) copy-start(s32[1,10]{1,0:T(1,128)} %param.10) | copy-start | bytes 124
  5.5 7.6 %copy-start.7 = (s32[1,20]{1,0:T(1,128)S(1)}, s32[1,20]{1,0:T(1,128)}, u32[]{:S(2)}) copy-start(s32[1,20]{1,0:T(1,128)} %param.13) | copy-start | bytes 244
  5.5 32.5 %collective-permute-start.5 = (bf16[80,128,128]{2,1,0:T(8,128)(2,1)}, bf16[80,128,128]{2,1,0:T(8,128)(2,1)}, u32[]{:S(2)}, u32[]{:S(2)}) collective-permute-start(bf16[80,128,128]{2,1,0:T(8,128)(2,1)} %bitcast.19), channel_id=1, source_target_pairs={{2,114},{3,115},{4,116},{5,117},{6,118},{7,119},{10,122},{11,123},... | collective-permute-start | bytes 7864328 | tf_op jit(solution)/shard_map/ppermute | solution.py:25
  7.8 19.9 %collective-permute-start.1 = (bf16[22,128,128]{2,1,0:T(8,128)(2,1)}, bf16[22,128,128]{2,1,0:T(8,128)(2,1)}, u32[]{:S(2)}, u32[]{:S(2)}) collective-permute-start(bf16[22,128,128]{2,1,0:T(8,128)(2,1)} %get-tuple-element.22), channel_id=1, source_target_pairs={{0,5},{8,13},{16,21},{24,29},{32,37},{40,45},{48,53},{56,61},{64,6... | collective-permute-start | bytes 2162696 | tf_op jit(solution)/shard_map/ppermute | solution.py:25
  9.4 21.2 %collective-permute-start.3 = (bf16[70,128,128]{2,1,0:T(8,128)(2,1)}, bf16[70,128,128]{2,1,0:T(8,128)(2,1)}, u32[]{:S(2)}, u32[]{:S(2)}) collective-permute-start(bf16[70,128,128]{2,1,0:T(8,128)(2,1)} %get-tuple-element.26), channel_id=1, source_target_pairs={{0,31},{8,23},{16,15},{24,7},{32,63},{40,55},{48,47},{56,39},{64,9... | collective-permute-start | bytes 6881288 | tf_op jit(solution)/shard_map/ppermute | solution.py:25
  13.7 50.7 %copy-start.9 = (s32[90]{0:T(128)S(1)}, s32[90]{0:T(128)}, u32[]{:S(2)}) copy-start(s32[90]{0:T(128)} %pad_add_fusion.1.first_meta) | copy-start | bytes 1084
  13.7 54.3 %copy-start.5 = (s32[180]{0:T(256)S(1)}, s32[180]{0:T(256)}, u32[]{:S(2)}) copy-start(s32[180]{0:T(256)} %pad_add_fusion.second_meta) | copy-start | bytes 2164
  27.7 10.3 %collective-permute-start.2 = (bf16[68,128,128]{2,1,0:T(8,128)(2,1)}, bf16[68,128,128]{2,1,0:T(8,128)(2,1)}, u32[]{:S(2)}, u32[]{:S(2)}) collective-permute-start(bf16[68,128,128]{2,1,0:T(8,128)(2,1)} %collective-permute-done), channel_id=1, source_target_pairs={{0,31},{8,23},{16,15},{24,7},{32,63},{40,55},{48,47},{56,39},{64,9... | collective-permute-start | bytes 6684680 | tf_op jit(solution)/shard_map/ppermute | solution.py:25
  29.8 6.1 %collective-permute-start.4 = (bf16[22,128,128]{2,1,0:T(8,128)(2,1)}, bf16[22,128,128]{2,1,0:T(8,128)(2,1)S(1)}, u32[]{:S(2)}, u32[]{:S(2)}) collective-permute-start(bf16[22,128,128]{2,1,0:T(8,128)(2,1)} %collective-permute-done.1), channel_id=1, source_target_pairs={{5,29},{13,21},{21,13},{29,5},{37,61},{45,53},{53,45},{61,37},{69,... | collective-permute-start | bytes 2162696 | tf_op jit(solution)/shard_map/ppermute | solution.py:25
  30.5 46.5 %collective-permute-start.9 = (bf16[80,128,128]{2,1,0:T(8,128)(2,1)}, bf16[80,128,128]{2,1,0:T(8,128)(2,1)}, u32[]{:S(2)}, u32[]{:S(2)}) collective-permute-start(bf16[80,128,128]{2,1,0:T(8,128)(2,1)} %bitcast.21), channel_id=1, source_target_pairs={{0,112},{1,113},{8,120},{9,121},{16,0},{17,1},{24,8},{25,9},{32,16... | collective-permute-start | bytes 7864328 | tf_op jit(solution)/shard_map/ppermute | solution.py:25
  35.9 41.1 %collective-permute-start.10 = (bf16[70,128,128]{2,1,0:T(8,128)(2,1)}, bf16[70,128,128]{2,1,0:T(8,128)(2,1)}, u32[]{:S(2)}, u32[]{:S(2)}) collective-permute-start(bf16[70,128,128]{2,1,0:T(8,128)(2,1)} %collective-permute-done.3), channel_id=1, source_target_pairs={{7,23},{15,31},{23,7},{31,15},{39,55},{47,63},{55,39},{63,47},{71,... | collective-permute-start | bytes 6881288 | tf_op jit(solution)/shard_map/ppermute | solution.py:25
  63.0 0.7 collective-permute-start.11
  63.7 14.1 %collective-permute-start.12 = (bf16[22,128,128]{2,1,0:T(8,128)(2,1)S(1)}, bf16[22,128,128]{2,1,0:T(8,128)(2,1)S(1)}, u32[]{:S(2)}, u32[]{:S(2)}) collective-permute-start(bf16[22,128,128]{2,1,0:T(8,128)(2,1)S(1)} %collective-permute-done.11), channel_id=1, source_target_pairs={{5,7},{13,15},{21,23},{29,31},{37,39},{45,47},{53,55},{61,63},{69,... | collective-permute-start | bytes 2162696 | tf_op jit(solution)/shard_map/ppermute | solution.py:25
  64.4 12.6 %collective-permute-start.7 = (s32[90]{0:T(128)S(1)}, s32[90]{0:T(128)S(1)}, u32[]{:S(2)}, u32[]{:S(2)}) collective-permute-start(s32[90]{0:T(128)S(1)} %copy-done.9), channel_id=1, source_target_pairs={{0,112},{1,113},{2,114},{3,115},{4,116},{5,117},{6,118},{7,119},{8... | collective-permute-start | bytes 1088 | tf_op jit(solution)/shard_map/ppermute | solution.py:25
  68.0 9.8 %collective-permute-start.8 = (s32[180]{0:T(256)S(1)}, s32[180]{0:T(256)S(1)}, u32[]{:S(2)}, u32[]{:S(2)}) collective-permute-start(s32[180]{0:T(256)S(1)} %copy-done.5), channel_id=1, source_target_pairs={{0,15},{1,0},{2,1},{3,2},{4,3},{5,4},{6,5},{7,6},{8,7},{9,8},{10,9... | collective-permute-start | bytes 2168 | tf_op jit(solution)/shard_map/ppermute | solution.py:25
  77.0 0.8 copy-start.6
  77.8 0.6 copy-start.4
  77.8 0.9 copy-start

commit v11 on v10

--- a/solution.py
+++ b/solution.py
@@ -83,10 +83,10 @@
 
 def first_stop_kernel(
     first_meta, second_meta, kept_columns, first, second,
-    total, blank, table, held, rows, zeros, held_sem, row_sem, blank_sem,
+    total, blank, table, held, rows, sums, zeros, held_sem, row_sem, sum_sem, blank_sem,
 ):
     i = pl.program_id(0)
-    kept = total.shape[1]
+    kept = total.shape[0] // pl.num_programs(0)
     slots = rows.shape[0] * kept // kept_columns.shape[0]
     part = zeros.shape[0]
     panel = held.at[pl.ds(0, second.shape[0])]
@@ -104,12 +104,15 @@
             pltpu.make_async_copy(zeros, blank.at[pl.ds(j * part, part)], blank_sem).start()
 
     def put(f, value):
-        total[0, f] = value
+        l = i * kept + f
+        sums[l] = value
+        pltpu.make_async_copy(sums.at[l], total.at[l], sum_sem).start()
 
     row_products(table, first_meta, kept_columns, i, slots, kept, rows, held, put)
 
     @pl.when(i == pl.num_programs(0) - 1)
     def _():
+        pltpu.make_async_copy(sums, total, sum_sem).wait()
         pltpu.make_async_copy(blank, blank, blank_sem).wait()
 
 
@@ -203,22 +206,21 @@
             num_scalar_prefetch=3,
             grid=(rows,),
             in_specs=[pl.BlockSpec(memory_space=pl.ANY)] * 2,
-            out_specs=[
-                pl.BlockSpec((1, kept, side, side), lambda i, *_: (i, 0, 0, 0)),
-                pl.BlockSpec(memory_space=pl.ANY),
-            ],
+            out_specs=[pl.BlockSpec(memory_space=pl.ANY)] * 2,
             scratch_shapes=[
                 pltpu.SMEM(((TABLE_ROWS + 1) * TABLE_ROWS,), jnp.int32),
                 pltpu.VMEM((second_total + 1, side, side), second.dtype),
                 pltpu.VMEM(first.shape, first.dtype),
+                pltpu.VMEM((rows * kept, side, side), jnp.float32),
                 pltpu.VMEM((part, side, side), second.dtype),
+                pltpu.SemaphoreType.DMA,
                 pltpu.SemaphoreType.DMA,
                 pltpu.SemaphoreType.DMA,
                 pltpu.SemaphoreType.DMA,
             ],
         ),
         out_shape=[
-            jax.ShapeDtypeStruct((rows, kept, side, side), jnp.float32),
+            jax.ShapeDtypeStruct((rows * kept, side, side), jnp.float32),
             jax.ShapeDtypeStruct((outgoing, side, side), second.dtype),
         ],
         compiler_params=pltpu.CompilerParams(vmem_limit_bytes=LARGE_VMEM_LIMIT),
@@ -333,7 +335,7 @@
     first = a_blocks[0].reshape(-1, side, side)
     second = b_blocks[0].reshape(-1, side, side)
     total = second.shape[0]
-    large_a, large_b = total * 17 // 40, total * 7 // 16
+    large_a, large_b = total * 3 // 8, total * 37 // 80
     spot = lax.axis_index("col") % span
     crossing = (spot == 0).astype(jnp.int32)[None]
 
@@ -348,13 +350,14 @@
     def at(place, step):
         return lambda r, c: step(r, c) if c % span == place else None
 
-    (part_a,) = cut(crossing, second, 0, (large_a,))
-    part_a = move(part_a, at(0, near))
+    (cut_first,) = cut(crossing, second, 0, (large_a,))
+    part_a = move(cut_first, at(0, near))
     part_b, part_c = cut(crossing, second, large_a, (large_b, total - large_a - large_b))
     part_b = move(part_b, at(0, lambda r, c: far(r, c + last)))
     part_c = move(part_c, at(0, lambda r, c: (r, c + middle)))
     early = move(first, lambda r, c: (r - 1, c) if c % span > 1 else None)
-    second_next = move(second, lambda r, c: (r, c - 1) if c % span else None)
+    _, second_sent = lax.optimization_barrier((cut_first, second))
+    second_next = move(second_sent, lambda r, c: (r, c - 1) if c % span else None)
 
     own_first_meta = flat_meta(a_cols[0], a_count[0])
     own_second_meta = flat_meta(b_cols[0], b_count[0])
@@ -373,18 +376,22 @@
     part_b, part_c = lax.optimization_barrier((part_b, part_c))
     part_b = move(part_b, at(last, near))
 
-    part_a, part_c, early, second_next, first_meta, second_meta = lax.optimization_barrier(
-        (part_a, part_c, early, second_next, own_first_meta, own_second_meta)
+    part_a, part_c, early, first_meta = lax.optimization_barrier(
+        (part_a, part_c, early, own_first_meta)
     )
     part_c = move(part_c, at(middle, near))
     first_meta = move(first_meta, lambda r, c: (r - 1, c))
+
+    part_c, second_next, second_meta = lax.optimization_barrier(
+        (part_c, second_next, own_second_meta)
+    )
     second_meta = move(second_meta, lambda r, c: (r, c - 1))
     part_c = move(part_c, at(middle, lambda r, c: (r, c + last - middle)))
 
     place = jnp.stack([spot == span - 1, spot < 2]).astype(jnp.int32)
     outgoing = last_stop(
         first_meta, second_meta, kept_columns, owner, place,
-        early, late, before.reshape(-1, side, side), second_next, part_a, part_b, part_c, blank, devices,
+        early, late, before, second_next, part_a, part_b, part_c, blank, devices,
     )
     arrived = lax.all_to_all(
         outgoing.reshape(devices, per_owner, side, side),

time: 218 us -> 218 us (level)
  waiting for transfers between devices: 27.1 us -> 41.8 us
  blocking collectives: 125 us -> 116 us
  Pallas kernels: 27.9 us -> 23.7 us
    ppermute x13, waiting for transfers between devices: 27.1 us -> 41.8 us  [move(): return lax.ppermute(value, ('row', 'col'), pairs)]
    all_to_all x1, blocking collectives: 125 us -> 116 us  [on_device(): lax.all_to_all(outgoing.reshape(devices, per_owner, side, side), ('row',...]
    pallas_call x1, Pallas kernels: 14 us -> 9.88 us  [first_stop(): pl.pallas_call(first_stop_kernel, grid_spec=pltpu.PrefetchScalarGridSpec(...]
  transfers between devices with their start and end apart: 13 -> 13, of which waited for: 3 -> 2; matrix products, arithmetic and copies ran while one was open for 1% -> 1% of each run, Pallas kernels for 6% -> 5%
where the time goes in v11:
time: 218 us; the launch traced here: 217 us
  blocking collectives  116 us (53%)
  waiting for transfers between devices  41.8 us (19%)
  starting transfers between devices  31.8 us (15%)
  Pallas kernels  23.7 us (11%)
    all_to_all x1, blocking collectives, on_device(): lax.all_to_all(outgoing.reshape(devices, per_owner, side, side), ('row',...  116 us
    ppermute x13, waiting for transfers between devices, move(): return lax.ppermute(value, ('row', 'col'), pairs)  41.8 us
    ppermute x13, starting transfers between devices, move(): return lax.ppermute(value, ('row', 'col'), pairs)  31.8 us
    pallas_call x1, Pallas kernels, last_stop(): pl.pallas_call(last_stop_kernel, grid_spec=pltpu.PrefetchScalarGridSpec(n...  10.5 us
    pallas_call x1, Pallas kernels, first_stop(): pl.pallas_call(first_stop_kernel, grid_spec=pltpu.PrefetchScalarGridSpec(...  9.88 us
  transfers between devices with their start and end apart: 13, of which 2 were waited for; matrix products, arithmetic and copies ran while one was open for 1% of the time, Pallas kernels for 5%

profile of v11, /device:TPU:1, one launch (start us, length us, event | category | flops | bytes accessed | tf_op | source)
XLA Modules:
  0.0 217.1 jit_solution(7206871176085626419)
XLA Ops:
  0.0 2.0 collective-permute-start
  2.0 2.3 %collective-permute-start.5 = (bf16[80,128,128]{2,1,0:T(8,128)(2,1)}, bf16[80,128,128]{2,1,0:T(8,128)(2,1)}, u32[]{:S(2)}, u32[]{:S(2)}) collective-permute-start(bf16[80,128,128]{2,1,0:T(8,128)(2,1)} %bitcast.17), channel_id=1, source_target_pairs={{2,114},{3,115},{4,116},{5,117},{6,118},{7,119},{10,122},{11,123},... | collective-permute-start | bytes 7864328 | tf_op jit(solution)/shard_map/ppermute | solution.py:25
  4.3 1.7 collective-permute-start.1
  6.0 2.1 collective-permute-start.3
  8.1 12.4 %collective-permute-start.8 = (bf16[160,128,128]{2,1,0:T(8,128)(2,1)}, bf16[160,128,128]{2,1,0:T(8,128)(2,1)}, u32[]{:S(2)}, u32[]{:S(2)}) collective-permute-start(bf16[160,128,128]{2,1,0:T(8,128)(2,1)} %bitcast.13), channel_id=1, source_target_pairs={{1,0},{2,1},{3,2},{4,3},{5,4},{6,5},{7,6},{9,8},{10,9},{11,10},{12... | collective-permute-start | bytes 15728648 | tf_op jit(solution)/shard_map/ppermute | solution.py:25
  20.7 0.6 reshape_squeeze.19.kept_columns
  21.4 0.1 reshape_squeeze.18
  21.5 0.6 pad_add_fusion.1.first_meta
  22.1 0.7 pad_add_fusion.second_meta
  22.8 9.9 %shard_map.84 = (f32[120,128,128]{2,1,0:T(8,128)}, bf16[256,128,128]{2,1,0:T(8,128)(2,1)}) custom-call(s32[90]{0:T(128)} %pad_add_fusion.1.first_meta, s32[180]{0:T(256)} %pad_add_fusion.second_meta, s32[120]{0:T(128)} %reshape_squeeze.19.kept_columns, bf16[80,128,128]{2,1,0:T(8,128)(2,1)} %bitcast.18, bf16[160,128,128]{2,1,0:T(8,128)(2,1)} %bitcast.14), custom_call_target="tpu_custom_call" | custom-call | flops 805306368000 | bytes 31457280 | tf_op jit(solution)/shard_map/pallas_call | solution.py:203
  32.7 0.8 collective-permute-start.2
  33.5 0.7 collective-permute-start.4
  34.2 5.2 %collective-permute-start.10 = (bf16[80,128,128]{2,1,0:T(8,128)(2,1)}, bf16[80,128,128]{2,1,0:T(8,128)(2,1)}, u32[]{:S(2)}, u32[]{:S(2)}) collective-permute-start(bf16[80,128,128]{2,1,0:T(8,128)(2,1)} %bitcast.19), channel_id=1, source_target_pairs={{0,112},{1,113},{8,120},{9,121},{16,0},{17,1},{24,8},{25,9},{32,16... | collective-permute-start | bytes 7864328 | tf_op jit(solution)/shard_map/ppermute | solution.py:25
  39.5 2.1 collective-permute-start.11
  41.6 0.7 collective-permute-start.7
  42.4 32.3 %collective-permute-done.8.second = bf16[160,128,128]{2,1,0:T(8,128)(2,1)} collective-permute-done((bf16[160,128,128]{2,1,0:T(8,128)(2,1)}, bf16[160,128,128]{2,1,0:T(8,128)(2,1)}, u32[]{:S(2)}, u32[]{:S(2)}) %collective-permute-start.8) | collective-permute-done | bytes 5242912 | tf_op jit(solution)/shard_map/ppermute | solution.py:25
  74.6 1.7 collective-permute-start.12
  76.3 0.2 collective-permute-start.6
  76.5 0.6 add_convert_fusion.place
  77.0 9.5 %collective-permute-done.6.first_meta = s32[90]{0:T(128)S(1)} collective-permute-done((s32[90]{0:T(128)S(1)}, s32[90]{0:T(128)S(1)}, u32[]{:S(2)}, u32[]{:S(2)}) %collective-permute-start.6) | collective-permute-done | bytes 392 | tf_op jit(solution)/shard_map/ppermute | solution.py:25
  86.6 0.5 copy-done.6
  87.2 10.5 %shard_map.85 = bf16[256,128,128]{2,1,0:T(8,128)(2,1)} custom-call(s32[90]{0:T(128)} %copy-done.6, s32[180]{0:T(256)} %copy-done.4, s32[120]{0:T(128)} %reshape_squeeze.19.kept_columns, s32[120]{0:T(128)} %bitcast.15, s32[2]{0:T(128)} %add_convert_fusion.place, bf16[80,128,128]{2,1,0:T(8,128)(2,1)} %collective-permute-done.5.early, ...), custom_call_target="tpu_custom_call", output_to_operand_aliasing={{}: (12, {})} | custom-call | flops 1024 | bytes 1024 | tf_op jit(solution)/shard_map/pallas_call | solution.py:243
  97.7 116.1 %all_to_all.5.source = bf16[128,2,128,128]{3,2,1,0:T(8,128)(2,1)S(1)} all-to-all(bf16[128,2,128,128]{3,2,1,0:T(8,128)(2,1)} %bitcast.10), channel_id=1, replica_groups=mesh['row'=8,'col'=16] {'row','col'}, dimensions={0} | all-to-all | bytes 16777216 | tf_op jit(solution)/shard_map/all_to_all | solution.py:396
  213.8 3.3 %shard_map.86 = bf16[128,2,128,128]{3,2,1,0:T(8,128)(2,1)} custom-call(bf16[128,2,128,128]{3,2,1,0:T(8,128)(2,1)S(1)} %all_to_all.5.source), custom_call_target="tpu_custom_call" | custom-call | tf_op jit(solution)/shard_map/pallas_call | solution.py:319
  (37 shorter events, 0.5 us)
Async XLA Ops:
  0.0 32.7 %collective-permute-start = (bf16[60,128,128]{2,1,0:T(8,128)(2,1)}, bf16[60,128,128]{2,1,0:T(8,128)(2,1)}, u32[]{:S(2)}, u32[]{:S(2)}) collective-permute-start(bf16[60,128,128]{2,1,0:T(8,128)(2,1)} %shard_map.82), channel_id=1, source_target_pairs={{0,16},{8,24},{16,0},{24,8},{32,48},{40,56},{48,32},{56,40},{64,80... | collective-permute-start | bytes 5898248 | tf_op jit(solution)/shard_map/ppermute | solution.py:25
  2.0 18.5 %copy-start.2 = (s32[1,10,8]{1,2,0:T(8,128)S(1)}, s32[1,10,8]{1,2,0:T(8,128)}, u32[]{:S(2)}) copy-start(s32[1,10,8]{1,2,0:T(8,128)} %param.9) | copy-start | bytes 964
  2.0 18.7 %copy-start.1 = (s32[1,10,12]{2,0,1:T(1,128)S(1)}, s32[1,10,12]{2,0,1:T(1,128)}, u32[]{:S(2)}) copy-start(s32[1,10,12]{2,0,1:T(1,128)} %param.14) | copy-start | bytes 1444
  2.0 19.3 %copy-start.3 = (s32[1,20,8]{1,2,0:T(8,128)S(1)}, s32[1,20,8]{1,2,0:T(8,128)}, u32[]{:S(2)}) copy-start(s32[1,20,8]{1,2,0:T(8,128)} %param.12) | copy-start | bytes 1924
  2.0 19.4 %copy-start.8 = (s32[1,10]{1,0:T(1,128)S(1)}, s32[1,10]{1,0:T(1,128)}, u32[]{:S(2)}) copy-start(s32[1,10]{1,0:T(1,128)} %param.10) | copy-start | bytes 124
  2.0 20.1 %copy-start.7 = (s32[1,20]{1,0:T(1,128)S(1)}, s32[1,20]{1,0:T(1,128)}, u32[]{:S(2)}) copy-start(s32[1,20]{1,0:T(1,128)} %param.13) | copy-start | bytes 244
  2.0 39.6 %collective-permute-start.5 = (bf16[80,128,128]{2,1,0:T(8,128)(2,1)}, bf16[80,128,128]{2,1,0:T(8,128)(2,1)}, u32[]{:S(2)}, u32[]{:S(2)}) collective-permute-start(bf16[80,128,128]{2,1,0:T(8,128)(2,1)} %bitcast.17), channel_id=1, source_target_pairs={{2,114},{3,115},{4,116},{5,117},{6,118},{7,119},{10,122},{11,123},... | collective-permute-start | bytes 7864328 | tf_op jit(solution)/shard_map/ppermute | solution.py:25
  4.3 28.3 %collective-permute-start.1 = (bf16[26,128,128]{2,1,0:T(8,128)(2,1)}, bf16[26,128,128]{2,1,0:T(8,128)(2,1)}, u32[]{:S(2)}, u32[]{:S(2)}) collective-permute-start(bf16[26,128,128]{2,1,0:T(8,128)(2,1)} %get-tuple-element.24), channel_id=1, source_target_pairs={{0,5},{8,13},{16,21},{24,29},{32,37},{40,45},{48,53},{56,61},{64,6... | collective-permute-start | bytes 2555912 | tf_op jit(solution)/shard_map/ppermute | solution.py:25
  6.0 28.2 %collective-permute-start.3 = (bf16[74,128,128]{2,1,0:T(8,128)(2,1)}, bf16[74,128,128]{2,1,0:T(8,128)(2,1)}, u32[]{:S(2)}, u32[]{:S(2)}) collective-permute-start(bf16[74,128,128]{2,1,0:T(8,128)(2,1)} %get-tuple-element.28), channel_id=1, source_target_pairs={{0,31},{8,23},{16,15},{24,7},{32,63},{40,55},{48,47},{56,39},{64,9... | collective-permute-start | bytes 7274504 | tf_op jit(solution)/shard_map/ppermute | solution.py:25
  8.1 66.5 %collective-permute-start.8 = (bf16[160,128,128]{2,1,0:T(8,128)(2,1)}, bf16[160,128,128]{2,1,0:T(8,128)(2,1)}, u32[]{:S(2)}, u32[]{:S(2)}) collective-permute-start(bf16[160,128,128]{2,1,0:T(8,128)(2,1)} %bitcast.13), channel_id=1, source_target_pairs={{1,0},{2,1},{3,2},{4,3},{5,4},{6,5},{7,6},{9,8},{10,9},{11,10},{12... | collective-permute-start | bytes 15728648 | tf_op jit(solution)/shard_map/ppermute | solution.py:25
  22.8 53.5 %copy-start.9 = (s32[90]{0:T(128)S(1)}, s32[90]{0:T(128)}, u32[]{:S(2)}) copy-start(s32[90]{0:T(128)} %pad_add_fusion.1.first_meta) | copy-start | bytes 1084
  22.8 53.7 %copy-start.5 = (s32[180]{0:T(256)S(1)}, s32[180]{0:T(256)}, u32[]{:S(2)}) copy-start(s32[180]{0:T(256)} %pad_add_fusion.second_meta) | copy-start | bytes 2164
  32.7 8.9 %collective-permute-start.2 = (bf16[60,128,128]{2,1,0:T(8,128)(2,1)}, bf16[60,128,128]{2,1,0:T(8,128)(2,1)S(1)}, u32[]{:S(2)}, u32[]{:S(2)}) collective-permute-start(bf16[60,128,128]{2,1,0:T(8,128)(2,1)} %collective-permute-done), channel_id=1, source_target_pairs={{0,31},{8,23},{16,15},{24,7},{32,63},{40,55},{48,47},{56,39},{64,9... | collective-permute-start | bytes 5898248 | tf_op jit(solution)/shard_map/ppermute | solution.py:25
  33.5 6.0 %collective-permute-start.4 = (bf16[26,128,128]{2,1,0:T(8,128)(2,1)}, bf16[26,128,128]{2,1,0:T(8,128)(2,1)S(1)}, u32[]{:S(2)}, u32[]{:S(2)}) collective-permute-start(bf16[26,128,128]{2,1,0:T(8,128)(2,1)} %collective-permute-done.1), channel_id=1, source_target_pairs={{5,29},{13,21},{21,13},{29,5},{37,61},{45,53},{53,45},{61,37},{69,... | collective-permute-start | bytes 2555912 | tf_op jit(solution)/shard_map/ppermute | solution.py:25
  34.2 52.4 %collective-permute-start.10 = (bf16[80,128,128]{2,1,0:T(8,128)(2,1)}, bf16[80,128,128]{2,1,0:T(8,128)(2,1)}, u32[]{:S(2)}, u32[]{:S(2)}) collective-permute-start(bf16[80,128,128]{2,1,0:T(8,128)(2,1)} %bitcast.19), channel_id=1, source_target_pairs={{0,112},{1,113},{8,120},{9,121},{16,0},{17,1},{24,8},{25,9},{32,16... | collective-permute-start | bytes 7864328 | tf_op jit(solution)/shard_map/ppermute | solution.py:25
  39.5 47.1 %collective-permute-start.11 = (bf16[74,128,128]{2,1,0:T(8,128)(2,1)}, bf16[74,128,128]{2,1,0:T(8,128)(2,1)}, u32[]{:S(2)}, u32[]{:S(2)}) collective-permute-start(bf16[74,128,128]{2,1,0:T(8,128)(2,1)} %collective-permute-done.3), channel_id=1, source_target_pairs={{7,23},{15,31},{23,7},{31,15},{39,55},{47,63},{55,39},{63,47},{71,... | collective-permute-start | bytes 7274504 | tf_op jit(solution)/shard_map/ppermute | solution.py:25
  41.6 45.0 %copy-start = (bf16[60,128,128]{2,1,0:T(8,128)(2,1)}, bf16[60,128,128]{2,1,0:T(8,128)(2,1)S(1)}, u32[]{:S(2)}) copy-start(bf16[60,128,128]{2,1,0:T(8,128)(2,1)S(1)} %collective-permute-done.2.part_a) | copy-start | bytes 5898244
  41.6 0.7 collective-permute-start.7
  74.6 12.0 %collective-permute-start.12 = (bf16[26,128,128]{2,1,0:T(8,128)(2,1)S(1)}, bf16[26,128,128]{2,1,0:T(8,128)(2,1)}, u32[]{:S(2)}, u32[]{:S(2)}) collective-permute-start(bf16[26,128,128]{2,1,0:T(8,128)(2,1)S(1)} %collective-permute-done.7), channel_id=1, source_target_pairs={{5,7},{13,15},{21,23},{29,31},{37,39},{45,47},{53,55},{61,63},{69,... | collective-permute-start | bytes 2555912 | tf_op jit(solution)/shard_map/ppermute | solution.py:25
  76.3 10.3 %collective-permute-start.6 = (s32[90]{0:T(128)S(1)}, s32[90]{0:T(128)S(1)}, u32[]{:S(2)}, u32[]{:S(2)}) collective-permute-start(s32[90]{0:T(128)S(1)} %copy-done.9), channel_id=1, source_target_pairs={{0,112},{1,113},{2,114},{3,115},{4,116},{5,117},{6,118},{7,119},{8... | collective-permute-start | bytes 1088 | tf_op jit(solution)/shard_map/ppermute | solution.py:25
  76.5 10.1 %collective-permute-start.9 = (s32[180]{0:T(256)S(1)}, s32[180]{0:T(256)S(1)}, u32[]{:S(2)}, u32[]{:S(2)}) collective-permute-start(s32[180]{0:T(256)S(1)} %copy-done.5), channel_id=1, source_target_pairs={{0,15},{1,0},{2,1},{3,2},{4,3},{5,4},{6,5},{7,6},{8,7},{9,8},{10,9... | collective-permute-start | bytes 2168 | tf_op jit(solution)/shard_map/ppermute | solution.py:25
  86.6 0.5 copy-start.6
  86.6 0.6 copy-start.4

commit v12 on v10

--- a/solution.py
+++ b/solution.py
@@ -333,7 +333,7 @@
     first = a_blocks[0].reshape(-1, side, side)
     second = b_blocks[0].reshape(-1, side, side)
     total = second.shape[0]
-    large_a, large_b = total * 17 // 40, total * 7 // 16
+    large_a, large_b = total * 17 // 40, total * 13 // 32
     spot = lax.axis_index("col") % span
     crossing = (spot == 0).astype(jnp.int32)[None]
 

time: 218 us -> 218 us (level)
  waiting for transfers between devices: 27.1 us -> 30 us
    ppermute x13, waiting for transfers between devices: 27.1 us -> 30 us  [move(): return lax.ppermute(value, ('row', 'col'), pairs)]
  transfers between devices with their start and end apart: 13 -> 13, of which waited for: 3 -> 2; matrix products, arithmetic and copies ran while one was open for 1% -> 1% of each run, Pallas kernels for 6% -> 7%
where the time goes in v12:
time: 218 us
  blocking collectives  124 us (57%)
  starting transfers between devices  32 us (15%)
  waiting for transfers between devices  30 us (14%)
  Pallas kernels  28 us (13%)
    all_to_all x1, blocking collectives, on_device(): lax.all_to_all(outgoing.reshape(devices, per_owner, side, side), ('row',...  124 us
    ppermute x13, starting transfers between devices, move(): return lax.ppermute(value, ('row', 'col'), pairs)  32 us
    ppermute x13, waiting for transfers between devices, move(): return lax.ppermute(value, ('row', 'col'), pairs)  30 us
    pallas_call x1, Pallas kernels, first_stop(): pl.pallas_call(first_stop_kernel, grid_spec=pltpu.PrefetchScalarGridSpec(...  14.1 us
    pallas_call x1, Pallas kernels, last_stop(): pl.pallas_call(last_stop_kernel, grid_spec=pltpu.PrefetchScalarGridSpec(n...  10.6 us
  transfers between devices with their start and end apart: 13, of which 2 were waited for; matrix products, arithmetic and copies ran while one was open for 1% of the time, Pallas kernels for 7%

profile of v12, /device:TPU:1, one launch (start us, length us, event | category | flops | bytes accessed | tf_op | source)
XLA Modules:
  0.0 217.9 jit_solution(17750151537830558614)
XLA Ops:
  0.0 3.3 %collective-permute-start.6 = (bf16[160,128,128]{2,1,0:T(8,128)(2,1)}, bf16[160,128,128]{2,1,0:T(8,128)(2,1)}, u32[]{:S(2)}, u32[]{:S(2)}) collective-permute-start(bf16[160,128,128]{2,1,0:T(8,128)(2,1)} %bitcast.12), channel_id=1, source_target_pairs={{1,0},{2,1},{3,2},{4,3},{5,4},{6,5},{7,6},{9,8},{10,9},{11,10},{12... | collective-permute-start | bytes 15728648 | tf_op jit(solution)/shard_map/ppermute | solution.py:25
  3.4 2.1 collective-permute-start
  5.5 2.3 %collective-permute-start.5 = (bf16[80,128,128]{2,1,0:T(8,128)(2,1)}, bf16[80,128,128]{2,1,0:T(8,128)(2,1)}, u32[]{:S(2)}, u32[]{:S(2)}) collective-permute-start(bf16[80,128,128]{2,1,0:T(8,128)(2,1)} %bitcast.19), channel_id=1, source_target_pairs={{2,114},{3,115},{4,116},{5,117},{6,118},{7,119},{10,122},{11,123},... | collective-permute-start | bytes 7864328 | tf_op jit(solution)/shard_map/ppermute | solution.py:25
  7.8 1.6 collective-permute-start.1
  9.4 2.0 collective-permute-start.3
  11.6 0.6 reshape_squeeze.19.kept_columns
  12.3 0.6 pad_add_fusion.1.first_meta
  12.9 0.6 pad_add_fusion.second_meta
  13.5 14.1 %shard_map.84 = (f32[10,12,128,128]{3,2,1,0:T(8,128)}, bf16[256,128,128]{2,1,0:T(8,128)(2,1)}) custom-call(s32[90]{0:T(128)} %pad_add_fusion.1.first_meta, s32[180]{0:T(256)} %pad_add_fusion.second_meta, s32[120]{0:T(128)} %reshape_squeeze.19.kept_columns, bf16[80,128,128]{2,1,0:T(8,128)(2,1)} %bitcast.20, bf16[160,128,128]{2,1,0:T(8,128)(2,1)} %bitcast.15), custom_call_target="tpu_custom_call" | custom-call | flops 805306368000 | bytes 31457280 | tf_op jit(solution)/shard_map/pallas_call | solution.py:200
  27.6 2.0 collective-permute-start.2
  29.7 0.7 collective-permute-start.4
  30.4 5.7 %collective-permute-start.9 = (bf16[80,128,128]{2,1,0:T(8,128)(2,1)}, bf16[80,128,128]{2,1,0:T(8,128)(2,1)}, u32[]{:S(2)}, u32[]{:S(2)}) collective-permute-start(bf16[80,128,128]{2,1,0:T(8,128)(2,1)} %bitcast.21), channel_id=1, source_target_pairs={{0,112},{1,113},{8,120},{9,121},{16,0},{17,1},{24,8},{25,9},{32,16... | collective-permute-start | bytes 7864328 | tf_op jit(solution)/shard_map/ppermute | solution.py:25
  36.1 2.0 collective-permute-start.10
  38.1 24.9 %collective-permute-done.6.second = bf16[160,128,128]{2,1,0:T(8,128)(2,1)} collective-permute-done((bf16[160,128,128]{2,1,0:T(8,128)(2,1)}, bf16[160,128,128]{2,1,0:T(8,128)(2,1)}, u32[]{:S(2)}, u32[]{:S(2)}) %collective-permute-start.6) | collective-permute-done | bytes 5242912 | tf_op jit(solution)/shard_map/ppermute | solution.py:25
  63.0 0.7 collective-permute-start.11
  63.7 0.7 collective-permute-start.12
  64.4 3.6 %collective-permute-start.7 = (s32[90]{0:T(128)S(1)}, s32[90]{0:T(128)S(1)}, u32[]{:S(2)}, u32[]{:S(2)}) collective-permute-start(s32[90]{0:T(128)S(1)} %copy-done.9), channel_id=1, source_target_pairs={{0,112},{1,113},{2,114},{3,115},{4,116},{5,117},{6,118},{7,119},{8... | collective-permute-start | bytes 1088 | tf_op jit(solution)/shard_map/ppermute | solution.py:25
  68.0 5.3 %collective-permute-start.8 = (s32[180]{0:T(256)S(1)}, s32[180]{0:T(256)S(1)}, u32[]{:S(2)}, u32[]{:S(2)}) collective-permute-start(s32[180]{0:T(256)S(1)} %copy-done.5), channel_id=1, source_target_pairs={{0,15},{1,0},{2,1},{3,2},{4,3},{5,4},{6,5},{7,6},{8,7},{9,8},{10,9... | collective-permute-start | bytes 2168 | tf_op jit(solution)/shard_map/ppermute | solution.py:25
  73.3 0.6 add_convert_fusion.place
  73.9 5.1 %collective-permute-done.9.late = bf16[80,128,128]{2,1,0:T(8,128)(2,1)} collective-permute-done((bf16[80,128,128]{2,1,0:T(8,128)(2,1)}, bf16[80,128,128]{2,1,0:T(8,128)(2,1)}, u32[]{:S(2)}, u32[]{:S(2)}) %collective-permute-start.9) | collective-permute-done | bytes 2621472 | tf_op jit(solution)/shard_map/ppermute | solution.py:25
  79.1 0.5 copy-done.6
  80.0 10.6 %shard_map.85 = bf16[256,128,128]{2,1,0:T(8,128)(2,1)} custom-call(s32[90]{0:T(128)} %copy-done.6, s32[180]{0:T(256)} %copy-done.4, s32[120]{0:T(128)} %reshape_squeeze.19.kept_columns, s32[120]{0:T(128)} %bitcast.17, s32[2]{0:T(128)} %add_convert_fusion.place, bf16[80,128,128]{2,1,0:T(8,128)(2,1)} %collective-permute-done.5.early, ...), custom_call_target="tpu_custom_call", output_to_operand_aliasing={{}: (12, {})} | custom-call | flops 1024 | bytes 1024 | tf_op jit(solution)/shard_map/pallas_call | solution.py:241
  90.6 124.0 %all_to_all.5.source = bf16[128,2,128,128]{3,2,1,0:T(8,128)(2,1)S(1)} all-to-all(bf16[128,2,128,128]{3,2,1,0:T(8,128)(2,1)} %bitcast.11), channel_id=1, replica_groups=mesh['row'=8,'col'=16] {'row','col'}, dimensions={0} | all-to-all | bytes 16777216 | tf_op jit(solution)/shard_map/all_to_all | solution.py:389
  214.6 3.3 %shard_map.86 = bf16[128,2,128,128]{3,2,1,0:T(8,128)(2,1)} custom-call(bf16[128,2,128,128]{3,2,1,0:T(8,128)(2,1)S(1)} %all_to_all.5.source), custom_call_target="tpu_custom_call" | custom-call | tf_op jit(solution)/shard_map/pallas_call | solution.py:317
  (37 shorter events, 0.8 us)
Async XLA Ops:
  0.0 63.0 %collective-permute-start.6 = (bf16[160,128,128]{2,1,0:T(8,128)(2,1)}, bf16[160,128,128]{2,1,0:T(8,128)(2,1)}, u32[]{:S(2)}, u32[]{:S(2)}) collective-permute-start(bf16[160,128,128]{2,1,0:T(8,128)(2,1)} %bitcast.12), channel_id=1, source_target_pairs={{1,0},{2,1},{3,2},{4,3},{5,4},{6,5},{7,6},{9,8},{10,9},{11,10},{12... | collective-permute-start | bytes 15728648 | tf_op jit(solution)/shard_map/ppermute | solution.py:25
  3.4 24.2 %collective-permute-start = (bf16[68,128,128]{2,1,0:T(8,128)(2,1)}, bf16[68,128,128]{2,1,0:T(8,128)(2,1)}, u32[]{:S(2)}, u32[]{:S(2)}) collective-permute-start(bf16[68,128,128]{2,1,0:T(8,128)(2,1)} %shard_map.82), channel_id=1, source_target_pairs={{0,16},{8,24},{16,0},{24,8},{32,48},{40,56},{48,32},{56,40},{64,80... | collective-permute-start | bytes 6684680 | tf_op jit(solution)/shard_map/ppermute | solution.py:25
  5.5 5.9 %copy-start.2 = (s32[1,10,8]{1,2,0:T(8,128)S(1)}, s32[1,10,8]{1,2,0:T(8,128)}, u32[]{:S(2)}) copy-start(s32[1,10,8]{1,2,0:T(8,128)} %param.9) | copy-start | bytes 964
  5.5 6.1 %copy-start.1 = (s32[1,10,12]{2,0,1:T(1,128)S(1)}, s32[1,10,12]{2,0,1:T(1,128)}, u32[]{:S(2)}) copy-start(s32[1,10,12]{2,0,1:T(1,128)} %param.14) | copy-start | bytes 1444
  5.5 6.7 %copy-start.3 = (s32[1,20,8]{1,2,0:T(8,128)S(1)}, s32[1,20,8]{1,2,0:T(8,128)}, u32[]{:S(2)}) copy-start(s32[1,20,8]{1,2,0:T(8,128)} %param.12) | copy-start | bytes 1924
  5.5 6.9 %copy-start.8 = (s32[1,10]{1,0:T(1,128)S(1)}, s32[1,10]{1,0:T(1,128)}, u32[]{:S(2)}) copy-start(s32[1,10]{1,0:T(1,128)} %param.10) | copy-start | bytes 124
  5.5 7.4 %copy-start.7 = (s32[1,20]{1,0:T(1,128)S(1)}, s32[1,20]{1,0:T(1,128)}, u32[]{:S(2)}) copy-start(s32[1,20]{1,0:T(1,128)} %param.13) | copy-start | bytes 244
  5.5 32.6 %collective-permute-start.5 = (bf16[80,128,128]{2,1,0:T(8,128)(2,1)}, bf16[80,128,128]{2,1,0:T(8,128)(2,1)}, u32[]{:S(2)}, u32[]{:S(2)}) collective-permute-start(bf16[80,128,128]{2,1,0:T(8,128)(2,1)} %bitcast.19), channel_id=1, source_target_pairs={{2,114},{3,115},{4,116},{5,117},{6,118},{7,119},{10,122},{11,123},... | collective-permute-start | bytes 7864328 | tf_op jit(solution)/shard_map/ppermute | solution.py:25
  7.8 19.8 %collective-permute-start.1 = (bf16[27,128,128]{2,1,0:T(8,128)(2,1)}, bf16[27,128,128]{2,1,0:T(8,128)(2,1)}, u32[]{:S(2)}, u32[]{:S(2)}) collective-permute-start(bf16[27,128,128]{2,1,0:T(8,128)(2,1)} %get-tuple-element.22), channel_id=1, source_target_pairs={{0,5},{8,13},{16,21},{24,29},{32,37},{40,45},{48,53},{56,61},{64,6... | collective-permute-start | bytes 2654216 | tf_op jit(solution)/shard_map/ppermute | solution.py:25
  9.4 21.0 %collective-permute-start.3 = (bf16[65,128,128]{2,1,0:T(8,128)(2,1)}, bf16[65,128,128]{2,1,0:T(8,128)(2,1)}, u32[]{:S(2)}, u32[]{:S(2)}) collective-permute-start(bf16[65,128,128]{2,1,0:T(8,128)(2,1)} %get-tuple-element.26), channel_id=1, source_target_pairs={{0,31},{8,23},{16,15},{24,7},{32,63},{40,55},{48,47},{56,39},{64,9... | collective-permute-start | bytes 6389768 | tf_op jit(solution)/shard_map/ppermute | solution.py:25
  13.5 50.9 %copy-start.9 = (s32[90]{0:T(128)S(1)}, s32[90]{0:T(128)}, u32[]{:S(2)}) copy-start(s32[90]{0:T(128)} %pad_add_fusion.1.first_meta) | copy-start | bytes 1084
  13.5 54.5 %copy-start.5 = (s32[180]{0:T(256)S(1)}, s32[180]{0:T(256)}, u32[]{:S(2)}) copy-start(s32[180]{0:T(256)} %pad_add_fusion.second_meta) | copy-start | bytes 2164
  27.6 10.5 %collective-permute-start.2 = (bf16[68,128,128]{2,1,0:T(8,128)(2,1)}, bf16[68,128,128]{2,1,0:T(8,128)(2,1)}, u32[]{:S(2)}, u32[]{:S(2)}) collective-permute-start(bf16[68,128,128]{2,1,0:T(8,128)(2,1)} %collective-permute-done), channel_id=1, source_target_pairs={{0,31},{8,23},{16,15},{24,7},{32,63},{40,55},{48,47},{56,39},{64,9... | collective-permute-start | bytes 6684680 | tf_op jit(solution)/shard_map/ppermute | solution.py:25
  29.7 6.4 %collective-permute-start.4 = (bf16[27,128,128]{2,1,0:T(8,128)(2,1)}, bf16[27,128,128]{2,1,0:T(8,128)(2,1)S(1)}, u32[]{:S(2)}, u32[]{:S(2)}) collective-permute-start(bf16[27,128,128]{2,1,0:T(8,128)(2,1)} %collective-permute-done.1), channel_id=1, source_target_pairs={{5,29},{13,21},{21,13},{29,5},{37,61},{45,53},{53,45},{61,37},{69,... | collective-permute-start | bytes 2654216 | tf_op jit(solution)/shard_map/ppermute | solution.py:25
  30.4 48.7 %collective-permute-start.9 = (bf16[80,128,128]{2,1,0:T(8,128)(2,1)}, bf16[80,128,128]{2,1,0:T(8,128)(2,1)}, u32[]{:S(2)}, u32[]{:S(2)}) collective-permute-start(bf16[80,128,128]{2,1,0:T(8,128)(2,1)} %bitcast.21), channel_id=1, source_target_pairs={{0,112},{1,113},{8,120},{9,121},{16,0},{17,1},{24,8},{25,9},{32,16... | collective-permute-start | bytes 7864328 | tf_op jit(solution)/shard_map/ppermute | solution.py:25
  36.1 43.0 %collective-permute-start.10 = (bf16[65,128,128]{2,1,0:T(8,128)(2,1)}, bf16[65,128,128]{2,1,0:T(8,128)(2,1)}, u32[]{:S(2)}, u32[]{:S(2)}) collective-permute-start(bf16[65,128,128]{2,1,0:T(8,128)(2,1)} %collective-permute-done.3), channel_id=1, source_target_pairs={{7,23},{15,31},{23,7},{31,15},{39,55},{47,63},{55,39},{63,47},{71,... | collective-permute-start | bytes 6389768 | tf_op jit(solution)/shard_map/ppermute | solution.py:25
  63.0 0.7 collective-permute-start.11
  63.7 15.4 %collective-permute-start.12 = (bf16[27,128,128]{2,1,0:T(8,128)(2,1)S(1)}, bf16[27,128,128]{2,1,0:T(8,128)(2,1)S(1)}, u32[]{:S(2)}, u32[]{:S(2)}) collective-permute-start(bf16[27,128,128]{2,1,0:T(8,128)(2,1)S(1)} %collective-permute-done.11), channel_id=1, source_target_pairs={{5,7},{13,15},{21,23},{29,31},{37,39},{45,47},{53,55},{61,63},{69,... | collective-permute-start | bytes 2654216 | tf_op jit(solution)/shard_map/ppermute | solution.py:25
  64.4 14.7 %collective-permute-start.7 = (s32[90]{0:T(128)S(1)}, s32[90]{0:T(128)S(1)}, u32[]{:S(2)}, u32[]{:S(2)}) collective-permute-start(s32[90]{0:T(128)S(1)} %copy-done.9), channel_id=1, source_target_pairs={{0,112},{1,113},{2,114},{3,115},{4,116},{5,117},{6,118},{7,119},{8... | collective-permute-start | bytes 1088 | tf_op jit(solution)/shard_map/ppermute | solution.py:25
  68.0 11.1 %collective-permute-start.8 = (s32[180]{0:T(256)S(1)}, s32[180]{0:T(256)S(1)}, u32[]{:S(2)}, u32[]{:S(2)}) collective-permute-start(s32[180]{0:T(256)S(1)} %copy-done.5), channel_id=1, source_target_pairs={{0,15},{1,0},{2,1},{3,2},{4,3},{5,4},{6,5},{7,6},{8,7},{9,8},{10,9... | collective-permute-start | bytes 2168 | tf_op jit(solution)/shard_map/ppermute | solution.py:25
  79.1 0.6 copy-start.6
  79.1 0.6 copy-start.4
  79.1 0.9 copy-start
